TPU v7x, 32 devices: a whole 2x2x4 slice. The times are simulated.
32 devices in a mesh: rows: 16 (over z, x, core), vecs: 2 (over y).
Axes of the slice: x: 2, y: 2, z: 4, core: 2. Of those that a mesh axis runs over, the one named last changes fastest.
Arguments:
- tiles: bfloat16 [64, 6, 128, 128], P('rows'), as said below
- columns: int32 [64, 6], P('rows'), may hold values from 0 to 63, as said below
- start_vectors: float32 [1024, 8192], P('vecs', 'rows'), may hold values from -6 to 6
Outputs:
- basis: float32 [1024, 8192], P('vecs', 'rows')
Inputs may be any that keep to these rules, and one draw needn't show every extreme that they name: `columns`: the 6 column blocks of row block b are distinct; they are b, b - 1, b + 1 and three of b - 3, b - 2, b + 2, b + 3, all modulo 64, the first three in this order. The pattern is symmetric: block c is among those of row block b exactly when b is among those of row block c. `tiles`: H is symmetric: the tile of row block b at column block c is the transpose of the tile of row block c at column block b.
All inputs are finite; a program needn't handle non-finite values.
Results may differ from a plain program's by a relative error of at most 0.0003.
Values sent between devices are 32-bit elements; how exact they have to be, the bound alone decides.
No kernel may reach another device: no remote copies, remote signals or barrier semaphores. Data moves between devices by JAX's collectives and lax.ppermute only.
A program may use at most 64 MiB of HBM per device.

v0:
```python
import jax
import jax.numpy as jnp
from jax import lax
from jax.sharding import PartitionSpec as P

BS = 128
HB = 3
STEPS = 4


def with_halo(shard, sides, width):
    for axis, dim in sides:
        devices, length = (lax.axis_size(axis), shard.shape[dim])
        up = [(i, (i + 1) % devices) for i in range(devices)]
        down = [(j, i) for i, j in up]
        last = lax.slice_in_dim(shard, length - width, length, axis=dim)
        initial = lax.slice_in_dim(shard, 0, width, axis=dim)
        before = lax.ppermute(last, axis, up)
        after = lax.ppermute(initial, axis, down)
        shard = jnp.concatenate([before, shard, after], axis=dim)
    return shard


def operate(field, tiles32, slots):
    extended = with_halo(field, (("rows", 1),), HB * BS)
    width = field.shape[0]
    blocks_here = tiles32.shape[0]
    blocked = extended.reshape(width, blocks_here + 2 * HB, BS)
    picked = blocked[:, slots]
    result = jnp.einsum("mbtj,btij->mbi", picked, tiles32, precision=lax.Precision.HIGHEST)
    return result.reshape(width, blocks_here * BS)


def body(tiles, columns, start_vectors):
    blocks_here = tiles.shape[0]
    total_blocks = blocks_here * lax.axis_size("rows")
    first_block = lax.axis_index("rows") * blocks_here
    global_rows = first_block + jnp.arange(blocks_here, dtype=jnp.int32)
    offsets = jnp.mod(columns - global_rows[:, None] + HB, total_blocks)
    slots = jnp.arange(blocks_here, dtype=jnp.int32)[:, None] + offsets
    tiles32 = tiles.astype(jnp.float32)
    previous = start_vectors
    current = operate(start_vectors, tiles32, slots)
    for step in range(STEPS - 1):
        following = 2.0 * operate(current, tiles32, slots) - previous
        previous = current
        current = following
    scale = jnp.sqrt(jnp.float32(total_blocks * BS))
    width = current.shape[0]
    gathered = lax.all_gather(current, "vecs", axis=0, tiled=True)
    partial_rows = jnp.einsum("mn,kn->mk", current, gathered, precision=lax.Precision.HIGHEST)
    summed_rows = lax.psum(partial_rows, "rows")
    gram = lax.all_gather(summed_rows, "vecs", axis=0, tiled=True)
    factor = jnp.linalg.cholesky(gram)
    solved_all = lax.linalg.triangular_solve(factor, gathered, left_side=True, lower=True)
    own_rows = lax.dynamic_slice_in_dim(solved_all, lax.axis_index("vecs") * width, width, 0)
    return own_rows * scale


def solution(mesh):
    placed = (P("rows", None, None, None), P("rows", None), P("vecs", "rows"))
    return jax.shard_map(
        body, mesh=mesh, in_specs=placed, out_specs=P("vecs", "rows"), check_vma=False
    )
```

profile of v0, /device:TPU:5, one launch (start us, length us, event | category | flops | bytes accessed | tf_op | source)
XLA Modules:
  0.0 696.8 jit_solution(3390448644001559571)
XLA Ops:
  11.5 17.5 %collective-permute-done = f32[512,384]{0,1:T(8,128)S(1)} collective-permute-done((f32[512,384]{0,1:T(8,128)}, f32[512,384]{0,1:T(8,128)S(1)}, u32[]{:S(2)}, u32[]{:S(2)}) %collective-permute-start) | collective-permute-done | bytes 786464 | tf_op jit(solution)/shard_map/ppermute | solution.py:18
  38.8 6.4 fusion.71
  46.0 16.9 %collective-permute-done.2 = f32[512,384]{0,1:T(8,128)S(1)} collective-permute-done((f32[512,384]{0,1:T(8,128)S(1)}, f32[512,384]{0,1:T(8,128)S(1)}, u32[]{:S(2)}, u32[]{:S(2)}) %collective-permute-start.2) | collective-permute-done | bytes 786464 | tf_op jit(solution)/shard_map/ppermute | solution.py:18
  70.4 7.4 %fusion.1 = f32[4,512,128]{1,2,0:T(8,128)} fusion(f32[512,4,6,128]{3,0,2,1:T(8,128)} %bitcast.161, bf16[4,6,128,128]{3,2,1,0:T(8,128)(2,1)S(1)} %copy-done), kind=kOutput, calls=%fused_computation.17 | convolution fusion | flops 2416181248 | bytes 8126464 | tf_op jit(solution)/shard_map/mbtj,btij->mbi/dot_general | solution.py:30
  82.5 16.6 %collective-permute-done.4 = f32[512,384]{1,0:T(8,128)S(1)} collective-permute-done((f32[512,384]{1,0:T(8,128)S(1)}, f32[512,384]{1,0:T(8,128)S(1)}, u32[]{:S(2)}, u32[]{:S(2)}) %collective-permute-start.4) | collective-permute-done | bytes 786464 | tf_op jit(solution)/shard_map/ppermute | solution.py:18
  107.1 6.5 fusion.2
  116.5 16.6 %collective-permute-done.6 = f32[512,384]{0,1:T(8,128)S(1)} collective-permute-done((f32[512,384]{0,1:T(8,128)S(1)}, f32[512,384]{0,1:T(8,128)S(1)}, u32[]{:S(2)}, u32[]{:S(2)}) %collective-permute-start.6) | collective-permute-done | bytes 786464 | tf_op jit(solution)/shard_map/ppermute | solution.py:18
  140.6 7.4 %fusion.3 = f32[4,512,128]{1,2,0:T(8,128)} fusion(f32[512,4,6,128]{3,0,2,1:T(8,128)} %bitcast.159, bf16[4,6,128,128]{3,2,1,0:T(8,128)(2,1)S(1)} %copy-done), kind=kOutput, calls=%fused_computation.19 | convolution fusion | flops 2416181248 | bytes 8126464 | tf_op jit(solution)/shard_map/mbtj,btij->mbi/dot_general | solution.py:30
  150.8 32.8 %all-gather.3.cloned.1.call-done = f32[1024,512]{1,0:T(8,128)} async-done(((f32[512,512]{1,0:T(8,128)}), f32[1024,512]{1,0:T(8,128)}) %all-gather.3.cloned.1.call-update) | async-done | bytes 2097168 | tf_op jit(solution)/shard_map/all_gather | solution.py:50
  183.6 6.7 fusion.72
  190.4 98.0 %all-reduce.3.cloned.1.call-done = f32[512,1024]{0,1:T(8,128)} async-done(((f32[512,1024]{0,1:T(8,128)}), f32[512,1024]{0,1:T(8,128)}) %all-reduce.3.cloned.1.call-update) | async-done | bytes 2097168 | tf_op jit(solution)/shard_map/psum | solution.py:52
  288.5 57.5 %all-gather.5.cloned.1.call-done = f32[1024,1024]{0,1:T(8,128)} async-done(((f32[512,1024]{0,1:T(8,128)}), f32[1024,1024]{0,1:T(8,128)}) %all-gather.5.cloned.1.call-update) | async-done | bytes 4194320 | tf_op jit(solution)/shard_map/all_gather | solution.py:53
  345.9 5.7 copy.29
  351.7 4.4 fusion
  358.1 11.7 %cholesky.223 = f32[128,128]{1,0:T(8,128)S(1)} custom-call(f32[128,128]{1,0:T(8,128)S(1)} %cholesky.580), custom_call_target="Cholesky" | custom-call | tf_op jit(solution)/shard_map/jit(cholesky)/cholesky | solution.py:54
  369.8 9.8 %custom-call.62 = f32[1,128,128]{1,2,0:T(8,128)S(1)} custom-call(f32[1,128,128]{2,1,0:T(8,128)S(1)} %get-tuple-element.77), custom_call_target="InvertDiagBlocksLowerTriangular" | custom-call | tf_op jit(solution)/shard_map/jit(cholesky)/cholesky | solution.py:54
  386.1 11.9 %cholesky.244 = f32[128,128]{1,0:T(8,128)S(1)} custom-call(f32[128,128]{1,0:T(8,128)S(1)} %cholesky.584), custom_call_target="Cholesky" | custom-call | tf_op jit(solution)/shard_map/jit(cholesky)/cholesky | solution.py:54
  398.6 9.8 %custom-call.63 = f32[1,128,128]{1,2,0:T(8,128)S(1)} custom-call(f32[1,128,128]{2,1,0:T(8,128)S(1)} %get-tuple-element.74), custom_call_target="InvertDiagBlocksLowerTriangular" | custom-call | tf_op jit(solution)/shard_map/jit(cholesky)/cholesky | solution.py:54
  411.7 11.7 %cholesky.468 = f32[128,128]{1,0:T(8,128)S(1)} custom-call(f32[128,128]{1,0:T(8,128)S(1)} %cholesky.589), custom_call_target="Cholesky" | custom-call | tf_op jit(solution)/shard_map/jit(cholesky)/cholesky | solution.py:54
  424.7 9.8 %custom-call.64 = f32[1,128,128]{1,2,0:T(8,128)S(1)} custom-call(f32[1,128,128]{2,1,0:T(8,128)S(1)} %get-tuple-element.71), custom_call_target="InvertDiagBlocksLowerTriangular" | custom-call | tf_op jit(solution)/shard_map/jit(cholesky)/cholesky | solution.py:54
  438.0 11.9 %cholesky.487 = f32[128,128]{1,0:T(8,128)S(1)} custom-call(f32[128,128]{1,0:T(8,128)S(1)} %cholesky.594), custom_call_target="Cholesky" | custom-call | tf_op jit(solution)/shard_map/jit(cholesky)/cholesky | solution.py:54
  451.3 9.8 %custom-call.65 = f32[1,128,128]{1,2,0:T(8,128)S(1)} custom-call(f32[1,128,128]{2,1,0:T(8,128)S(1)} %get-tuple-element.68), custom_call_target="InvertDiagBlocksLowerTriangular" | custom-call | tf_op jit(solution)/shard_map/jit(cholesky)/cholesky | solution.py:54
  464.5 11.7 %cholesky.506 = f32[128,128]{1,0:T(8,128)S(1)} custom-call(f32[128,128]{1,0:T(8,128)S(1)} %cholesky.599), custom_call_target="Cholesky" | custom-call | tf_op jit(solution)/shard_map/jit(cholesky)/cholesky | solution.py:54
  477.5 10.2 %custom-call.66 = f32[1,128,128]{1,2,0:T(8,128)S(1)} custom-call(f32[1,128,128]{2,1,0:T(8,128)S(1)} %get-tuple-element.65), custom_call_target="InvertDiagBlocksLowerTriangular" | custom-call | tf_op jit(solution)/shard_map/jit(cholesky)/cholesky | solution.py:54
  491.1 11.7 %cholesky.526 = f32[128,128]{1,0:T(8,128)S(1)} custom-call(f32[128,128]{1,0:T(8,128)S(1)} %cholesky.604), custom_call_target="Cholesky" | custom-call | tf_op jit(solution)/shard_map/jit(cholesky)/cholesky | solution.py:54
  504.1 9.8 %custom-call.67 = f32[1,128,128]{1,2,0:T(8,128)S(1)} custom-call(f32[1,128,128]{2,1,0:T(8,128)S(1)} %get-tuple-element.62), custom_call_target="InvertDiagBlocksLowerTriangular" | custom-call | tf_op jit(solution)/shard_map/jit(cholesky)/cholesky | solution.py:54
  516.9 11.9 %cholesky.546 = f32[128,128]{1,0:T(8,128)S(1)} custom-call(f32[128,128]{1,0:T(8,128)S(1)} %cholesky.609), custom_call_target="Cholesky" | custom-call | tf_op jit(solution)/shard_map/jit(cholesky)/cholesky | solution.py:54
  530.0 9.8 %custom-call.68 = f32[1,128,128]{1,2,0:T(8,128)S(1)} custom-call(f32[1,128,128]{2,1,0:T(8,128)S(1)} %get-tuple-element.59), custom_call_target="InvertDiagBlocksLowerTriangular" | custom-call | tf_op jit(solution)/shard_map/jit(cholesky)/cholesky | solution.py:54
  542.4 11.7 %cholesky.564 = f32[128,128]{1,0:T(8,128)S(1)} custom-call(f32[128,128]{1,0:T(8,128)S(1)} %convolution_subtract_fusion.13), custom_call_target="Cholesky" | custom-call | tf_op jit(solution)/shard_map/jit(cholesky)/cholesky | solution.py:54
  561.1 4.9 select_select_fusion
  566.0 27.7 %while.1 = (s32[]{:T(128)}, f32[1024,1024]{1,0:T(8,128)}, s32[8,2]{0,1:T(2,128)S(1)}, f32[8,128,128]{2,1,0:T(8,128)}, s32[]{:T(128)}) while((s32[]{:T(128)}, f32[1024,1024]{1,0:T(8,128)}, s32[8,2]{0,1:T(2,128)S(1)}, f32[8,128,128]{2,1,0:T(8,128)}, s32[]{:T(128)}) %tuple.61), condition=%wide.while_cond, body=%wide.while_body.sunk | while | flops 2 | bytes 132205 | solution.py:55
  593.8 79.6 %custom-call.69 = f32[8,128,128]{1,2,0:T(8,128)S(1)} custom-call(f32[8,128,128]{2,1,0:T(8,128)} %get-tuple-element.12), custom_call_target="InvertDiagBlocksLowerTriangular" | custom-call | tf_op jit(solution)/shard_map/triangular_solve | solution.py:55
  (143 shorter events, 130.0 us)
Async XLA Ops:
  6.5 32.3 %copy-start = (bf16[4,6,128,128]{3,2,1,0:T(8,128)(2,1)S(1)}, bf16[4,6,128,128]{3,2,1,0:T(8,128)(2,1)}, u32[]{:S(2)}) copy-start(bf16[4,6,128,128]{3,2,1,0:T(8,128)(2,1)} %param.3) | copy-start | bytes 2359300
  6.5 4.8 copy-start.8
  6.5 177.1 %all-gather.3.cloned.1.call-start = ((), (), s32[]{:S(2)}) async-start(), calls=%async_computation | async-start | bytes 3145728 | tf_op jit(solution)/shard_map/all_gather | solution.py:50
  9.5 19.4 %collective-permute-start = (f32[512,384]{0,1:T(8,128)}, f32[512,384]{0,1:T(8,128)S(1)}, u32[]{:S(2)}, u32[]{:S(2)}) collective-permute-start(f32[512,384]{0,1:T(8,128)} %get-tuple-element.29), channel_id=1, source_target_pairs={{0,2},{2,4},{4,6},{6,8},{8,10},{10,12},{12,14},{14,16},{16,18},{18... | collective-permute-start | bytes 2359304 | tf_op jit(solution)/shard_map/ppermute | solution.py:18
  11.3 20.1 %collective-permute-start.1 = (f32[512,384]{0,1:T(8,128)}, f32[512,384]{0,1:T(8,128)S(1)}, u32[]{:S(2)}, u32[]{:S(2)}) collective-permute-start(f32[512,384]{0,1:T(8,128)} %get-tuple-element.30), channel_id=1, source_target_pairs={{2,0},{4,2},{6,4},{8,6},{10,8},{12,10},{14,12},{16,14},{18,16},{20... | collective-permute-start | bytes 2359304 | tf_op jit(solution)/shard_map/ppermute | solution.py:19
  45.3 19.4 %copy-start.3 = (f32[4,512,128,1]{1,2,3,0:T(8,128)}, f32[4,512,128,1]{1,2,3,0:T(8,128)S(1)}, u32[]{:S(2)}) copy-start(f32[4,512,128,1]{1,2,3,0:T(8,128)S(1)} %fusion.71) | copy-start | bytes 3145732
  45.5 17.4 %collective-permute-start.2 = (f32[512,384]{0,1:T(8,128)S(1)}, f32[512,384]{0,1:T(8,128)S(1)}, u32[]{:S(2)}, u32[]{:S(2)}) collective-permute-start(f32[512,384]{0,1:T(8,128)S(1)} %get-tuple-element.27), channel_id=1, source_target_pairs={{0,2},{2,4},{4,6},{6,8},{8,10},{10,12},{12,14},{14,16},{16,18},{18... | collective-permute-start | bytes 2359304 | tf_op jit(solution)/shard_map/ppermute | solution.py:18
  45.5 17.4 %collective-permute-start.3 = (f32[512,384]{0,1:T(8,128)S(1)}, f32[512,384]{0,1:T(8,128)S(1)}, u32[]{:S(2)}, u32[]{:S(2)}) collective-permute-start(f32[512,384]{0,1:T(8,128)S(1)} %get-tuple-element.28), channel_id=1, source_target_pairs={{2,0},{4,2},{6,4},{8,6},{10,8},{12,10},{14,12},{16,14},{18,16},{20... | collective-permute-start | bytes 2359304 | tf_op jit(solution)/shard_map/ppermute | solution.py:19
  77.8 1.7 copy-start.7
  79.6 19.4 %copy-start.1 = (f32[512,512]{1,0:T(8,128)}, f32[512,512]{1,0:T(8,128)S(1)}, u32[]{:S(2)}) copy-start(f32[512,512]{1,0:T(8,128)S(1)} %sub.19) | copy-start | bytes 3145732
  79.8 19.3 %collective-permute-start.4 = (f32[512,384]{1,0:T(8,128)S(1)}, f32[512,384]{1,0:T(8,128)S(1)}, u32[]{:S(2)}, u32[]{:S(2)}) collective-permute-start(f32[512,384]{1,0:T(8,128)S(1)} %get-tuple-element.25), channel_id=1, source_target_pairs={{0,2},{2,4},{4,6},{6,8},{8,10},{10,12},{12,14},{14,16},{16,18},{18... | collective-permute-start | bytes 2359304 | tf_op jit(solution)/shard_map/ppermute | solution.py:18
  82.3 16.7 %collective-permute-start.5 = (f32[512,384]{1,0:T(8,128)S(1)}, f32[512,384]{1,0:T(8,128)S(1)}, u32[]{:S(2)}, u32[]{:S(2)}) collective-permute-start(f32[512,384]{1,0:T(8,128)S(1)} %get-tuple-element.26), channel_id=1, source_target_pairs={{2,0},{4,2},{6,4},{8,6},{10,8},{12,10},{14,12},{16,14},{18,16},{20... | collective-permute-start | bytes 2359304 | tf_op jit(solution)/shard_map/ppermute | solution.py:19
  107.1 6.5 copy-start.4
  113.9 19.1 %collective-permute-start.6 = (f32[512,384]{0,1:T(8,128)S(1)}, f32[512,384]{0,1:T(8,128)S(1)}, u32[]{:S(2)}, u32[]{:S(2)}) collective-permute-start(f32[512,384]{0,1:T(8,128)S(1)} %get-tuple-element.23), channel_id=1, source_target_pairs={{0,2},{2,4},{4,6},{6,8},{8,10},{10,12},{12,14},{14,16},{16,18},{18... | collective-permute-start | bytes 2359304 | tf_op jit(solution)/shard_map/ppermute | solution.py:18
  116.5 16.6 %collective-permute-start.7 = (f32[512,384]{0,1:T(8,128)S(1)}, f32[512,384]{0,1:T(8,128)S(1)}, u32[]{:S(2)}, u32[]{:S(2)}) collective-permute-start(f32[512,384]{0,1:T(8,128)S(1)} %get-tuple-element.24), channel_id=1, source_target_pairs={{2,0},{4,2},{6,4},{8,6},{10,8},{12,10},{14,12},{16,14},{18,16},{20... | collective-permute-start | bytes 2359304 | tf_op jit(solution)/shard_map/ppermute | solution.py:19
  147.9 1.7 copy-start.2
  150.8 137.6 %all-reduce.3.cloned.1.call-start = ((), (), s32[]{:S(2)}) async-start(), calls=%async_computation.1 | async-start | bytes 4194304 | tf_op jit(solution)/shard_map/psum | solution.py:52
  190.4 155.6 %all-gather.5.cloned.1.call-start = ((), (), s32[]{:S(2)}) async-start(), calls=%async_computation.2 | async-start | bytes 6291456 | tf_op jit(solution)/shard_map/all_gather | solution.py:53
  356.1 1.9 copy-start.5
  561.1 112.3 %copy-start.6 = (f32[1024,512]{1,0:T(8,128)S(1)}, f32[1024,512]{1,0:T(8,128)}, u32[]{:S(2)}) copy-start(f32[1024,512]{1,0:T(8,128)} %all-gather.3.cloned.1.call-done) | copy-start | bytes 6291460
Sparse Core Ops, SparseCore 0:
  150.9 32.6 all-gather.2
  190.5 97.8 all-reduce.2
  290.1 55.8 all-gather.4
where the time goes:
time: 708 us; the launch traced here: 697 us
  other arithmetic  269 us (38%)
  waiting for transfers between devices  258 us (36%)
  matrix products  73 us (10%)
  local copies, waits for them, and re-layouts  69.8 us (10%)
  between operations  18.8 us (3%)
  starting transfers between devices  7.65 us (1%)
    another operation x30, other arithmetic, body(): factor = jnp.linalg.cholesky(gram)  172 us
    psum x1, waiting for transfers between devices, body(): summed_rows = lax.psum(partial_rows, 'rows')  98 us
    another operation x3, other arithmetic, body(): lax.linalg.triangular_solve(factor, gathered, left_side=True, lower=True)  84.6 us
    ppermute x4, waiting for transfers between devices, with_halo(): before = lax.ppermute(last, axis, up)  67.5 us
    all_gather x1, waiting for transfers between devices, body(): gram = lax.all_gather(summed_rows, 'vecs', axis=0, tiled=True)  57.5 us
    all_gather x1, waiting for transfers between devices, body(): gathered = lax.all_gather(current, 'vecs', axis=0, tiled=True)  32.8 us
    another operation x24, local copies, waits for them, and re-layouts  27.7 us
    dot_general x4, matrix products, operate(): jnp.einsum('mbtj,btij->mbi', picked, tiles32, precision=lax.Precision.HIG...  27.7 us
  transfers between devices with their start and end apart: 11, of which 8 were waited for; matrix products, arithmetic and copies ran while one was open for 0% of the time, Pallas kernels for 0%

commit v1 on v0

v1 whole, which is shorter than its diff:
```python
import functools

import jax
import jax.numpy as jnp
from jax import lax
from jax.experimental import pallas as pl
from jax.experimental.pallas import tpu as pltpu
from jax.sharding import PartitionSpec as P

BS = 128
HB = 3
STEPS = 4
NB = 128
SUB = 8
CHUNKS = 2
NT = (((1,), (1,)), ((), ()))
NN = (((1,), (0,)), ((), ()))
SCALARS = pl.BlockSpec(memory_space=pltpu.SMEM)
WHOLE = pl.BlockSpec(memory_space=pltpu.VMEM)
AFAR = pl.BlockSpec(memory_space=pltpu.HBM)
ROOMY = pltpu.CompilerParams(vmem_limit_bytes=28 * 2 ** 20)


def split(x):
    high = x.astype(jnp.bfloat16)
    return high, (x - high.astype(jnp.float32)).astype(jnp.bfloat16)


def dot3(a, b, dims):
    def dot(x, y):
        return lax.dot_general(x, y, dims, preferred_element_type=jnp.float32)

    return dot(a[0], b[0]) + (dot(a[0], b[1]) + dot(a[1], b[0]))


def band_kernel(slots_ref, tiles_ref, band_ref):
    band_ref[...] = jnp.zeros_like(band_ref)
    for b in range(tiles_ref.shape[0]):
        for t in range(tiles_ref.shape[1]):
            start = pl.multiple_of(slots_ref[b, t] * BS, BS)
            flipped = tiles_ref[b, t].astype(jnp.float32).T
            band_ref[pl.ds(start, BS), b * BS:(b + 1) * BS] = flipped.astype(jnp.bfloat16)


def band_matrix(tiles, slots):
    blocks = tiles.shape[0]
    return pl.pallas_call(
        band_kernel,
        out_shape=jax.ShapeDtypeStruct(((blocks + 2 * HB) * BS, blocks * BS), jnp.bfloat16),
        in_specs=[SCALARS, WHOLE],
        out_specs=WHOLE,
        compiler_params=ROOMY,
        name="band_matrix",
    )(slots, tiles)


def step_kernel(has_previous, has_edges, *refs):
    before_ref, current_ref, after_ref, band_ref = refs[:4]
    outs = refs[4 + has_previous:]
    parts = [ref[...] for ref in (before_ref, current_ref, after_ref)]
    highs, lows = zip(*[split(part) for part in parts])
    high, low = jnp.concatenate(highs, axis=1), jnp.concatenate(lows, axis=1)
    columns = current_ref.shape[1]
    blocks = columns // BS
    halo = HB * BS
    for b in range(0, blocks, 2):
        end = min(b + 2, blocks)
        here = slice(b * BS, end * BS)
        depth = slice(b * BS, (end + 2 * HB) * BS)
        band = band_ref[depth, here]

        def dot(x):
            return jnp.dot(x[:, depth], band, preferred_element_type=jnp.float32)

        result = dot(high) + dot(low)
        if has_previous:
            result = 2.0 * result - refs[4][:, here]
        outs[0][:, here] = result
    if has_edges:
        outs[1][...] = outs[0][:, columns - halo:]
        outs[2][...] = outs[0][:, :halo]


def filter_step(halos, current, band, previous, has_edges):
    before, after = halos
    width, columns = current.shape
    f32 = jnp.float32
    edge = jax.ShapeDtypeStruct((width, HB * BS), f32)
    shapes = (jax.ShapeDtypeStruct((width, columns), f32),) + (edge, edge) * has_edges
    operands = (before, current, after, band) + ((previous,) if previous is not None else ())
    return pl.pallas_call(
        functools.partial(step_kernel, previous is not None, has_edges),
        out_shape=shapes,
        in_specs=[WHOLE] * len(operands),
        out_specs=(WHOLE,) * len(shapes),
        compiler_params=ROOMY,
        cost_estimate=pl.CostEstimate(
            flops=4 * width * columns * (2 + 2 * HB) * BS,
            bytes_accessed=4 * width * columns * 6,
            transcendentals=0,
        ),
        name="filter_step",
    )(*operands)


def exchange_edges(last, first):
    devices = lax.axis_size("rows")
    up = [(i, (i + 1) % devices) for i in range(devices)]
    down = [(j, i) for i, j in up]
    return lax.ppermute(last, "rows", up), lax.ppermute(first, "rows", down)


def chebyshev(tiles, slots, start_vectors):
    rows = start_vectors.shape[0] // CHUNKS
    halo = HB * BS
    current = [start_vectors[c * rows:(c + 1) * rows] for c in range(CHUNKS)]
    previous = [None] * CHUNKS
    halos = [exchange_edges(x[:, x.shape[1] - halo:], x[:, :halo]) for x in current]
    band = band_matrix(tiles, slots)
    for step in range(STEPS):
        more = step < STEPS - 1
        for c in range(CHUNKS):
            following, *edges = filter_step(halos[c], current[c], band, previous[c], more)
            previous[c], current[c] = current[c], following
            if more:
                halos[c] = exchange_edges(*edges)
    return current


def lane(x, j):
    return jnp.broadcast_to(x[:, j:j + 1], x.shape)


def row(x, i):
    return jnp.broadcast_to(x[i:i + 1, :], x.shape)


def total_of(terms):
    while len(terms) > 1:
        terms = [x + y for x, y in zip(terms[::2], terms[1::2])] + terms[len(terms) & ~1:]
    return terms[0]


def small_factor(columns):
    a = {(i, j): row(columns[j], i) for j in range(SUB) for i in range(j, SUB)}
    factor, inverse = {}, {}
    for j in range(SUB):
        root = lax.rsqrt(a[j, j])
        inverse[j, j] = root
        for i in range(j + 1, SUB):
            factor[i, j] = a[i, j] * root
        for k in range(j + 1, SUB):
            for i in range(k, SUB):
                a[i, k] = a[i, k] - factor[i, j] * factor[k, j]
        for k in range(j):
            terms = [factor[j, i] * inverse[i, k] for i in range(k, j)]
            inverse[j, k] = total_of(terms) * -root
    return inverse


def inverse_factor(block):
    strips = NB // SUB
    left = [block[SUB * t:SUB * (t + 1), :] for t in range(strips)]
    rows = lax.broadcasted_iota(jnp.int32, (SUB, NB), 0)
    lanes = lax.broadcasted_iota(jnp.int32, (SUB, NB), 1)
    right = [jnp.where(lanes == rows + SUB * t, 1.0, 0.0) for t in range(strips)]
    done = []
    columns = [lane(left[0], j) for j in range(SUB)]
    for s in range(strips):
        inverse = small_factor(columns)
        factors = {}
        for t in range(s + 1, strips):
            old = [lane(left[t], SUB * s + j) for j in range(SUB)]
            factors[t] = [
                total_of([old[m] * inverse[j, m] for m in range(j + 1)]) for j in range(SUB)
            ]
            if t == s + 1:
                ahead = [lane(left[t], SUB * t + j) for j in range(SUB)]
                columns = [
                    ahead[j] - total_of([x * row(x, j) for x in factors[t]]) for j in range(SUB)
                ]
        upper_rows = [row(left[s], j) for j in range(SUB)]
        solved_rows = [row(right[s], j) for j in range(SUB)]
        spread = []
        for j in range(SUB):
            column = jnp.where(rows == j, inverse[j, j], 0.0)
            for i in range(j + 1, SUB):
                column = jnp.where(rows == i, inverse[i, j], column)
            spread.append(column)
        upper = total_of([x * y for x, y in zip(spread, upper_rows)])
        solved = total_of([x * y for x, y in zip(spread, solved_rows)])
        done.append(solved)
        upper_rows = [row(upper, j) for j in range(SUB)]
        solved_rows = [row(solved, j) for j in range(SUB)]
        for t in range(s + 1, strips):
            left[t] = left[t] - total_of([x * y for x, y in zip(factors[t], upper_rows)])
            right[t] = right[t] - total_of([x * y for x, y in zip(factors[t], solved_rows)])
    return jnp.concatenate(done, axis=0)


def eliminate(gram_ref, field_ref, low, done, total_ref, steps):
    for ref in (*low, *done):
        ref[...] = jnp.zeros_like(ref)

    def step(k, carry):
        here = pl.ds(pl.multiple_of(k * NB, NB), NB)
        mine = (low[0][here, :], low[1][here, :])
        block = gram_ref[here, here] - dot3(mine, mine, NT)
        inverse = split(inverse_factor(block))
        column = gram_ref[:, here] - dot3((low[0][...], low[1][...]), mine, NT)
        field = field_ref[here, :] - dot3(mine, (done[0][...], done[1][...]), NN)
        low[0][:, here], low[1][:, here] = split(dot3(split(column), inverse, NT))
        solved = dot3(inverse, split(field), NN)
        total_ref[here, :] = solved
        done[0][here, :], done[1][here, :] = split(solved)
        return carry

    lax.fori_loop(0, steps, step, 0)


def elimination_scratch(size, columns):
    shapes = ((size, size), (size, columns))
    return [pltpu.VMEM(shape, jnp.bfloat16) for shape in shapes for part in range(2)]


def factor_kernel(scale, place_ref, gram_ref, field_ref, out_ref, low0, low1, done0, done1, total):
    width = out_ref.shape[0]
    place = place_ref[0]
    steps = ((place + 1) * width + NB - 1) // NB
    eliminate(gram_ref, field_ref, (low0, low1), (done0, done1), total, steps)
    out_ref[...] = total[pl.ds(pl.multiple_of(place * width, SUB), width), :] * scale


def factor_and_solve(gram, field, place, width, scale):
    size, columns = field.shape
    return pl.pallas_call(
        functools.partial(factor_kernel, scale),
        out_shape=jax.ShapeDtypeStruct((width, columns), jnp.float32),
        in_specs=[SCALARS, WHOLE, WHOLE],
        out_specs=WHOLE,
        scratch_shapes=elimination_scratch(size, columns)
        + [pltpu.VMEM((size, columns), jnp.float32)],
        compiler_params=ROOMY,
        name="factor_and_solve",
    )(place, gram, field)


def joined(refs):
    return jnp.concatenate([ref[...] for ref in refs], axis=0)


def scatter_order(start, rows):
    quarter = start // (rows // 4)
    return ((quarter % 2) * 2 + quarter // 2 - quarter) * (rows // 4) + start


def own_gram_kernel(*refs):
    field, out_ref = joined(refs[:-1]), refs[-1]
    high, low = split(field)
    rows, unit = out_ref.shape[0], NB // 2
    for i in range(field.shape[0] // NB):
        here = slice(i * NB, (i + 1) * NB)
        end = (i + 1) * NB
        product = dot3((high[here], low[here]), (high[:end], low[:end]), NT)
        for j in range(i + 1):
            for part in range(0, NB, unit):
                start = scatter_order((i * (i + 1) // 2 + j) * NB + part, rows)
                out_ref[start:start + unit, :] = product[part:part + unit, j * NB:(j + 1) * NB]


def own_gram(field):
    blocks = sum(part.shape[0] for part in field) // NB
    rows = blocks * (blocks + 1) // 2 * NB
    return pl.pallas_call(
        own_gram_kernel,
        out_shape=jax.ShapeDtypeStruct((rows, NB), jnp.float32),
        in_specs=[WHOLE] * len(field),
        out_specs=WHOLE,
        compiler_params=ROOMY,
        name="own_gram",
    )(*field)


def cross_gram_kernel(*refs):
    half = (len(refs) - 1) // 2
    out_ref = refs[-1]
    mine, other = split(joined(refs[:half])), split(joined(refs[half:-1]))
    rows = out_ref.shape[0]
    blocks = mine[0].shape[0] // NB
    for i in range(blocks):
        here = slice(i * NB, (i + 1) * NB)
        product = dot3((mine[0][here], mine[1][here]), other, NT)
        for j in range(blocks):
            start = scatter_order((i * blocks + j) * NB, rows)
            out_ref[start:start + NB, :] = product[:, j * NB:(j + 1) * NB]


def cross_gram(field, other):
    size = sum(part.shape[0] for part in field)
    return pl.pallas_call(
        cross_gram_kernel,
        out_shape=jax.ShapeDtypeStruct((size * size // NB, NB), jnp.float32),
        in_specs=[WHOLE] * (2 * len(field)),
        out_specs=WHOLE,
        compiler_params=ROOMY,
        name="cross_gram",
    )(*field, *other)


def fetch(pairs, sems):
    copies = [pltpu.make_async_copy(x, y, sems.at[i]) for i, (x, y) in enumerate(pairs)]
    for copy in copies:
        copy.start()
    for copy in copies:
        copy.wait()


def rows_of(ref, start, rows):
    return ref.at[pl.ds(pl.multiple_of(start, SUB), rows), :]


def stacked(parts, target, columns):
    rows = parts[0].shape[0]
    return [(part, target.at[i * rows:(i + 1) * rows, :columns]) for i, part in enumerate(parts)]


def lower_blocks(flat, gram_ref):
    blocks = gram_ref.shape[0] // NB
    for i in range(blocks):
        for j in range(blocks):
            place = i * (i + 1) // 2 + j
            block = flat[place * NB:(place + 1) * NB, :] if j <= i else jnp.zeros((NB, NB), jnp.float32)
            gram_ref[i * NB:(i + 1) * NB, j * NB:(j + 1) * NB] = block


def first_half_kernel(where_ref, *refs):
    pieces, mine, other = refs[:4], refs[4:4 + CHUNKS], refs[4 + CHUNKS:4 + 2 * CHUNKS]
    top_ref, inverse_ref, flat, gram, field, total, low0, low1, done0, done1, sems = refs[4 + 2 * CHUNKS:]
    place, near, far = where_ref[0], where_ref[1], where_ref[2]
    size, columns = top_ref.shape
    rows = pieces[0].shape[1]
    pairs = [
        (piece.at[j], rows_of(flat, ((near ^ i) * 4 + (far ^ j)) * rows, rows))
        for i, piece in enumerate(pieces) for j in range(4)
    ]

    @pl.when(place == 0)
    def _():
        fetch(pairs + stacked(mine, field, columns), sems)

    @pl.when(place != 0)
    def _():
        fetch(pairs + stacked(other, field, columns), sems)

    lower_blocks(flat, gram)
    rows = lax.broadcasted_iota(jnp.int32, (size, size), 0)
    lanes = lax.broadcasted_iota(jnp.int32, (size, size), 1)
    field[:, columns:] = jnp.where(rows == lanes, 1.0, 0.0)
    eliminate(gram, field, (low0, low1), (done0, done1), total, size // NB)
    top_ref[...] = total[:, :columns]
    inverse_ref[...] = total[:, columns:]


def first_half(where, pieces, mine, other):
    size, columns = sum(part.shape[0] for part in mine), mine[0].shape[1]
    f32 = jnp.float32
    flat_rows = 4 * pieces[0].shape[0] * pieces[0].shape[1]
    operands = (*pieces, *mine, *other)
    shapes = ((size, columns), (size, size))
    return pl.pallas_call(
        first_half_kernel,
        out_shape=tuple(jax.ShapeDtypeStruct(shape, f32) for shape in shapes),
        in_specs=[SCALARS] + [AFAR] * len(operands),
        out_specs=(WHOLE, WHOLE),
        scratch_shapes=[
            pltpu.VMEM((flat_rows, NB), f32),
            pltpu.VMEM((size, size), f32),
            pltpu.VMEM((size, columns + size), f32),
            pltpu.VMEM((size, columns + size), f32),
        ] + elimination_scratch(size, columns + size) + [pltpu.SemaphoreType.DMA((16 + CHUNKS,))],
        compiler_params=ROOMY,
        cost_estimate=pl.CostEstimate(flops=2 * 10 ** 10, bytes_accessed=10 ** 7, transcendentals=0),
        name="first_half",
    )(where, *operands)


def second_half_kernel(scale, where_ref, *refs):
    rest, mine = refs[0], refs[1:1 + CHUNKS]
    top_ref, inverse_ref, out_ref = refs[1 + CHUNKS:4 + CHUNKS]
    flat, corner, gram, field, total, low0, low1, done0, done1, sems = refs[4 + CHUNKS:]
    place = where_ref[0]
    size, columns = top_ref.shape
    blocks = size // NB
    rows = rest.shape[2] - NB

    @pl.when(place == 0)
    def _():
        out_ref[...] = top_ref[...] * scale

    @pl.when(place != 0)
    def _():
        pairs = stacked(mine, field, columns)
        for i in range(4):
            for j in range(4):
                pairs.append((rest.at[i, j, :rows], rows_of(flat, (i * 4 + j) * rows, rows)))
                pairs.append((rest.at[i, j, rows:], corner.at[i * NB:(i + 1) * NB, j * NB:(j + 1) * NB]))
        fetch(pairs, sems)
        lower_blocks(flat, gram)
        low = split(dot3(split(corner[...]), split(inverse_ref[...]), NT))
        gram[...] = gram[...] - dot3(low, low, NT)
        field[...] = field[...] - dot3(low, split(top_ref[...]), NN)
        eliminate(gram, field, (low0, low1), (done0, done1), total, blocks)
        out_ref[...] = total[...] * scale


def second_half(where, rest, mine, top, inverse, scale):
    size, columns = top.shape
    f32 = jnp.float32
    return pl.pallas_call(
        functools.partial(second_half_kernel, scale),
        out_shape=jax.ShapeDtypeStruct((size, columns), f32),
        in_specs=[SCALARS] + [AFAR] * (1 + CHUNKS) + [WHOLE] * 2,
        out_specs=WHOLE,
        scratch_shapes=[
            pltpu.VMEM((16 * (rest.shape[2] - NB), NB), f32),
            pltpu.VMEM((size, size), f32),
            pltpu.VMEM((size, size), f32),
            pltpu.VMEM((size, columns), f32),
            pltpu.VMEM((size, columns), f32),
        ] + elimination_scratch(size, columns) + [pltpu.SemaphoreType.DMA((32 + CHUNKS,))],
        compiler_params=ROOMY,
        name="second_half",
    )(where, rest, *mine, top, inverse)


NEAR, FAR = 1, 4


def send(x, stride, planes=None):
    devices, sides = lax.axis_size("rows"), lax.axis_size("vecs")
    pairs = [
        (i * sides + v, (i ^ stride) * sides + v)
        for i in range(devices) for v in (range(sides) if planes is None else planes)
    ]
    return lax.ppermute(x, ("rows", "vecs"), pairs)


def send_up(x, stride):
    devices, sides = lax.axis_size("rows"), lax.axis_size("vecs")
    pairs = [(i * sides, (i ^ stride) * sides + 1) for i in range(devices)]
    return lax.ppermute(x, ("rows", "vecs"), pairs)


def swap_half(x, bit, stride, planes=None):
    halves = x.reshape(2, -1, NB)
    kept = lax.dynamic_index_in_dim(halves, bit, 0, keepdims=False)
    given = lax.dynamic_index_in_dim(halves, 1 - bit, 0, keepdims=False)
    return kept + send(given, stride, planes)


def reduce_group(x, here, stride, planes=None):
    parts = x.reshape(4, -1, NB)
    total = lax.dynamic_index_in_dim(parts, here, 0, keepdims=False)
    others = [
        send(lax.dynamic_index_in_dim(parts, here ^ i, 0, keepdims=False), i * stride, planes)
        for i in range(1, 4)
    ]
    return total + others[0] + (others[1] + others[2])


def orthonormalize_planes(current, scale):
    together = lax.optimization_barrier
    rank = lax.axis_index("rows")
    place = lax.axis_index("vecs")
    near, far = rank % 4, rank // 4
    where = jnp.stack([place, near, far]).astype(jnp.int32)
    near_groups = [list(range(4 * g, 4 * g + 4)) for g in range(4)]
    far_groups = [list(range(g, 16, 4)) for g in range(4)]
    below = [send_up(part, 0) for part in current]
    own, below[0] = together((current, below[0]))
    half = swap_half(own_gram(own), near % 2, 1)
    fourth = swap_half(half, near // 2, 2)
    fourth, *below = together((fourth, *below))
    corner = cross_gram(current, below)
    corner = swap_half(corner, near % 2, 1, (1,))
    mine = reduce_group(fourth, far, FAR)
    mine, corner = together((mine, corner))
    first = jnp.where(place == 0, mine, send_up(mine, 0))
    corner = swap_half(corner, near // 2, 2, (1,))
    first, corner = together((first, corner))
    first = jnp.stack([first] + [send(first, i * FAR) for i in range(1, 4)])
    corner = reduce_group(corner, far, FAR, (1,))
    first, corner = together((first, corner))
    rest = jnp.concatenate([mine, corner], axis=0)
    rest = lax.all_gather(rest, "rows", axis_index_groups=far_groups)
    pieces = [first] + [send(first, i * NEAR) for i in range(1, 4)]
    pieces, rest = together((pieces, rest))
    rest = lax.all_gather(rest, "rows", axis_index_groups=near_groups)
    top, inverse = first_half(where, pieces, current, below)
    return second_half(where, rest, current, top, inverse, scale)


def orthonormalize(current, scale):
    current = jnp.concatenate(current, axis=0)
    width = current.shape[0]
    gathered = lax.all_gather(current, "vecs", axis=0, tiled=True)
    partial_rows = jnp.einsum("mn,kn->mk", current, gathered, precision=lax.Precision.HIGHEST)
    summed_rows = lax.psum(partial_rows, "rows")
    gram = lax.all_gather(summed_rows, "vecs", axis=0, tiled=True)
    place = lax.axis_index("vecs").astype(jnp.int32)[None]
    return factor_and_solve(gram, gathered, place, width, scale)


def body(tiles, columns, start_vectors):
    blocks_here = tiles.shape[0]
    total_blocks = blocks_here * lax.axis_size("rows")
    first_block = lax.axis_index("rows") * blocks_here
    global_rows = first_block + jnp.arange(blocks_here, dtype=jnp.int32)
    offsets = jnp.mod(columns - global_rows[:, None] + HB, total_blocks)
    slots = jnp.arange(blocks_here, dtype=jnp.int32)[:, None] + offsets
    current = chebyshev(tiles, slots, start_vectors)
    scale = float((total_blocks * BS) ** 0.5)
    fits = (
        lax.axis_size("vecs") == 2
        and lax.axis_size("rows") == 16
        and start_vectors.shape[0] == 4 * NB
    )
    return (orthonormalize_planes if fits else orthonormalize)(current, scale)


def solution(mesh):
    placed = (P("rows", None, None, None), P("rows", None), P("vecs", "rows"))
    return jax.shard_map(
        body, mesh=mesh, in_specs=placed, out_specs=P("vecs", "rows"), check_vma=False
    )
```

time: 708 us -> 231 us (0.33); the launches traced: 697 us -> 229 us
  other arithmetic: 269 us -> 0.37 us
  waiting for transfers between devices: 258 us -> 86.7 us
  matrix products: 73 us -> 0 us
  Pallas kernels: 0 us -> 58.2 us
  local copies, waits for them, and re-layouts: 69.8 us -> 13.8 us
  starting transfers between devices: 7.65 us -> 42.2 us
  blocking collectives: 0 us -> 13.4 us
    another operation x33 -> x2, other arithmetic: 257 us -> 0.09 us  [the longest x1 0.08 us: orthonormalize_planes(): where = jnp.stack([place, near, far]).astype(jnp.int32)]
    psum x1 -> x0, waiting for transfers between devices: 98 us -> none  [body(): summed_rows = lax.psum(partial_rows, 'rows')]
    all_gather x2 -> x1, waiting for transfers between devices: 90.2 us -> 0.02 us  [orthonormalize_planes(): rest = lax.all_gather(rest, 'rows', axis_index_groups=near_groups)]
    pallas_call x0 -> x13, Pallas kernels: none -> 58.2 us  [the longest x1 23.5 us: second_half(): pl.pallas_call(functools.partial(second_half_kernel, scale), out_shape=ja...]
    another operation x29 -> x0, matrix products: 38.6 us -> none  [the longest x14 23.1 us: body(): factor = jnp.linalg.cholesky(gram)]
    ppermute x8 -> x35, starting transfers between devices: 7.57 us -> 42.2 us  [the longest x16 29.3 us: send(): return lax.ppermute(x, ('rows', 'vecs'), pairs)]
    dot_general x5 -> x0, matrix products: 34.4 us -> none  [the longest x4 27.7 us: operate(): jnp.einsum('mbtj,btij->mbi', picked, tiles32, precision=lax.Precision.HIG...]
    another operation x33 -> x0, local copies, waits for them, and re-layouts: 30.3 us -> none
  transfers between devices with their start and end apart: 11 -> 36, of which waited for: 8 -> 22; matrix products, arithmetic and copies ran while one was open for 0% -> 1% of each run, Pallas kernels for 0% -> 13%
where the time goes in v1:
time: 231 us; the launch traced here: 229 us
  waiting for transfers between devices  86.7 us (38%)
  Pallas kernels  58.2 us (25%)
  starting transfers between devices  42.2 us (18%)
  between operations  13.9 us (6%)
  local copies, waits for them, and re-layouts  13.8 us (6%)
  blocking collectives  13.4 us (6%)
    ppermute x16, waiting for transfers between devices, exchange_edges(): return (lax.ppermute(last, 'rows', up), lax.ppermute(first, 'rows', down))  61.5 us
    ppermute x16, starting transfers between devices, send(): return lax.ppermute(x, ('rows', 'vecs'), pairs)  29.3 us
    pallas_call x1, Pallas kernels, second_half(): pl.pallas_call(functools.partial(second_half_kernel, scale), out_shape=ja...  23.5 us
    pallas_call x1, Pallas kernels, first_half(): pl.pallas_call(first_half_kernel, out_shape=tuple((jax.ShapeDtypeStruct(s...  21.4 us
    ppermute x16, waiting for transfers between devices, send(): return lax.ppermute(x, ('rows', 'vecs'), pairs)  17.5 us
    all_gather x1, blocking collectives, orthonormalize_planes(): rest = lax.all_gather(rest, 'rows', axis_index_groups=far_groups)  13.4 us
    ppermute x16, starting transfers between devices, exchange_edges(): return (lax.ppermute(last, 'rows', up), lax.ppermute(first, 'rows', down))  9.01 us
    unnamed x30, local copies, waits for them, and re-layouts  8.98 us
  transfers between devices with their start and end apart: 36, of which 22 were waited for; matrix products, arithmetic and copies ran while one was open for 1% of the time, Pallas kernels for 13%

profile of v1, /device:TPU:5, one launch (start us, length us, event | category | flops | bytes accessed | tf_op | source)
XLA Modules:
  0.0 228.7 jit_solution(10100551932540345832)
XLA Ops:
  6.5 2.6 %fusion.4 = (f32[256,384]{1,0:T(8,128)}, f32[256,384]{1,0:T(8,128)}, f32[256,384]{1,0:T(8,128)}, f32[256,384]{1,0:T(8,128)}) fusion(f32[512,512]{1,0:T(8,128)} %param.5), kind=kLoop, calls=%fused_computation.28 | loop fusion | bytes 3145728 | tf_op jit(solution)/shard_map/slice | solution.py:118
  9.1 1.8 collective-permute-start
  13.2 6.9 %collective-permute-done.refs_0_ = f32[256,384]{1,0:T(8,128)S(1)} collective-permute-done((f32[256,384]{1,0:T(8,128)}, f32[256,384]{1,0:T(8,128)S(1)}, u32[]{:S(2)}, u32[]{:S(2)}) %collective-permute-start) | collective-permute-done | bytes 393248 | tf_op jit(solution)/shard_map/ppermute | solution.py:110
  20.1 2.4 %collective-permute-done.1.refs_2_ = f32[256,384]{1,0:T(8,128)S(1)} collective-permute-done((f32[256,384]{1,0:T(8,128)}, f32[256,384]{1,0:T(8,128)S(1)}, u32[]{:S(2)}, u32[]{:S(2)}) %collective-permute-start.1) | collective-permute-done | bytes 393248 | tf_op jit(solution)/shard_map/ppermute | solution.py:110
  25.4 11.1 %collective-permute-done.2.refs_0_ = f32[256,384]{1,0:T(8,128)S(1)} collective-permute-done((f32[256,384]{1,0:T(8,128)S(1)}, f32[256,384]{1,0:T(8,128)S(1)}, u32[]{:S(2)}, u32[]{:S(2)}) %collective-permute-start.2) | collective-permute-done | bytes 393248 | tf_op jit(solution)/shard_map/ppermute | solution.py:110
  36.5 6.2 %collective-permute-done.3.refs_2_ = f32[256,384]{1,0:T(8,128)S(1)} collective-permute-done((f32[256,384]{1,0:T(8,128)S(1)}, f32[256,384]{1,0:T(8,128)S(1)}, u32[]{:S(2)}, u32[]{:S(2)}) %collective-permute-start.3) | collective-permute-done | bytes 393248 | tf_op jit(solution)/shard_map/ppermute | solution.py:110
  44.0 2.9 %collective-permute-done.9.refs_2_ = f32[256,384]{1,0:T(8,128)S(1)} collective-permute-done((f32[256,384]{1,0:T(8,128)S(1)}, f32[256,384]{1,0:T(8,128)S(1)}, u32[]{:S(2)}, u32[]{:S(2)}) %collective-permute-start.9) | collective-permute-done | bytes 393248 | tf_op jit(solution)/shard_map/ppermute | solution.py:110
  48.2 6.5 %collective-permute-done.4.refs_0_ = f32[256,384]{1,0:T(8,128)S(1)} collective-permute-done((f32[256,384]{1,0:T(8,128)S(1)}, f32[256,384]{1,0:T(8,128)S(1)}, u32[]{:S(2)}, u32[]{:S(2)}) %collective-permute-start.4) | collective-permute-done | bytes 393248 | tf_op jit(solution)/shard_map/ppermute | solution.py:110
  56.1 2.0 collective-permute-start.6
  58.9 9.0 %collective-permute-done.11.refs_2_ = f32[256,384]{1,0:T(8,128)S(1)} collective-permute-done((f32[256,384]{1,0:T(8,128)S(1)}, f32[256,384]{1,0:T(8,128)S(1)}, u32[]{:S(2)}, u32[]{:S(2)}) %collective-permute-start.11) | collective-permute-done | bytes 393248 | tf_op jit(solution)/shard_map/ppermute | solution.py:110
  69.3 2.3 %collective-permute-done.6.refs_0_ = f32[256,384]{1,0:T(8,128)S(1)} collective-permute-done((f32[256,384]{1,0:T(8,128)S(1)}, f32[256,384]{1,0:T(8,128)S(1)}, u32[]{:S(2)}, u32[]{:S(2)}) %collective-permute-start.6) | collective-permute-done | bytes 393248 | tf_op jit(solution)/shard_map/ppermute | solution.py:110
  79.9 7.1 %collective-permute-done.14.refs_0_ = f32[256,384]{1,0:T(8,128)S(1)} collective-permute-done((f32[256,384]{1,0:T(8,128)}, f32[256,384]{1,0:T(8,128)S(1)}, u32[]{:S(2)}, u32[]{:S(2)}) %collective-permute-start.14) | collective-permute-done | bytes 393248 | tf_op jit(solution)/shard_map/ppermute | solution.py:110
  87.7 2.5 %collective-permute-done.15.refs_2_ = f32[256,384]{1,0:T(8,128)} collective-permute-done((f32[256,384]{1,0:T(8,128)}, f32[256,384]{1,0:T(8,128)}, u32[]{:S(2)}, u32[]{:S(2)}) %collective-permute-start.15) | collective-permute-done | bytes 393248 | tf_op jit(solution)/shard_map/ppermute | solution.py:110
  91.2 1.7 filter_step.15.refs_1_.refs_5_.refs_2_
  96.1 5.6 %collective-permute-done.18 = f32[320,128]{1,0:T(8,128)S(1)} collective-permute-done((f32[320,128]{1,0:T(8,128)S(1)}, f32[320,128]{1,0:T(8,128)S(1)}, u32[]{:S(2)}, u32[]{:S(2)}) %collective-permute-start.18) | collective-permute-done | bytes 163872 | tf_op jit(solution)/shard_map/ppermute | solution.py:445
  101.7 7.6 %collective-permute-done.19.refs_3_.refs_7_ = f32[256,512]{1,0:T(8,128)S(1)} collective-permute-done((f32[256,512]{1,0:T(8,128)S(1)}, f32[256,512]{1,0:T(8,128)S(1)}, u32[]{:S(2)}, u32[]{:S(2)}) %collective-permute-start.19) | collective-permute-done | bytes 524320 | tf_op jit(solution)/shard_map/ppermute | solution.py:451
  109.3 3.4 %cross_gram.1 = f32[2048,128]{1,0:T(8,128)S(1)} custom-call(f32[256,512]{1,0:T(8,128)S(1)} %filter_step.11.refs_0_.refs_4_.refs_1_, f32[256,512]{1,0:T(8,128)S(1)} %filter_step.15.refs_1_.refs_5_.refs_2_, f32[256,512]{1,0:T(8,128)} %collective-permute-done.16.refs_2_.refs_6_, f32[256,512]{1,0:T(8,128)S(1)} %collective-permute-done.19.refs_3_.refs_7_), custom_call_target="tpu_custom_call" | custom-call | tf_op jit(solution)/shard_map/cross_gram/pallas_call | solution.py:300
  113.6 3.2 %collective-permute-start.23 = (f32[1024,128]{1,0:T(8,128)}, f32[1024,128]{1,0:T(8,128)S(1)}, u32[]{:S(2)}, u32[]{:S(2)}) collective-permute-start(f32[1024,128]{1,0:T(8,128)} %dynamic-slice_bitcast_fusion), channel_id=1, source_target_pairs={{1,3},{3,1},{5,7},{7,5},{9,11},{11,9},{13,15},{15,13},{17,19},{19,... | collective-permute-start | bytes 1572872 | tf_op jit(solution)/shard_map/ppermute | solution.py:445
  116.9 1.9 collective-permute-start.21
  118.8 1.6 collective-permute-start.22
  120.7 2.7 %collective-permute-done.22 = f32[80,128]{1,0:T(8,128)S(1)} collective-permute-done((f32[80,128]{1,0:T(8,128)S(1)}, f32[80,128]{1,0:T(8,128)S(1)}, u32[]{:S(2)}, u32[]{:S(2)}) %collective-permute-start.22) | collective-permute-done | bytes 40992 | tf_op jit(solution)/shard_map/ppermute | solution.py:445
  124.9 4.3 %collective-permute-start.25 = (f32[512,128]{1,0:T(8,128)S(1)}, f32[512,128]{1,0:T(8,128)S(1)}, u32[]{:S(2)}, u32[]{:S(2)}) collective-permute-start(f32[512,128]{1,0:T(8,128)S(1)} %dynamic-slice_bitcast_fusion.2), channel_id=1, source_target_pairs={{1,5},{3,7},{5,1},{7,3},{9,13},{11,15},{13,9},{15,11},{17,21},{19,... | collective-permute-start | bytes 786440 | tf_op jit(solution)/shard_map/ppermute | solution.py:445
  129.2 4.8 %collective-permute-done.25 = f32[512,128]{1,0:T(8,128)S(1)} collective-permute-done((f32[512,128]{1,0:T(8,128)S(1)}, f32[512,128]{1,0:T(8,128)S(1)}, u32[]{:S(2)}, u32[]{:S(2)}) %collective-permute-start.25) | collective-permute-done | bytes 262176 | tf_op jit(solution)/shard_map/ppermute | solution.py:445
  134.5 1.8 collective-permute-start.27
  137.8 1.9 collective-permute-start.29
  139.7 3.9 %collective-permute-start.30 = (f32[128,128]{1,0:T(8,128)S(1)}, f32[128,128]{1,0:T(8,128)S(1)}, u32[]{:S(2)}, u32[]{:S(2)}) collective-permute-start(f32[128,128]{1,0:T(8,128)S(1)} %get-tuple-element.86), channel_id=1, source_target_pairs={{1,17},{3,19},{5,21},{7,23},{9,25},{11,27},{13,29},{15,31},{17,1},... | collective-permute-start | bytes 196616 | tf_op jit(solution)/shard_map/ppermute | solution.py:445
  143.6 3.4 %collective-permute-start.31 = (f32[128,128]{1,0:T(8,128)S(1)}, f32[128,128]{1,0:T(8,128)S(1)}, u32[]{:S(2)}, u32[]{:S(2)}) collective-permute-start(f32[128,128]{1,0:T(8,128)S(1)} %get-tuple-element.85), channel_id=1, source_target_pairs={{1,25},{3,27},{5,29},{7,31},{9,17},{11,19},{13,21},{15,23},{17,9},... | collective-permute-start | bytes 196616 | tf_op jit(solution)/shard_map/ppermute | solution.py:445
  147.1 3.8 %collective-permute-done.31 = f32[128,128]{1,0:T(8,128)S(1)} collective-permute-done((f32[128,128]{1,0:T(8,128)S(1)}, f32[128,128]{1,0:T(8,128)S(1)}, u32[]{:S(2)}, u32[]{:S(2)}) %collective-permute-start.31) | collective-permute-done | bytes 65568 | tf_op jit(solution)/shard_map/ppermute | solution.py:445
  150.9 3.5 %collective-permute-start.32 = (f32[4,80,128]{2,1,0:T(8,128)S(1)}, f32[4,80,128]{2,1,0:T(8,128)S(1)}, u32[]{:S(2)}, u32[]{:S(2)}) collective-permute-start(f32[4,80,128]{2,1,0:T(8,128)S(1)} %pad_maximum_fusion.refs_0_), channel_id=1, source_target_pairs={{0,2},{1,3},{2,0},{3,1},{4,6},{5,7},{6,4},{7,5},{8,10},{9,11},{10,... | collective-permute-start | bytes 491528 | tf_op jit(solution)/shard_map/ppermute | solution.py:445
  156.1 13.4 %all-gather = f32[832,128]{1,0:T(8,128)} all-gather(f32[208,128]{1,0:T(8,128)S(1)} %pad_maximum_fusion.1), channel_id=2, replica_groups={{0,8,16,24},{2,10,18,26},{4,12,20,28},{6,14,22,30},{1,9,17,25},{3,11,19..., dimensions={0}, use_global_device_ids=true | all-gather | bytes 532480 | tf_op jit(solution)/shard_map/all_gather | solution.py:495
  175.4 21.4 %first_half.1 = (f32[512,512]{1,0:T(8,128)S(1)}, f32[512,512]{1,0:T(8,128)S(1)}) custom-call(s32[3]{0:T(128)S(1)} %pad_add_fusion.where_ref, f32[4,80,128]{2,1,0:T(8,128)S(1)} %pad_maximum_fusion.refs_0_, f32[4,80,128]{2,1,0:T(8,128)S(1)} %copy-done.7, f32[4,80,128]{2,1,0:T(8,128)S(1)} %copy-done.9, f32[4,80,128]{2,1,0:T(8,128)S(1)} %copy-done.11, ...), custom_call_target="tpu_custom_call" | custom-call | flops 20000000000 | bytes 10000000 | tf_op jit(solution)/shard_map/first_half/pallas_call | solution.py:370
  198.3 23.5 %second_half.1 = f32[512,512]{1,0:T(8,128)} custom-call(s32[3]{0:T(128)S(1)} %pad_add_fusion.where_ref, f32[4,4,208,128]{3,2,1,0:T(8,128)S(1)} %bitcast.55, f32[256,512]{1,0:T(8,128)S(1)} %filter_step.11.refs_0_.refs_4_.refs_1_, f32[256,512]{1,0:T(8,128)S(1)} %filter_step.15.refs_1_.refs_5_.refs_2_, f32[512,512]{1,0:T(8,128)S(1)} %get-tuple-element.77.refs_3_, ...), custom_call_target="tpu_custom_call" | custom-call | tf_op jit(solution)/shard_map/second_half/pallas_call | solution.py:419
  (105 shorter events, 38.1 us)
Async XLA Ops:
  6.5 190.3 %all-gather.4.cloned.1.call-start = ((), (), s32[]{:S(2)}) async-start(), calls=%async_computation | async-start | bytes 2129920 | tf_op jit(solution)/shard_map/all_gather | solution.py:498
  9.1 11.0 %collective-permute-start = (f32[256,384]{1,0:T(8,128)}, f32[256,384]{1,0:T(8,128)S(1)}, u32[]{:S(2)}, u32[]{:S(2)}) collective-permute-start(f32[256,384]{1,0:T(8,128)} %get-tuple-element.82), channel_id=1, source_target_pairs={{0,2},{2,4},{4,6},{6,8},{8,10},{10,12},{12,14},{14,16},{16,18},{18... | collective-permute-start | bytes 1179656 | tf_op jit(solution)/shard_map/ppermute | solution.py:110
  10.9 11.6 %collective-permute-start.1 = (f32[256,384]{1,0:T(8,128)}, f32[256,384]{1,0:T(8,128)S(1)}, u32[]{:S(2)}, u32[]{:S(2)}) collective-permute-start(f32[256,384]{1,0:T(8,128)} %get-tuple-element.81), channel_id=1, source_target_pairs={{2,0},{4,2},{6,4},{8,6},{10,8},{12,10},{14,12},{16,14},{18,16},{20... | collective-permute-start | bytes 1179656 | tf_op jit(solution)/shard_map/ppermute | solution.py:110
  23.3 13.2 %collective-permute-start.2 = (f32[256,384]{1,0:T(8,128)S(1)}, f32[256,384]{1,0:T(8,128)S(1)}, u32[]{:S(2)}, u32[]{:S(2)}) collective-permute-start(f32[256,384]{1,0:T(8,128)S(1)} %get-tuple-element.42), channel_id=1, source_target_pairs={{0,2},{2,4},{4,6},{6,8},{8,10},{10,12},{12,14},{14,16},{16,18},{18... | collective-permute-start | bytes 1179656 | tf_op jit(solution)/shard_map/ppermute | solution.py:110
  23.3 19.3 %collective-permute-start.3 = (f32[256,384]{1,0:T(8,128)S(1)}, f32[256,384]{1,0:T(8,128)S(1)}, u32[]{:S(2)}, u32[]{:S(2)}) collective-permute-start(f32[256,384]{1,0:T(8,128)S(1)} %get-tuple-element.44), channel_id=1, source_target_pairs={{2,0},{4,2},{6,4},{8,6},{10,8},{12,10},{14,12},{16,14},{18,16},{20... | collective-permute-start | bytes 1179656 | tf_op jit(solution)/shard_map/ppermute | solution.py:110
  23.8 20.1 %collective-permute-start.8 = (f32[256,384]{1,0:T(8,128)S(1)}, f32[256,384]{1,0:T(8,128)S(1)}, u32[]{:S(2)}, u32[]{:S(2)}) collective-permute-start(f32[256,384]{1,0:T(8,128)S(1)} %copy-done.13), channel_id=1, source_target_pairs={{0,2},{2,4},{4,6},{6,8},{8,10},{10,12},{12,14},{14,16},{16,18},{18... | collective-permute-start | bytes 1179656 | tf_op jit(solution)/shard_map/ppermute | solution.py:110
  25.1 21.7 %collective-permute-start.9 = (f32[256,384]{1,0:T(8,128)S(1)}, f32[256,384]{1,0:T(8,128)S(1)}, u32[]{:S(2)}, u32[]{:S(2)}) collective-permute-start(f32[256,384]{1,0:T(8,128)S(1)} %copy-done.12), channel_id=1, source_target_pairs={{2,0},{4,2},{6,4},{8,6},{10,8},{12,10},{14,12},{16,14},{18,16},{20... | collective-permute-start | bytes 1179656 | tf_op jit(solution)/shard_map/ppermute | solution.py:110
  43.4 11.3 %collective-permute-start.4 = (f32[256,384]{1,0:T(8,128)S(1)}, f32[256,384]{1,0:T(8,128)S(1)}, u32[]{:S(2)}, u32[]{:S(2)}) collective-permute-start(f32[256,384]{1,0:T(8,128)S(1)} %get-tuple-element.45), channel_id=1, source_target_pairs={{0,2},{2,4},{4,6},{6,8},{8,10},{10,12},{12,14},{14,16},{16,18},{18... | collective-permute-start | bytes 1179656 | tf_op jit(solution)/shard_map/ppermute | solution.py:110
  43.5 11.8 %collective-permute-start.5 = (f32[256,384]{1,0:T(8,128)S(1)}, f32[256,384]{1,0:T(8,128)S(1)}, u32[]{:S(2)}, u32[]{:S(2)}) collective-permute-start(f32[256,384]{1,0:T(8,128)S(1)} %get-tuple-element.47), channel_id=1, source_target_pairs={{2,0},{4,2},{6,4},{8,6},{10,8},{12,10},{14,12},{16,14},{18,16},{20... | collective-permute-start | bytes 1179656 | tf_op jit(solution)/shard_map/ppermute | solution.py:110
  47.6 11.3 %collective-permute-start.10 = (f32[256,384]{1,0:T(8,128)S(1)}, f32[256,384]{1,0:T(8,128)S(1)}, u32[]{:S(2)}, u32[]{:S(2)}) collective-permute-start(f32[256,384]{1,0:T(8,128)S(1)} %get-tuple-element.51), channel_id=1, source_target_pairs={{0,2},{2,4},{4,6},{6,8},{8,10},{10,12},{12,14},{14,16},{16,18},{18... | collective-permute-start | bytes 1179656 | tf_op jit(solution)/shard_map/ppermute | solution.py:110
  47.7 20.3 %collective-permute-start.11 = (f32[256,384]{1,0:T(8,128)S(1)}, f32[256,384]{1,0:T(8,128)S(1)}, u32[]{:S(2)}, u32[]{:S(2)}) collective-permute-start(f32[256,384]{1,0:T(8,128)S(1)} %get-tuple-element.53), channel_id=1, source_target_pairs={{2,0},{4,2},{6,4},{8,6},{10,8},{12,10},{14,12},{16,14},{18,16},{20... | collective-permute-start | bytes 1179656 | tf_op jit(solution)/shard_map/ppermute | solution.py:110
  56.1 15.5 %collective-permute-start.6 = (f32[256,384]{1,0:T(8,128)S(1)}, f32[256,384]{1,0:T(8,128)S(1)}, u32[]{:S(2)}, u32[]{:S(2)}) collective-permute-start(f32[256,384]{1,0:T(8,128)S(1)} %get-tuple-element.48), channel_id=1, source_target_pairs={{0,2},{2,4},{4,6},{6,8},{8,10},{10,12},{12,14},{14,16},{16,18},{18... | collective-permute-start | bytes 1179656 | tf_op jit(solution)/shard_map/ppermute | solution.py:110
  58.0 14.2 %collective-permute-start.7 = (f32[256,384]{1,0:T(8,128)S(1)}, f32[256,384]{1,0:T(8,128)S(1)}, u32[]{:S(2)}, u32[]{:S(2)}) collective-permute-start(f32[256,384]{1,0:T(8,128)S(1)} %get-tuple-element.50), channel_id=1, source_target_pairs={{2,0},{4,2},{6,4},{8,6},{10,8},{12,10},{14,12},{16,14},{18,16},{20... | collective-permute-start | bytes 1179656 | tf_op jit(solution)/shard_map/ppermute | solution.py:110
  68.7 7.1 %collective-permute-start.12 = (f32[256,384]{1,0:T(8,128)S(1)}, f32[256,384]{1,0:T(8,128)S(1)}, u32[]{:S(2)}, u32[]{:S(2)}) collective-permute-start(f32[256,384]{1,0:T(8,128)S(1)} %get-tuple-element.54), channel_id=1, source_target_pairs={{0,2},{2,4},{4,6},{6,8},{8,10},{10,12},{12,14},{14,16},{16,18},{18... | collective-permute-start | bytes 1179656 | tf_op jit(solution)/shard_map/ppermute | solution.py:110
  68.8 8.0 %collective-permute-start.13 = (f32[256,384]{1,0:T(8,128)S(1)}, f32[256,384]{1,0:T(8,128)S(1)}, u32[]{:S(2)}, u32[]{:S(2)}) collective-permute-start(f32[256,384]{1,0:T(8,128)S(1)} %get-tuple-element.56), channel_id=1, source_target_pairs={{2,0},{4,2},{6,4},{8,6},{10,8},{12,10},{14,12},{16,14},{18,16},{20... | collective-permute-start | bytes 1179656 | tf_op jit(solution)/shard_map/ppermute | solution.py:110
  72.9 20.0 %collective-permute-start.16 = (f32[256,512]{1,0:T(8,128)S(1)}, f32[256,512]{1,0:T(8,128)}, u32[]{:S(2)}, u32[]{:S(2)}) collective-permute-start(f32[256,512]{1,0:T(8,128)S(1)} %filter_step.11.refs_0_.refs_4_.refs_1_), channel_id=1, source_target_pairs={{0,1},{2,3},{4,5},{6,7},{8,9},{10,11},{12,13},{14,15},{16,17},{18,... | collective-permute-start | bytes 1572872 | tf_op jit(solution)/shard_map/ppermute | solution.py:451
  78.4 8.6 %collective-permute-start.14 = (f32[256,384]{1,0:T(8,128)}, f32[256,384]{1,0:T(8,128)S(1)}, u32[]{:S(2)}, u32[]{:S(2)}) collective-permute-start(f32[256,384]{1,0:T(8,128)} %get-tuple-element.57), channel_id=1, source_target_pairs={{0,2},{2,4},{4,6},{6,8},{8,10},{10,12},{12,14},{14,16},{16,18},{18... | collective-permute-start | bytes 1179656 | tf_op jit(solution)/shard_map/ppermute | solution.py:110
  79.9 10.3 %collective-permute-start.15 = (f32[256,384]{1,0:T(8,128)}, f32[256,384]{1,0:T(8,128)}, u32[]{:S(2)}, u32[]{:S(2)}) collective-permute-start(f32[256,384]{1,0:T(8,128)} %get-tuple-element.59), channel_id=1, source_target_pairs={{2,0},{4,2},{6,4},{8,6},{10,8},{12,10},{14,12},{16,14},{18,16},{20... | collective-permute-start | bytes 1179656 | tf_op jit(solution)/shard_map/ppermute | solution.py:110
  94.4 14.9 %collective-permute-start.19 = (f32[256,512]{1,0:T(8,128)S(1)}, f32[256,512]{1,0:T(8,128)S(1)}, u32[]{:S(2)}, u32[]{:S(2)}) collective-permute-start(f32[256,512]{1,0:T(8,128)S(1)} %filter_step.15.refs_1_.refs_5_.refs_2_), channel_id=1, source_target_pairs={{0,1},{2,3},{4,5},{6,7},{8,9},{10,11},{12,13},{14,15},{16,17},{18,... | collective-permute-start | bytes 1572872 | tf_op jit(solution)/shard_map/ppermute | solution.py:451
  96.0 5.7 %collective-permute-start.18 = (f32[320,128]{1,0:T(8,128)S(1)}, f32[320,128]{1,0:T(8,128)S(1)}, u32[]{:S(2)}, u32[]{:S(2)}) collective-permute-start(f32[320,128]{1,0:T(8,128)S(1)} %dynamic-slice_bitcast_fusion.3), channel_id=1, source_target_pairs={{0,4},{1,5},{2,6},{3,7},{4,0},{5,1},{6,2},{7,3},{8,12},{9,13},{10,... | collective-permute-start | bytes 491528 | tf_op jit(solution)/shard_map/ppermute | solution.py:445
  113.6 9.9 %collective-permute-start.23 = (f32[1024,128]{1,0:T(8,128)}, f32[1024,128]{1,0:T(8,128)S(1)}, u32[]{:S(2)}, u32[]{:S(2)}) collective-permute-start(f32[1024,128]{1,0:T(8,128)} %dynamic-slice_bitcast_fusion), channel_id=1, source_target_pairs={{1,3},{3,1},{5,7},{7,5},{9,11},{11,9},{13,15},{15,13},{17,19},{19,... | collective-permute-start | bytes 1572872 | tf_op jit(solution)/shard_map/ppermute | solution.py:445
  123.5 5.7 %collective-permute-start.24 = (f32[80,128]{1,0:T(8,128)S(1)}, f32[80,128]{1,0:T(8,128)S(1)}, u32[]{:S(2)}, u32[]{:S(2)}) collective-permute-start(f32[80,128]{1,0:T(8,128)S(1)} %fusion.1), channel_id=1, source_target_pairs={{0,1},{2,3},{4,5},{6,7},{8,9},{10,11},{12,13},{14,15},{16,17},{18,... | collective-permute-start | bytes 122888 | tf_op jit(solution)/shard_map/ppermute | solution.py:451
  124.9 9.2 %collective-permute-start.25 = (f32[512,128]{1,0:T(8,128)S(1)}, f32[512,128]{1,0:T(8,128)S(1)}, u32[]{:S(2)}, u32[]{:S(2)}) collective-permute-start(f32[512,128]{1,0:T(8,128)S(1)} %dynamic-slice_bitcast_fusion.2), channel_id=1, source_target_pairs={{1,5},{3,7},{5,1},{7,3},{9,13},{11,15},{13,9},{15,11},{17,21},{19,... | collective-permute-start | bytes 786440 | tf_op jit(solution)/shard_map/ppermute | solution.py:445
  134.1 9.5 %collective-permute-start.26 = (f32[80,128]{1,0:T(8,128)S(1)}, f32[80,128]{1,0:T(8,128)S(1)}, u32[]{:S(2)}, u32[]{:S(2)}) collective-permute-start(f32[80,128]{1,0:T(8,128)S(1)} %broadcast_select_fusion), channel_id=1, source_target_pairs={{0,8},{1,9},{2,10},{3,11},{4,12},{5,13},{6,14},{7,15},{8,0},{9,1},... | collective-permute-start | bytes 122888 | tf_op jit(solution)/shard_map/ppermute | solution.py:445
  134.5 12.6 %collective-permute-start.27 = (f32[80,128]{1,0:T(8,128)S(1)}, f32[80,128]{1,0:T(8,128)S(1)}, u32[]{:S(2)}, u32[]{:S(2)}) collective-permute-start(f32[80,128]{1,0:T(8,128)S(1)} %broadcast_select_fusion), channel_id=1, source_target_pairs={{0,16},{1,17},{2,18},{3,19},{4,20},{5,21},{6,22},{7,23},{8,24},{9,... | collective-permute-start | bytes 122888 | tf_op jit(solution)/shard_map/ppermute | solution.py:445
  136.2 10.8 %collective-permute-start.28 = (f32[80,128]{1,0:T(8,128)S(1)}, f32[80,128]{1,0:T(8,128)S(1)}, u32[]{:S(2)}, u32[]{:S(2)}) collective-permute-start(f32[80,128]{1,0:T(8,128)S(1)} %broadcast_select_fusion), channel_id=1, source_target_pairs={{0,24},{1,25},{2,26},{3,27},{4,28},{5,29},{6,30},{7,31},{8,16},{9,... | collective-permute-start | bytes 122888 | tf_op jit(solution)/shard_map/ppermute | solution.py:445
  137.8 9.4 %collective-permute-start.29 = (f32[128,128]{1,0:T(8,128)S(1)}, f32[128,128]{1,0:T(8,128)S(1)}, u32[]{:S(2)}, u32[]{:S(2)}) collective-permute-start(f32[128,128]{1,0:T(8,128)S(1)} %get-tuple-element.87), channel_id=1, source_target_pairs={{1,9},{3,11},{5,13},{7,15},{9,1},{11,3},{13,5},{15,7},{17,25},{19,... | collective-permute-start | bytes 196616 | tf_op jit(solution)/shard_map/ppermute | solution.py:445
  139.7 7.4 %collective-permute-start.30 = (f32[128,128]{1,0:T(8,128)S(1)}, f32[128,128]{1,0:T(8,128)S(1)}, u32[]{:S(2)}, u32[]{:S(2)}) collective-permute-start(f32[128,128]{1,0:T(8,128)S(1)} %get-tuple-element.86), channel_id=1, source_target_pairs={{1,17},{3,19},{5,21},{7,23},{9,25},{11,27},{13,29},{15,31},{17,1},... | collective-permute-start | bytes 196616 | tf_op jit(solution)/shard_map/ppermute | solution.py:445
  143.6 7.2 %collective-permute-start.31 = (f32[128,128]{1,0:T(8,128)S(1)}, f32[128,128]{1,0:T(8,128)S(1)}, u32[]{:S(2)}, u32[]{:S(2)}) collective-permute-start(f32[128,128]{1,0:T(8,128)S(1)} %get-tuple-element.85), channel_id=1, source_target_pairs={{1,25},{3,27},{5,29},{7,31},{9,17},{11,19},{13,21},{15,23},{17,9},... | collective-permute-start | bytes 196616 | tf_op jit(solution)/shard_map/ppermute | solution.py:445
  150.9 18.6 %collective-permute-start.32 = (f32[4,80,128]{2,1,0:T(8,128)S(1)}, f32[4,80,128]{2,1,0:T(8,128)S(1)}, u32[]{:S(2)}, u32[]{:S(2)}) collective-permute-start(f32[4,80,128]{2,1,0:T(8,128)S(1)} %pad_maximum_fusion.refs_0_), channel_id=1, source_target_pairs={{0,2},{1,3},{2,0},{3,1},{4,6},{5,7},{6,4},{7,5},{8,10},{9,11},{10,... | collective-permute-start | bytes 491528 | tf_op jit(solution)/shard_map/ppermute | solution.py:445
  154.4 15.8 %collective-permute-start.33 = (f32[4,80,128]{2,1,0:T(8,128)S(1)}, f32[4,80,128]{2,1,0:T(8,128)S(1)}, u32[]{:S(2)}, u32[]{:S(2)}) collective-permute-start(f32[4,80,128]{2,1,0:T(8,128)S(1)} %pad_maximum_fusion.refs_0_), channel_id=1, source_target_pairs={{0,4},{1,5},{2,6},{3,7},{4,0},{5,1},{6,2},{7,3},{8,12},{9,13},{10,... | collective-permute-start | bytes 491528 | tf_op jit(solution)/shard_map/ppermute | solution.py:445
  155.9 15.0 %collective-permute-start.34 = (f32[4,80,128]{2,1,0:T(8,128)S(1)}, f32[4,80,128]{2,1,0:T(8,128)S(1)}, u32[]{:S(2)}, u32[]{:S(2)}) collective-permute-start(f32[4,80,128]{2,1,0:T(8,128)S(1)} %pad_maximum_fusion.refs_0_), channel_id=1, source_target_pairs={{0,6},{1,7},{2,4},{3,5},{4,2},{5,3},{6,0},{7,1},{8,14},{9,15},{10,... | collective-permute-start | bytes 491528 | tf_op jit(solution)/shard_map/ppermute | solution.py:445
  (19 other events, 58.3 us)
Sparse Core Ops, SparseCore 0:
  171.7 23.9 all-gather.3

commit v2 on v1

--- a/solution.py
+++ b/solution.py
@@ -17,8 +17,9 @@
 NN = (((1,), (0,)), ((), ()))
 SCALARS = pl.BlockSpec(memory_space=pltpu.SMEM)
 WHOLE = pl.BlockSpec(memory_space=pltpu.VMEM)
-AFAR = pl.BlockSpec(memory_space=pltpu.HBM)
+AFAR = pl.BlockSpec(memory_space=pl.ANY)
 ROOMY = pltpu.CompilerParams(vmem_limit_bytes=28 * 2 ** 20)
+ALONE = pltpu.CompilerParams(vmem_limit_bytes=48 * 2 ** 20)
 
 
 def split(x):
@@ -120,6 +121,7 @@
     for step in range(STEPS):
         more = step < STEPS - 1
         for c in range(CHUNKS):
+            halos[c], current[c - 1] = lax.optimization_barrier((halos[c], current[c - 1]))
             following, *edges = filter_step(halos[c], current[c], band, previous[c], more)
             previous[c], current[c] = current[c], following
             if more:
@@ -324,18 +326,28 @@
     return [(part, target.at[i * rows:(i + 1) * rows, :columns]) for i, part in enumerate(parts)]
 
 
-def lower_blocks(flat, gram_ref):
+def lower_blocks(flat, gram_ref, first):
     blocks = gram_ref.shape[0] // NB
     for i in range(blocks):
         for j in range(blocks):
-            place = i * (i + 1) // 2 + j
+            place = (first + i) * (first + i + 1) // 2 + first + j
             block = flat[place * NB:(place + 1) * NB, :] if j <= i else jnp.zeros((NB, NB), jnp.float32)
             gram_ref[i * NB:(i + 1) * NB, j * NB:(j + 1) * NB] = block
 
 
-def first_half_kernel(where_ref, *refs):
-    pieces, mine, other = refs[:4], refs[4:4 + CHUNKS], refs[4 + CHUNKS:4 + 2 * CHUNKS]
-    top_ref, inverse_ref, flat, gram, field, total, low0, low1, done0, done1, sems = refs[4 + 2 * CHUNKS:]
+def inverted(low, first, second):
+    return -dot3(split(second), split(dot3(low, first, NN)), NN)
+
+
+def identity(size):
+    rows = lax.broadcasted_iota(jnp.int32, (size, size), 0)
+    lanes = lax.broadcasted_iota(jnp.int32, (size, size), 1)
+    return jnp.where(rows == lanes, 1.0, 0.0)
+
+
+def first_quarter_kernel(where_ref, *refs):
+    pieces, mine, other, top_ref, inverse_ref = refs[:4], refs[4], refs[5], refs[6], refs[7]
+    flat, gram, field, total, low0, low1, done0, done1, sems = refs[8:]
     place, near, far = where_ref[0], where_ref[1], where_ref[2]
     size, columns = top_ref.shape
     rows = pieces[0].shape[1]
@@ -346,91 +358,129 @@
 
     @pl.when(place == 0)
     def _():
-        fetch(pairs + stacked(mine, field, columns), sems)
+        fetch(pairs + stacked([mine], field, columns), sems)
 
     @pl.when(place != 0)
     def _():
-        fetch(pairs + stacked(other, field, columns), sems)
-
-    lower_blocks(flat, gram)
-    rows = lax.broadcasted_iota(jnp.int32, (size, size), 0)
-    lanes = lax.broadcasted_iota(jnp.int32, (size, size), 1)
-    field[:, columns:] = jnp.where(rows == lanes, 1.0, 0.0)
+        fetch(pairs + stacked([other], field, columns), sems)
+
+    lower_blocks(flat, gram, 0)
+    field[:, columns:] = identity(size)
     eliminate(gram, field, (low0, low1), (done0, done1), total, size // NB)
-    top_ref[...] = total[:, :columns]
-    inverse_ref[...] = total[:, columns:]
-
-
-def first_half(where, pieces, mine, other):
-    size, columns = sum(part.shape[0] for part in mine), mine[0].shape[1]
+    fetch([(total.at[:, :columns], top_ref), (total.at[:, columns:], inverse_ref)], sems)
+
+
+def second_quarter_kernel(where_ref, *refs):
+    pieces, mine, other, top_in, inverse_in, top_ref, inverse_ref = refs[:4], *refs[4:10]
+    flat, gram, corner, top, inverse, field, total, low0, low1, done0, done1, sems = refs[10:]
+    place, near, far = where_ref[0], where_ref[1], where_ref[2]
+    size, columns = mine.shape
+    rows = pieces[0].shape[1]
+    pairs = [
+        (piece.at[j], rows_of(flat, ((near ^ i) * 4 + (far ^ j)) * rows, rows))
+        for i, piece in enumerate(pieces) for j in range(4)
+    ] + [(top_in, top), (inverse_in, inverse)]
+
+    @pl.when(place == 0)
+    def _():
+        fetch(pairs + stacked([mine], field, columns), sems)
+
+    @pl.when(place != 0)
+    def _():
+        fetch(pairs + stacked([other], field, columns), sems)
+
+    blocks = size // NB
+    lower_blocks(flat, gram, blocks)
+    for i in range(blocks):
+        for j in range(blocks):
+            start = ((blocks + i) * (blocks + i + 1) // 2 + j) * NB
+            corner[i * NB:(i + 1) * NB, j * NB:(j + 1) * NB] = flat[start:start + NB, :]
+    first = split(inverse[...])
+    low = split(dot3(split(corner[...]), first, NT))
+    gram[...] = gram[...] - dot3(low, low, NT)
+    field[:, :columns] = field[:, :columns] - dot3(low, split(top[...]), NN)
+    field[:, columns:] = identity(size)
+    eliminate(gram, field, (low0, low1), (done0, done1), total, blocks)
+    corner[...] = inverted(low, first, total[:, columns:])
+    gram[...] = jnp.zeros_like(gram)
+    fetch([
+        (top, top_ref.at[:size]),
+        (total.at[:, :columns], top_ref.at[size:]),
+        (inverse, inverse_ref.at[:size, :size]),
+        (gram, inverse_ref.at[:size, size:]),
+        (corner, inverse_ref.at[size:, :size]),
+        (total.at[:, columns:], inverse_ref.at[size:, size:]),
+    ], sems)
+
+
+def quarter(kernel, where, pieces, mine, other, *before):
+    size, columns = mine.shape
     f32 = jnp.float32
     flat_rows = 4 * pieces[0].shape[0] * pieces[0].shape[1]
-    operands = (*pieces, *mine, *other)
-    shapes = ((size, columns), (size, size))
-    return pl.pallas_call(
-        first_half_kernel,
-        out_shape=tuple(jax.ShapeDtypeStruct(shape, f32) for shape in shapes),
+    operands = (*pieces, mine, other, *before)
+    results = 2 * size if before else size
+    square, wide = pltpu.VMEM((size, size), f32), pltpu.VMEM((size, columns + size), f32)
+    earlier = [square, pltpu.VMEM((size, columns), f32), square] if before else []
+    return pl.pallas_call(
+        kernel,
+        out_shape=tuple(jax.ShapeDtypeStruct((results, n), f32) for n in (columns, results)),
         in_specs=[SCALARS] + [AFAR] * len(operands),
-        out_specs=(WHOLE, WHOLE),
-        scratch_shapes=[
-            pltpu.VMEM((flat_rows, NB), f32),
-            pltpu.VMEM((size, size), f32),
-            pltpu.VMEM((size, columns + size), f32),
-            pltpu.VMEM((size, columns + size), f32),
-        ] + elimination_scratch(size, columns + size) + [pltpu.SemaphoreType.DMA((16 + CHUNKS,))],
-        compiler_params=ROOMY,
-        cost_estimate=pl.CostEstimate(flops=2 * 10 ** 10, bytes_accessed=10 ** 7, transcendentals=0),
-        name="first_half",
+        out_specs=(AFAR, AFAR),
+        scratch_shapes=[pltpu.VMEM((flat_rows, NB), f32), square] + earlier + [wide, wide]
+        + elimination_scratch(size, columns + size) + [pltpu.SemaphoreType.DMA((19,))],
+        compiler_params=ALONE,
+        cost_estimate=pl.CostEstimate(flops=10 ** 10, bytes_accessed=10 ** 7, transcendentals=0),
+        name="second_quarter" if before else "first_quarter",
     )(where, *operands)
 
 
 def second_half_kernel(scale, where_ref, *refs):
-    rest, mine = refs[0], refs[1:1 + CHUNKS]
-    top_ref, inverse_ref, out_ref = refs[1 + CHUNKS:4 + CHUNKS]
-    flat, corner, gram, field, total, low0, low1, done0, done1, sems = refs[4 + CHUNKS:]
-    place = where_ref[0]
-    size, columns = top_ref.shape
+    pieces, corners, mine = refs[0], refs[1:5], refs[5:5 + CHUNKS]
+    top_in, inverse_in, out_ref = refs[5 + CHUNKS:8 + CHUNKS]
+    flat, corner, gram, top, inverse, field, total, low0, low1, done0, done1, sems = refs[8 + CHUNKS:]
+    place, near, far = where_ref[0], where_ref[1], where_ref[2]
+    size, columns = top.shape
     blocks = size // NB
-    rows = rest.shape[2] - NB
+    rows = pieces.shape[2]
 
     @pl.when(place == 0)
     def _():
-        out_ref[...] = top_ref[...] * scale
+        fetch([(top_in, top)], sems)
+        out_ref[...] = top[...] * scale
 
     @pl.when(place != 0)
     def _():
-        pairs = stacked(mine, field, columns)
+        pairs = stacked(mine, field, columns) + [(top_in, top), (inverse_in, inverse)]
         for i in range(4):
             for j in range(4):
-                pairs.append((rest.at[i, j, :rows], rows_of(flat, (i * 4 + j) * rows, rows)))
-                pairs.append((rest.at[i, j, rows:], corner.at[i * NB:(i + 1) * NB, j * NB:(j + 1) * NB]))
+                pairs.append((pieces.at[i, j], rows_of(flat, (i * 4 + (far ^ j)) * rows, rows)))
+                lanes = pl.ds(pl.multiple_of((far ^ j) * NB, NB), NB)
+                target = corner.at[pl.ds(pl.multiple_of((near ^ i) * NB, NB), NB), lanes]
+                pairs.append((corners[i].at[j], target))
         fetch(pairs, sems)
-        lower_blocks(flat, gram)
-        low = split(dot3(split(corner[...]), split(inverse_ref[...]), NT))
+        lower_blocks(flat, gram, 0)
+        low = split(dot3(split(corner[...]), split(inverse[...]), NT))
         gram[...] = gram[...] - dot3(low, low, NT)
-        field[...] = field[...] - dot3(low, split(top_ref[...]), NN)
+        field[...] = field[...] - dot3(low, split(top[...]), NN)
         eliminate(gram, field, (low0, low1), (done0, done1), total, blocks)
         out_ref[...] = total[...] * scale
 
 
-def second_half(where, rest, mine, top, inverse, scale):
+def second_half(where, pieces, corners, mine, top, inverse, scale):
     size, columns = top.shape
     f32 = jnp.float32
+    square, wide = pltpu.VMEM((size, size), f32), pltpu.VMEM((size, columns), f32)
     return pl.pallas_call(
         functools.partial(second_half_kernel, scale),
         out_shape=jax.ShapeDtypeStruct((size, columns), f32),
-        in_specs=[SCALARS] + [AFAR] * (1 + CHUNKS) + [WHOLE] * 2,
+        in_specs=[SCALARS] + [AFAR] * (7 + CHUNKS),
         out_specs=WHOLE,
         scratch_shapes=[
-            pltpu.VMEM((16 * (rest.shape[2] - NB), NB), f32),
-            pltpu.VMEM((size, size), f32),
-            pltpu.VMEM((size, size), f32),
-            pltpu.VMEM((size, columns), f32),
-            pltpu.VMEM((size, columns), f32),
-        ] + elimination_scratch(size, columns) + [pltpu.SemaphoreType.DMA((32 + CHUNKS,))],
-        compiler_params=ROOMY,
+            pltpu.VMEM((16 * pieces.shape[2], NB), f32), square, square, wide, square, wide, wide,
+        ] + elimination_scratch(size, columns) + [pltpu.SemaphoreType.DMA((34 + CHUNKS,))],
+        compiler_params=ALONE,
         name="second_half",
-    )(where, rest, *mine, top, inverse)
+    )(where, pieces, *corners, *mine, top, inverse)
 
 
 NEAR, FAR = 1, 4
@@ -475,29 +525,31 @@
     near, far = rank % 4, rank // 4
     where = jnp.stack([place, near, far]).astype(jnp.int32)
     near_groups = [list(range(4 * g, 4 * g + 4)) for g in range(4)]
-    far_groups = [list(range(g, 16, 4)) for g in range(4)]
     below = [send_up(part, 0) for part in current]
     own, below[0] = together((current, below[0]))
     half = swap_half(own_gram(own), near % 2, 1)
     fourth = swap_half(half, near // 2, 2)
-    fourth, *below = together((fourth, *below))
-    corner = cross_gram(current, below)
-    corner = swap_half(corner, near % 2, 1, (1,))
     mine = reduce_group(fourth, far, FAR)
-    mine, corner = together((mine, corner))
+    mine, *below = together((mine, *below))
     first = jnp.where(place == 0, mine, send_up(mine, 0))
+    corner = swap_half(cross_gram(current, below), near % 2, 1, (1,))
+    first, corner = together((first, corner))
+    both = jnp.concatenate([first, mine], axis=0)
+    both = jnp.stack([both] + [send(both, i * FAR) for i in range(1, 4)])
     corner = swap_half(corner, near // 2, 2, (1,))
-    first, corner = together((first, corner))
-    first = jnp.stack([first] + [send(first, i * FAR) for i in range(1, 4)])
+    both, corner = together((both, corner))
+    rows = mine.shape[0]
+    first, second = both[:, :rows], both[:, rows:]
+    second = lax.all_gather(second, "rows", axis_index_groups=near_groups)
+    pieces = [first] + [send(first, i * NEAR) for i in range(1, 4)]
     corner = reduce_group(corner, far, FAR, (1,))
-    first, corner = together((first, corner))
-    rest = jnp.concatenate([mine, corner], axis=0)
-    rest = lax.all_gather(rest, "rows", axis_index_groups=far_groups)
-    pieces = [first] + [send(first, i * NEAR) for i in range(1, 4)]
-    pieces, rest = together((pieces, rest))
-    rest = lax.all_gather(rest, "rows", axis_index_groups=near_groups)
-    top, inverse = first_half(where, pieces, current, below)
-    return second_half(where, rest, current, top, inverse, scale)
+    pieces, corner = together((pieces, corner))
+    top, inverse = quarter(first_quarter_kernel, where, pieces, current[0], below[0])
+    corner = jnp.stack([corner] + [send(corner, i * FAR, (1,)) for i in range(1, 4)])
+    top, inverse, corner = together((top, inverse, corner))
+    top, inverse = quarter(second_quarter_kernel, where, pieces, current[1], below[1], top, inverse)
+    corners = [corner] + [send(corner, i * NEAR, (1,)) for i in range(1, 4)]
+    return second_half(where, second, corners, current, top, inverse, scale)
 
 
 def orthonormalize(current, scale):

time: 231 us -> 227 us (0.983)
  starting transfers between devices: 42.2 us -> 63 us
  between operations: 13.9 us -> 0.74 us
  local copies, waits for them, and re-layouts: 13.8 us -> 8.34 us
  blocking collectives: 13.4 us -> 8.01 us
    ppermute x16 -> x22, starting transfers between devices: 29.3 us -> 48.8 us  [send(): return lax.ppermute(x, ('rows', 'vecs'), pairs)]
    ppermute x16, waiting for transfers between devices: 61.5 us -> 54.7 us  [exchange_edges(): return (lax.ppermute(last, 'rows', up), lax.ppermute(first, 'rows', down))]
    unnamed x30 -> x13, local copies, waits for them, and re-layouts: 8.98 us -> 3.49 us
    all_gather x1, blocking collectives: 13.4 us -> 8.01 us  [orthonormalize_planes(): second = lax.all_gather(second, 'rows', axis_index_groups=near_groups)]
    ppermute x3, waiting for transfers between devices: 7.59 us -> 11.6 us  [send_up(): return lax.ppermute(x, ('rows', 'vecs'), pairs)]
    pallas_call x1 -> x2, Pallas kernels: 21.4 us -> 24.2 us  [quarter(): pl.pallas_call(kernel, out_shape=tuple((jax.ShapeDtypeStruct((results, n)...]
    ppermute x16 -> x22, waiting for transfers between devices: 17.5 us -> 19.1 us  [send(): return lax.ppermute(x, ('rows', 'vecs'), pairs)]
  transfers between devices with their start and end apart: 36 -> 41, of which waited for: 22 -> 20; matrix products, arithmetic and copies ran while one was open for 1% -> 1% of each run, Pallas kernels for 13% -> 14%
where the time goes in v2:
time: 227 us; the launch traced here: 226 us
  waiting for transfers between devices  85.4 us (38%)
  starting transfers between devices  63 us (28%)
  Pallas kernels  60.4 us (27%)
  local copies, waits for them, and re-layouts  8.34 us (4%)
  blocking collectives  8.01 us (4%)
    ppermute x16, waiting for transfers between devices, exchange_edges(): return (lax.ppermute(last, 'rows', up), lax.ppermute(first, 'rows', down))  54.7 us
    ppermute x22, starting transfers between devices, send(): return lax.ppermute(x, ('rows', 'vecs'), pairs)  48.8 us
    pallas_call x2, Pallas kernels, quarter(): pl.pallas_call(kernel, out_shape=tuple((jax.ShapeDtypeStruct((results, n)...  24.2 us
    pallas_call x1, Pallas kernels, second_half(): pl.pallas_call(functools.partial(second_half_kernel, scale), out_shape=ja...  23.9 us
    ppermute x22, waiting for transfers between devices, send(): return lax.ppermute(x, ('rows', 'vecs'), pairs)  19.1 us
    ppermute x3, waiting for transfers between devices, send_up(): return lax.ppermute(x, ('rows', 'vecs'), pairs)  11.6 us
    ppermute x16, starting transfers between devices, exchange_edges(): return (lax.ppermute(last, 'rows', up), lax.ppermute(first, 'rows', down))  10.4 us
    all_gather x1, blocking collectives, orthonormalize_planes(): second = lax.all_gather(second, 'rows', axis_index_groups=near_groups)  8.01 us
  transfers between devices with their start and end apart: 41, of which 20 were waited for; matrix products, arithmetic and copies ran while one was open for 1% of the time, Pallas kernels for 14%

profile of v2, /device:TPU:5, one launch (start us, length us, event | category | flops | bytes accessed | tf_op | source)
XLA Modules:
  0.0 226.3 jit_solution(4220875883723332344)
XLA Ops:
  0.0 2.6 %fusion.5 = (f32[256,384]{1,0:T(8,128)}, f32[256,384]{1,0:T(8,128)}, f32[256,384]{1,0:T(8,128)}, f32[256,384]{1,0:T(8,128)}) fusion(f32[512,512]{1,0:T(8,128)} %param.5), kind=kLoop, calls=%fused_computation.31 | loop fusion | bytes 3145728 | tf_op jit(solution)/shard_map/slice | solution.py:119
  10.0 7.8 %collective-permute-done.2.refs_0_ = f32[256,384]{1,0:T(8,128)S(1)} collective-permute-done((f32[256,384]{1,0:T(8,128)}, f32[256,384]{1,0:T(8,128)S(1)}, u32[]{:S(2)}, u32[]{:S(2)}) %collective-permute-start.2) | collective-permute-done | bytes 393248 | tf_op jit(solution)/shard_map/ppermute | solution.py:111
  17.8 2.5 %collective-permute-done.3.refs_2_ = f32[256,384]{1,0:T(8,128)} collective-permute-done((f32[256,384]{1,0:T(8,128)}, f32[256,384]{1,0:T(8,128)}, u32[]{:S(2)}, u32[]{:S(2)}) %collective-permute-start.3) | collective-permute-done | bytes 393248 | tf_op jit(solution)/shard_map/ppermute | solution.py:111
  22.6 6.0 %collective-permute-done.1.refs_2_ = f32[256,384]{1,0:T(8,128)S(1)} collective-permute-done((f32[256,384]{1,0:T(8,128)}, f32[256,384]{1,0:T(8,128)S(1)}, u32[]{:S(2)}, u32[]{:S(2)}) %collective-permute-start.1) | collective-permute-done | bytes 393248 | tf_op jit(solution)/shard_map/ppermute | solution.py:111
  30.0 11.3 %collective-permute-done.7.refs_2_ = f32[256,384]{1,0:T(8,128)S(1)} collective-permute-done((f32[256,384]{1,0:T(8,128)S(1)}, f32[256,384]{1,0:T(8,128)S(1)}, u32[]{:S(2)}, u32[]{:S(2)}) %collective-permute-start.7) | collective-permute-done | bytes 393248 | tf_op jit(solution)/shard_map/ppermute | solution.py:111
  42.6 2.9 %collective-permute-done.5.refs_2_ = f32[256,384]{1,0:T(8,128)S(1)} collective-permute-done((f32[256,384]{1,0:T(8,128)S(1)}, f32[256,384]{1,0:T(8,128)S(1)}, u32[]{:S(2)}, u32[]{:S(2)}) %collective-permute-start.5) | collective-permute-done | bytes 393248 | tf_op jit(solution)/shard_map/ppermute | solution.py:111
  46.8 8.4 %collective-permute-done.10.refs_0_ = f32[256,384]{1,0:T(8,128)S(1)} collective-permute-done((f32[256,384]{1,0:T(8,128)S(1)}, f32[256,384]{1,0:T(8,128)S(1)}, u32[]{:S(2)}, u32[]{:S(2)}) %collective-permute-start.10) | collective-permute-done | bytes 393248 | tf_op jit(solution)/shard_map/ppermute | solution.py:111
  56.0 2.5 %collective-permute-start.14 = (f32[256,384]{1,0:T(8,128)S(1)}, f32[256,384]{1,0:T(8,128)S(1)}, u32[]{:S(2)}, u32[]{:S(2)}) collective-permute-start(f32[256,384]{1,0:T(8,128)S(1)} %get-tuple-element.101), channel_id=1, source_target_pairs={{0,2},{2,4},{4,6},{6,8},{8,10},{10,12},{12,14},{14,16},{16,18},{18... | collective-permute-start | bytes 1179656 | tf_op jit(solution)/shard_map/ppermute | solution.py:111
  59.5 2.9 %collective-permute-done.9.refs_2_ = f32[256,384]{1,0:T(8,128)S(1)} collective-permute-done((f32[256,384]{1,0:T(8,128)S(1)}, f32[256,384]{1,0:T(8,128)S(1)}, u32[]{:S(2)}, u32[]{:S(2)}) %collective-permute-start.9) | collective-permute-done | bytes 393248 | tf_op jit(solution)/shard_map/ppermute | solution.py:111
  63.7 8.4 %collective-permute-done.14.refs_0_ = f32[256,384]{1,0:T(8,128)S(1)} collective-permute-done((f32[256,384]{1,0:T(8,128)S(1)}, f32[256,384]{1,0:T(8,128)S(1)}, u32[]{:S(2)}, u32[]{:S(2)}) %collective-permute-start.14) | collective-permute-done | bytes 393248 | tf_op jit(solution)/shard_map/ppermute | solution.py:111
  72.8 3.5 %collective-permute-done.12.refs_0_ = f32[256,384]{1,0:T(8,128)S(1)} collective-permute-done((f32[256,384]{1,0:T(8,128)S(1)}, f32[256,384]{1,0:T(8,128)S(1)}, u32[]{:S(2)}, u32[]{:S(2)}) %collective-permute-start.12) | collective-permute-done | bytes 393248 | tf_op jit(solution)/shard_map/ppermute | solution.py:111
  81.9 6.0 %collective-permute-done.16.refs_2_.refs_5_ = f32[256,512]{1,0:T(8,128)} collective-permute-done((f32[256,512]{1,0:T(8,128)S(1)}, f32[256,512]{1,0:T(8,128)}, u32[]{:S(2)}, u32[]{:S(2)}) %collective-permute-start.16) | collective-permute-done | bytes 524320 | tf_op jit(solution)/shard_map/ppermute | solution.py:501
  90.9 3.4 %collective-permute-start.18 = (f32[320,128]{1,0:T(8,128)S(1)}, f32[320,128]{1,0:T(8,128)S(1)}, u32[]{:S(2)}, u32[]{:S(2)}) collective-permute-start(f32[320,128]{1,0:T(8,128)S(1)} %dynamic-slice_bitcast_fusion.3), channel_id=1, source_target_pairs={{0,4},{1,5},{2,6},{3,7},{4,0},{5,1},{6,2},{7,3},{8,12},{9,13},{10,... | collective-permute-start | bytes 491528 | tf_op jit(solution)/shard_map/ppermute | solution.py:495
  95.7 3.0 %collective-permute-done.18 = f32[320,128]{1,0:T(8,128)S(1)} collective-permute-done((f32[320,128]{1,0:T(8,128)S(1)}, f32[320,128]{1,0:T(8,128)S(1)}, u32[]{:S(2)}, u32[]{:S(2)}) %collective-permute-start.18) | collective-permute-done | bytes 163872 | tf_op jit(solution)/shard_map/ppermute | solution.py:495
  109.1 3.2 %cross_gram.1 = f32[2048,128]{1,0:T(8,128)S(1)} custom-call(f32[256,512]{1,0:T(8,128)S(1)} %filter_step.14.refs_0_.refs_4_.refs_5_, f32[256,512]{1,0:T(8,128)S(1)} %filter_step.15.refs_1_.refs_4_.refs_6_, f32[256,512]{1,0:T(8,128)} %collective-permute-done.16.refs_2_.refs_5_, f32[256,512]{1,0:T(8,128)S(1)} %collective-permute-done.22.refs_3_.refs_5_), custom_call_target="tpu_custom_call" | custom-call | tf_op jit(solution)/shard_map/cross_gram/pallas_call | solution.py:302
  113.1 3.4 %collective-permute-start.24 = (f32[1024,128]{1,0:T(8,128)}, f32[1024,128]{1,0:T(8,128)S(1)}, u32[]{:S(2)}, u32[]{:S(2)}) collective-permute-start(f32[1024,128]{1,0:T(8,128)} %dynamic-slice_bitcast_fusion), channel_id=1, source_target_pairs={{1,3},{3,1},{5,7},{7,5},{9,11},{11,9},{13,15},{15,13},{17,19},{19,... | collective-permute-start | bytes 1572872 | tf_op jit(solution)/shard_map/ppermute | solution.py:495
  117.8 3.4 %collective-permute-done.23 = f32[80,128]{1,0:T(8,128)S(1)} collective-permute-done((f32[80,128]{1,0:T(8,128)S(1)}, f32[80,128]{1,0:T(8,128)S(1)}, u32[]{:S(2)}, u32[]{:S(2)}) %collective-permute-start.23) | collective-permute-done | bytes 40992 | tf_op jit(solution)/shard_map/ppermute | solution.py:501
  127.4 2.6 %collective-permute-done.26 = f32[160,128]{1,0:T(8,128)S(1)} collective-permute-done((f32[160,128]{1,0:T(8,128)S(1)}, f32[160,128]{1,0:T(8,128)S(1)}, u32[]{:S(2)}, u32[]{:S(2)}) %collective-permute-start.26) | collective-permute-done | bytes 81952 | tf_op jit(solution)/shard_map/ppermute | solution.py:495
  130.0 2.7 %collective-permute-done.27 = f32[160,128]{1,0:T(8,128)S(1)} collective-permute-done((f32[160,128]{1,0:T(8,128)S(1)}, f32[160,128]{1,0:T(8,128)S(1)}, u32[]{:S(2)}, u32[]{:S(2)}) %collective-permute-start.27) | collective-permute-done | bytes 81952 | tf_op jit(solution)/shard_map/ppermute | solution.py:495
  132.9 2.6 %collective-permute-start.29 = (f32[4,80,128]{2,1,0:T(8,128)S(1)}, f32[4,80,128]{2,1,0:T(8,128)S(1)}, u32[]{:S(2)}, u32[]{:S(2)}) collective-permute-start(f32[4,80,128]{2,1,0:T(8,128)S(1)} %get-tuple-element.121.refs_0_), channel_id=1, source_target_pairs={{0,2},{1,3},{2,0},{3,1},{4,6},{5,7},{6,4},{7,5},{8,10},{9,11},{10,... | collective-permute-start | bytes 491528 | tf_op jit(solution)/shard_map/ppermute | solution.py:495
  136.9 2.9 %collective-permute-start.32 = (f32[128,128]{1,0:T(8,128)S(1)}, f32[128,128]{1,0:T(8,128)S(1)}, u32[]{:S(2)}, u32[]{:S(2)}) collective-permute-start(f32[128,128]{1,0:T(8,128)S(1)} %get-tuple-element.143), channel_id=1, source_target_pairs={{1,9},{3,11},{5,13},{7,15},{9,1},{11,3},{13,5},{15,7},{17,25},{19,... | collective-permute-start | bytes 196616 | tf_op jit(solution)/shard_map/ppermute | solution.py:495
  139.8 3.2 %collective-permute-start.33 = (f32[128,128]{1,0:T(8,128)S(1)}, f32[128,128]{1,0:T(8,128)S(1)}, u32[]{:S(2)}, u32[]{:S(2)}) collective-permute-start(f32[128,128]{1,0:T(8,128)S(1)} %get-tuple-element.142), channel_id=1, source_target_pairs={{1,17},{3,19},{5,21},{7,23},{9,25},{11,27},{13,29},{15,31},{17,1},... | collective-permute-start | bytes 196616 | tf_op jit(solution)/shard_map/ppermute | solution.py:495
  143.1 3.1 %collective-permute-start.34 = (f32[128,128]{1,0:T(8,128)S(1)}, f32[128,128]{1,0:T(8,128)S(1)}, u32[]{:S(2)}, u32[]{:S(2)}) collective-permute-start(f32[128,128]{1,0:T(8,128)S(1)} %get-tuple-element.141), channel_id=1, source_target_pairs={{1,25},{3,27},{5,29},{7,31},{9,17},{11,19},{13,21},{15,23},{17,9},... | collective-permute-start | bytes 196616 | tf_op jit(solution)/shard_map/ppermute | solution.py:495
  146.2 8.0 %all-gather = f32[16,80,128]{2,1,0:T(8,128)S(1)} all-gather(f32[4,80,128]{2,1,0:T(8,128)S(1)} %get-tuple-element.140), channel_id=2, replica_groups={{0,2,4,6},{8,10,12,14},{16,18,20,22},{24,26,28,30},{1,3,5,7},{9,11,13,1..., dimensions={0}, use_global_device_ids=true | all-gather | bytes 819200 | tf_op jit(solution)/shard_map/all_gather | solution.py:543
  155.5 4.7 %collective-permute-done.31.refs_3_ = f32[4,80,128]{2,1,0:T(8,128)S(1)} collective-permute-done((f32[4,80,128]{2,1,0:T(8,128)S(1)}, f32[4,80,128]{2,1,0:T(8,128)S(1)}, u32[]{:S(2)}, u32[]{:S(2)}) %collective-permute-start.31) | collective-permute-done | bytes 163872 | tf_op jit(solution)/shard_map/ppermute | solution.py:495
  162.2 4.1 %collective-permute-start.36 = (f32[128,128]{1,0:T(8,128)S(1)}, f32[128,128]{1,0:T(8,128)S(1)}, u32[]{:S(2)}, u32[]{:S(2)}) collective-permute-start(f32[128,128]{1,0:T(8,128)S(1)} %fusion), channel_id=1, source_target_pairs={{1,17},{3,19},{5,21},{7,23},{9,25},{11,27},{13,29},{15,31},{17,1},... | collective-permute-start | bytes 196616 | tf_op jit(solution)/shard_map/ppermute | solution.py:495
  166.3 3.1 %collective-permute-start.37 = (f32[128,128]{1,0:T(8,128)S(1)}, f32[128,128]{1,0:T(8,128)S(1)}, u32[]{:S(2)}, u32[]{:S(2)}) collective-permute-start(f32[128,128]{1,0:T(8,128)S(1)} %fusion), channel_id=1, source_target_pairs={{1,25},{3,27},{5,29},{7,31},{9,17},{11,19},{13,21},{15,23},{17,9},... | collective-permute-start | bytes 196616 | tf_op jit(solution)/shard_map/ppermute | solution.py:495
  169.5 11.8 %first_quarter.1 = (f32[256,512]{1,0:T(8,128)S(1)}, f32[256,256]{1,0:T(8,128)S(1)}) custom-call(s32[3]{0:T(128)S(1)} %pad_add_fusion.where_ref, f32[4,80,128]{2,1,0:T(8,128)S(1)} %get-tuple-element.121.refs_0_, f32[4,80,128]{2,1,0:T(8,128)S(1)} %collective-permute-done.29.refs_1_, f32[4,80,128]{2,1,0:T(8,128)S(1)} %collective-permute-done.30.refs_2_, ...), custom_call_target="tpu_custom_call" | custom-call | flops 10000000000 | bytes 10000000 | tf_op jit(solution)/shard_map/first_quarter/pallas_call | solution.py:424
  181.3 3.0 %collective-permute-start.38 = (f32[4,128,128]{2,1,0:T(8,128)S(1)}, f32[4,128,128]{2,1,0:T(8,128)S(1)}, u32[]{:S(2)}, u32[]{:S(2)}) collective-permute-start(f32[4,128,128]{2,1,0:T(8,128)S(1)} %pad_maximum_fusion.1.refs_1_), channel_id=1, source_target_pairs={{1,3},{3,1},{5,7},{7,5},{9,11},{11,9},{13,15},{15,13},{17,19},{19,... | collective-permute-start | bytes 786440 | tf_op jit(solution)/shard_map/ppermute | solution.py:495
  184.3 3.1 %collective-permute-start.39 = (f32[4,128,128]{2,1,0:T(8,128)S(1)}, f32[4,128,128]{2,1,0:T(8,128)S(1)}, u32[]{:S(2)}, u32[]{:S(2)}) collective-permute-start(f32[4,128,128]{2,1,0:T(8,128)S(1)} %pad_maximum_fusion.1.refs_1_), channel_id=1, source_target_pairs={{1,5},{3,7},{5,1},{7,3},{9,13},{11,15},{13,9},{15,11},{17,21},{19,... | collective-permute-start | bytes 786440 | tf_op jit(solution)/shard_map/ppermute | solution.py:495
  189.7 12.4 %second_quarter.1 = (f32[512,512]{1,0:T(8,128)S(1)}, f32[512,512]{1,0:T(8,128)S(1)}) custom-call(s32[3]{0:T(128)S(1)} %pad_add_fusion.where_ref, f32[4,80,128]{2,1,0:T(8,128)S(1)} %get-tuple-element.121.refs_0_, f32[4,80,128]{2,1,0:T(8,128)S(1)} %collective-permute-done.29.refs_1_, f32[4,80,128]{2,1,0:T(8,128)S(1)} %collective-permute-done.30.refs_2_, ...), custom_call_target="tpu_custom_call" | custom-call | flops 10000000000 | bytes 10000000 | tf_op jit(solution)/shard_map/second_quarter/pallas_call | solution.py:424
  202.2 23.9 %second_half.1 = f32[512,512]{1,0:T(8,128)} custom-call(s32[3]{0:T(128)S(1)} %pad_add_fusion.where_ref, f32[4,4,80,128]{3,2,1,0:T(8,128)S(1)} %bitcast.56, f32[4,128,128]{2,1,0:T(8,128)S(1)} %pad_maximum_fusion.1.refs_1_, f32[4,128,128]{2,1,0:T(8,128)S(1)} %collective-permute-done.38.refs_2_, f32[4,128,128]{2,1,0:T(8,128)S(1)} %collective-permute-done.39.refs_3_, ...), custom_call_target="tpu_custom_call" | custom-call | tf_op jit(solution)/shard_map/second_half/pallas_call | solution.py:473
  (100 shorter events, 52.9 us)
Async XLA Ops:
  2.6 15.2 %collective-permute-start.2 = (f32[256,384]{1,0:T(8,128)}, f32[256,384]{1,0:T(8,128)S(1)}, u32[]{:S(2)}, u32[]{:S(2)}) collective-permute-start(f32[256,384]{1,0:T(8,128)} %get-tuple-element.136), channel_id=1, source_target_pairs={{0,2},{2,4},{4,6},{6,8},{8,10},{10,12},{12,14},{14,16},{16,18},{18... | collective-permute-start | bytes 1179656 | tf_op jit(solution)/shard_map/ppermute | solution.py:111
  4.4 15.9 %collective-permute-start.3 = (f32[256,384]{1,0:T(8,128)}, f32[256,384]{1,0:T(8,128)}, u32[]{:S(2)}, u32[]{:S(2)}) collective-permute-start(f32[256,384]{1,0:T(8,128)} %get-tuple-element.135), channel_id=1, source_target_pairs={{2,0},{4,2},{6,4},{8,6},{10,8},{12,10},{14,12},{16,14},{18,16},{20... | collective-permute-start | bytes 1179656 | tf_op jit(solution)/shard_map/ppermute | solution.py:111
  4.4 18.2 %collective-permute-start = (f32[256,384]{1,0:T(8,128)}, f32[256,384]{1,0:T(8,128)S(1)}, u32[]{:S(2)}, u32[]{:S(2)}) collective-permute-start(f32[256,384]{1,0:T(8,128)} %get-tuple-element.138), channel_id=1, source_target_pairs={{0,2},{2,4},{4,6},{6,8},{8,10},{10,12},{12,14},{14,16},{16,18},{18... | collective-permute-start | bytes 1179656 | tf_op jit(solution)/shard_map/ppermute | solution.py:111
  6.1 22.5 %collective-permute-start.1 = (f32[256,384]{1,0:T(8,128)}, f32[256,384]{1,0:T(8,128)S(1)}, u32[]{:S(2)}, u32[]{:S(2)}) collective-permute-start(f32[256,384]{1,0:T(8,128)} %get-tuple-element.137), channel_id=1, source_target_pairs={{2,0},{4,2},{6,4},{8,6},{10,8},{12,10},{14,12},{16,14},{18,16},{20... | collective-permute-start | bytes 1179656 | tf_op jit(solution)/shard_map/ppermute | solution.py:111
  22.1 7.9 %collective-permute-start.6 = (f32[256,384]{1,0:T(8,128)S(1)}, f32[256,384]{1,0:T(8,128)S(1)}, u32[]{:S(2)}, u32[]{:S(2)}) collective-permute-start(f32[256,384]{1,0:T(8,128)S(1)} %get-tuple-element.77), channel_id=1, source_target_pairs={{0,2},{2,4},{4,6},{6,8},{8,10},{10,12},{12,14},{14,16},{16,18},{18... | collective-permute-start | bytes 1179656 | tf_op jit(solution)/shard_map/ppermute | solution.py:111
  22.1 19.2 %collective-permute-start.7 = (f32[256,384]{1,0:T(8,128)S(1)}, f32[256,384]{1,0:T(8,128)S(1)}, u32[]{:S(2)}, u32[]{:S(2)}) collective-permute-start(f32[256,384]{1,0:T(8,128)S(1)} %get-tuple-element.78), channel_id=1, source_target_pairs={{2,0},{4,2},{6,4},{8,6},{10,8},{12,10},{14,12},{16,14},{18,16},{20... | collective-permute-start | bytes 1179656 | tf_op jit(solution)/shard_map/ppermute | solution.py:111
  29.4 13.2 %collective-permute-start.4 = (f32[256,384]{1,0:T(8,128)S(1)}, f32[256,384]{1,0:T(8,128)S(1)}, u32[]{:S(2)}, u32[]{:S(2)}) collective-permute-start(f32[256,384]{1,0:T(8,128)S(1)} %get-tuple-element.75), channel_id=1, source_target_pairs={{0,2},{2,4},{4,6},{6,8},{8,10},{10,12},{12,14},{14,16},{16,18},{18... | collective-permute-start | bytes 1179656 | tf_op jit(solution)/shard_map/ppermute | solution.py:111
  29.5 16.0 %collective-permute-start.5 = (f32[256,384]{1,0:T(8,128)S(1)}, f32[256,384]{1,0:T(8,128)S(1)}, u32[]{:S(2)}, u32[]{:S(2)}) collective-permute-start(f32[256,384]{1,0:T(8,128)S(1)} %get-tuple-element.76), channel_id=1, source_target_pairs={{2,0},{4,2},{6,4},{8,6},{10,8},{12,10},{14,12},{16,14},{18,16},{20... | collective-permute-start | bytes 1179656 | tf_op jit(solution)/shard_map/ppermute | solution.py:111
  42.0 13.2 %collective-permute-start.10 = (f32[256,384]{1,0:T(8,128)S(1)}, f32[256,384]{1,0:T(8,128)S(1)}, u32[]{:S(2)}, u32[]{:S(2)}) collective-permute-start(f32[256,384]{1,0:T(8,128)S(1)} %get-tuple-element.89), channel_id=1, source_target_pairs={{0,2},{2,4},{4,6},{6,8},{8,10},{10,12},{12,14},{14,16},{16,18},{18... | collective-permute-start | bytes 1179656 | tf_op jit(solution)/shard_map/ppermute | solution.py:111
  42.1 13.1 %collective-permute-start.11 = (f32[256,384]{1,0:T(8,128)S(1)}, f32[256,384]{1,0:T(8,128)S(1)}, u32[]{:S(2)}, u32[]{:S(2)}) collective-permute-start(f32[256,384]{1,0:T(8,128)S(1)} %get-tuple-element.90), channel_id=1, source_target_pairs={{2,0},{4,2},{6,4},{8,6},{10,8},{12,10},{14,12},{16,14},{18,16},{20... | collective-permute-start | bytes 1179656 | tf_op jit(solution)/shard_map/ppermute | solution.py:111
  46.2 13.2 %collective-permute-start.8 = (f32[256,384]{1,0:T(8,128)S(1)}, f32[256,384]{1,0:T(8,128)S(1)}, u32[]{:S(2)}, u32[]{:S(2)}) collective-permute-start(f32[256,384]{1,0:T(8,128)S(1)} %get-tuple-element.87), channel_id=1, source_target_pairs={{0,2},{2,4},{4,6},{6,8},{8,10},{10,12},{12,14},{14,16},{16,18},{18... | collective-permute-start | bytes 1179656 | tf_op jit(solution)/shard_map/ppermute | solution.py:111
  46.3 16.0 %collective-permute-start.9 = (f32[256,384]{1,0:T(8,128)S(1)}, f32[256,384]{1,0:T(8,128)S(1)}, u32[]{:S(2)}, u32[]{:S(2)}) collective-permute-start(f32[256,384]{1,0:T(8,128)S(1)} %get-tuple-element.88), channel_id=1, source_target_pairs={{2,0},{4,2},{6,4},{8,6},{10,8},{12,10},{14,12},{16,14},{18,16},{20... | collective-permute-start | bytes 1179656 | tf_op jit(solution)/shard_map/ppermute | solution.py:111
  56.0 16.1 %collective-permute-start.14 = (f32[256,384]{1,0:T(8,128)S(1)}, f32[256,384]{1,0:T(8,128)S(1)}, u32[]{:S(2)}, u32[]{:S(2)}) collective-permute-start(f32[256,384]{1,0:T(8,128)S(1)} %get-tuple-element.101), channel_id=1, source_target_pairs={{0,2},{2,4},{4,6},{6,8},{8,10},{10,12},{12,14},{14,16},{16,18},{18... | collective-permute-start | bytes 1179656 | tf_op jit(solution)/shard_map/ppermute | solution.py:111
  58.5 13.6 %collective-permute-start.15 = (f32[256,384]{1,0:T(8,128)S(1)}, f32[256,384]{1,0:T(8,128)S(1)}, u32[]{:S(2)}, u32[]{:S(2)}) collective-permute-start(f32[256,384]{1,0:T(8,128)S(1)} %get-tuple-element.102), channel_id=1, source_target_pairs={{2,0},{4,2},{6,4},{8,6},{10,8},{12,10},{14,12},{16,14},{18,16},{20... | collective-permute-start | bytes 1179656 | tf_op jit(solution)/shard_map/ppermute | solution.py:111
  63.1 13.2 %collective-permute-start.12 = (f32[256,384]{1,0:T(8,128)S(1)}, f32[256,384]{1,0:T(8,128)S(1)}, u32[]{:S(2)}, u32[]{:S(2)}) collective-permute-start(f32[256,384]{1,0:T(8,128)S(1)} %get-tuple-element.99), channel_id=1, source_target_pairs={{0,2},{2,4},{4,6},{6,8},{8,10},{10,12},{12,14},{14,16},{16,18},{18... | collective-permute-start | bytes 1179656 | tf_op jit(solution)/shard_map/ppermute | solution.py:111
  63.2 13.9 %collective-permute-start.13 = (f32[256,384]{1,0:T(8,128)S(1)}, f32[256,384]{1,0:T(8,128)S(1)}, u32[]{:S(2)}, u32[]{:S(2)}) collective-permute-start(f32[256,384]{1,0:T(8,128)S(1)} %get-tuple-element.100), channel_id=1, source_target_pairs={{2,0},{4,2},{6,4},{8,6},{10,8},{12,10},{14,12},{16,14},{18,16},{20... | collective-permute-start | bytes 1179656 | tf_op jit(solution)/shard_map/ppermute | solution.py:111
  77.8 10.0 %collective-permute-start.16 = (f32[256,512]{1,0:T(8,128)S(1)}, f32[256,512]{1,0:T(8,128)}, u32[]{:S(2)}, u32[]{:S(2)}) collective-permute-start(f32[256,512]{1,0:T(8,128)S(1)} %filter_step.14.refs_0_.refs_4_.refs_5_), channel_id=1, source_target_pairs={{0,1},{2,3},{4,5},{6,7},{8,9},{10,11},{12,13},{14,15},{16,17},{18,... | collective-permute-start | bytes 1572872 | tf_op jit(solution)/shard_map/ppermute | solution.py:501
  90.9 7.7 %collective-permute-start.18 = (f32[320,128]{1,0:T(8,128)S(1)}, f32[320,128]{1,0:T(8,128)S(1)}, u32[]{:S(2)}, u32[]{:S(2)}) collective-permute-start(f32[320,128]{1,0:T(8,128)S(1)} %dynamic-slice_bitcast_fusion.3), channel_id=1, source_target_pairs={{0,4},{1,5},{2,6},{3,7},{4,0},{5,1},{6,2},{7,3},{8,12},{9,13},{10,... | collective-permute-start | bytes 491528 | tf_op jit(solution)/shard_map/ppermute | solution.py:495
  94.4 14.7 %collective-permute-start.22 = (f32[256,512]{1,0:T(8,128)S(1)}, f32[256,512]{1,0:T(8,128)S(1)}, u32[]{:S(2)}, u32[]{:S(2)}) collective-permute-start(f32[256,512]{1,0:T(8,128)S(1)} %filter_step.15.refs_1_.refs_4_.refs_6_), channel_id=1, source_target_pairs={{0,1},{2,3},{4,5},{6,7},{8,9},{10,11},{12,13},{14,15},{16,17},{18,... | collective-permute-start | bytes 1572872 | tf_op jit(solution)/shard_map/ppermute | solution.py:501
  113.1 8.2 %collective-permute-start.24 = (f32[1024,128]{1,0:T(8,128)}, f32[1024,128]{1,0:T(8,128)S(1)}, u32[]{:S(2)}, u32[]{:S(2)}) collective-permute-start(f32[1024,128]{1,0:T(8,128)} %dynamic-slice_bitcast_fusion), channel_id=1, source_target_pairs={{1,3},{3,1},{5,7},{7,5},{9,11},{11,9},{13,15},{15,13},{17,19},{19,... | collective-permute-start | bytes 1572872 | tf_op jit(solution)/shard_map/ppermute | solution.py:495
  121.4 11.4 %collective-permute-start.28 = (f32[512,128]{1,0:T(8,128)S(1)}, f32[512,128]{1,0:T(8,128)S(1)}, u32[]{:S(2)}, u32[]{:S(2)}) collective-permute-start(f32[512,128]{1,0:T(8,128)S(1)} %dynamic-slice_bitcast_fusion.2), channel_id=1, source_target_pairs={{1,5},{3,7},{5,1},{7,3},{9,13},{11,15},{13,9},{15,11},{17,21},{19,... | collective-permute-start | bytes 786440 | tf_op jit(solution)/shard_map/ppermute | solution.py:495
  132.9 22.6 %collective-permute-start.29 = (f32[4,80,128]{2,1,0:T(8,128)S(1)}, f32[4,80,128]{2,1,0:T(8,128)S(1)}, u32[]{:S(2)}, u32[]{:S(2)}) collective-permute-start(f32[4,80,128]{2,1,0:T(8,128)S(1)} %get-tuple-element.121.refs_0_), channel_id=1, source_target_pairs={{0,2},{1,3},{2,0},{3,1},{4,6},{5,7},{6,4},{7,5},{8,10},{9,11},{10,... | collective-permute-start | bytes 491528 | tf_op jit(solution)/shard_map/ppermute | solution.py:495
  135.4 20.0 %collective-permute-start.30 = (f32[4,80,128]{2,1,0:T(8,128)S(1)}, f32[4,80,128]{2,1,0:T(8,128)S(1)}, u32[]{:S(2)}, u32[]{:S(2)}) collective-permute-start(f32[4,80,128]{2,1,0:T(8,128)S(1)} %get-tuple-element.121.refs_0_), channel_id=1, source_target_pairs={{0,4},{1,5},{2,6},{3,7},{4,0},{5,1},{6,2},{7,3},{8,12},{9,13},{10,... | collective-permute-start | bytes 491528 | tf_op jit(solution)/shard_map/ppermute | solution.py:495
  136.9 17.3 %collective-permute-start.32 = (f32[128,128]{1,0:T(8,128)S(1)}, f32[128,128]{1,0:T(8,128)S(1)}, u32[]{:S(2)}, u32[]{:S(2)}) collective-permute-start(f32[128,128]{1,0:T(8,128)S(1)} %get-tuple-element.143), channel_id=1, source_target_pairs={{1,9},{3,11},{5,13},{7,15},{9,1},{11,3},{13,5},{15,7},{17,25},{19,... | collective-permute-start | bytes 196616 | tf_op jit(solution)/shard_map/ppermute | solution.py:495
  139.8 15.6 %collective-permute-start.33 = (f32[128,128]{1,0:T(8,128)S(1)}, f32[128,128]{1,0:T(8,128)S(1)}, u32[]{:S(2)}, u32[]{:S(2)}) collective-permute-start(f32[128,128]{1,0:T(8,128)S(1)} %get-tuple-element.142), channel_id=1, source_target_pairs={{1,17},{3,19},{5,21},{7,23},{9,25},{11,27},{13,29},{15,31},{17,1},... | collective-permute-start | bytes 196616 | tf_op jit(solution)/shard_map/ppermute | solution.py:495
  143.1 12.4 %collective-permute-start.34 = (f32[128,128]{1,0:T(8,128)S(1)}, f32[128,128]{1,0:T(8,128)S(1)}, u32[]{:S(2)}, u32[]{:S(2)}) collective-permute-start(f32[128,128]{1,0:T(8,128)S(1)} %get-tuple-element.141), channel_id=1, source_target_pairs={{1,25},{3,27},{5,29},{7,31},{9,17},{11,19},{13,21},{15,23},{17,9},... | collective-permute-start | bytes 196616 | tf_op jit(solution)/shard_map/ppermute | solution.py:495
  160.2 21.1 %collective-permute-start.35 = (f32[128,128]{1,0:T(8,128)S(1)}, f32[128,128]{1,0:T(8,128)S(1)}, u32[]{:S(2)}, u32[]{:S(2)}) collective-permute-start(f32[128,128]{1,0:T(8,128)S(1)} %fusion), channel_id=1, source_target_pairs={{1,9},{3,11},{5,13},{7,15},{9,1},{11,3},{13,5},{15,7},{17,25},{19,... | collective-permute-start | bytes 196616 | tf_op jit(solution)/shard_map/ppermute | solution.py:495
  162.2 19.1 %collective-permute-start.36 = (f32[128,128]{1,0:T(8,128)S(1)}, f32[128,128]{1,0:T(8,128)S(1)}, u32[]{:S(2)}, u32[]{:S(2)}) collective-permute-start(f32[128,128]{1,0:T(8,128)S(1)} %fusion), channel_id=1, source_target_pairs={{1,17},{3,19},{5,21},{7,23},{9,25},{11,27},{13,29},{15,31},{17,1},... | collective-permute-start | bytes 196616 | tf_op jit(solution)/shard_map/ppermute | solution.py:495
  166.3 14.9 %collective-permute-start.37 = (f32[128,128]{1,0:T(8,128)S(1)}, f32[128,128]{1,0:T(8,128)S(1)}, u32[]{:S(2)}, u32[]{:S(2)}) collective-permute-start(f32[128,128]{1,0:T(8,128)S(1)} %fusion), channel_id=1, source_target_pairs={{1,25},{3,27},{5,29},{7,31},{9,17},{11,19},{13,21},{15,23},{17,9},... | collective-permute-start | bytes 196616 | tf_op jit(solution)/shard_map/ppermute | solution.py:495
  181.3 20.9 %collective-permute-start.38 = (f32[4,128,128]{2,1,0:T(8,128)S(1)}, f32[4,128,128]{2,1,0:T(8,128)S(1)}, u32[]{:S(2)}, u32[]{:S(2)}) collective-permute-start(f32[4,128,128]{2,1,0:T(8,128)S(1)} %pad_maximum_fusion.1.refs_1_), channel_id=1, source_target_pairs={{1,3},{3,1},{5,7},{7,5},{9,11},{11,9},{13,15},{15,13},{17,19},{19,... | collective-permute-start | bytes 786440 | tf_op jit(solution)/shard_map/ppermute | solution.py:495
  184.3 17.9 %collective-permute-start.39 = (f32[4,128,128]{2,1,0:T(8,128)S(1)}, f32[4,128,128]{2,1,0:T(8,128)S(1)}, u32[]{:S(2)}, u32[]{:S(2)}) collective-permute-start(f32[4,128,128]{2,1,0:T(8,128)S(1)} %pad_maximum_fusion.1.refs_1_), channel_id=1, source_target_pairs={{1,5},{3,7},{5,1},{7,3},{9,13},{11,15},{13,9},{15,11},{17,21},{19,... | collective-permute-start | bytes 786440 | tf_op jit(solution)/shard_map/ppermute | solution.py:495
  187.3 14.9 %collective-permute-start.40 = (f32[4,128,128]{2,1,0:T(8,128)S(1)}, f32[4,128,128]{2,1,0:T(8,128)S(1)}, u32[]{:S(2)}, u32[]{:S(2)}) collective-permute-start(f32[4,128,128]{2,1,0:T(8,128)S(1)} %pad_maximum_fusion.1.refs_1_), channel_id=1, source_target_pairs={{1,7},{3,5},{5,3},{7,1},{9,15},{11,13},{13,11},{15,9},{17,23},{19,... | collective-permute-start | bytes 786440 | tf_op jit(solution)/shard_map/ppermute | solution.py:495
  (15 other events, 58.7 us)

commit v3 on v1

--- a/solution.py
+++ b/solution.py
@@ -17,8 +17,9 @@
 NN = (((1,), (0,)), ((), ()))
 SCALARS = pl.BlockSpec(memory_space=pltpu.SMEM)
 WHOLE = pl.BlockSpec(memory_space=pltpu.VMEM)
-AFAR = pl.BlockSpec(memory_space=pltpu.HBM)
+AFAR = pl.BlockSpec(memory_space=pl.ANY)
 ROOMY = pltpu.CompilerParams(vmem_limit_bytes=28 * 2 ** 20)
+ALONE = pltpu.CompilerParams(vmem_limit_bytes=48 * 2 ** 20)
 
 
 def split(x):
@@ -120,6 +121,7 @@
     for step in range(STEPS):
         more = step < STEPS - 1
         for c in range(CHUNKS):
+            halos[c], current[c - 1] = lax.optimization_barrier((halos[c], current[c - 1]))
             following, *edges = filter_step(halos[c], current[c], band, previous[c], more)
             previous[c], current[c] = current[c], following
             if more:
@@ -285,13 +287,12 @@
     half = (len(refs) - 1) // 2
     out_ref = refs[-1]
     mine, other = split(joined(refs[:half])), split(joined(refs[half:-1]))
-    rows = out_ref.shape[0]
     blocks = mine[0].shape[0] // NB
     for i in range(blocks):
         here = slice(i * NB, (i + 1) * NB)
         product = dot3((mine[0][here], mine[1][here]), other, NT)
         for j in range(blocks):
-            start = scatter_order((i * blocks + j) * NB, rows)
+            start = (i * blocks + j) * NB
             out_ref[start:start + NB, :] = product[:, j * NB:(j + 1) * NB]
 
 
@@ -333,15 +334,15 @@
             gram_ref[i * NB:(i + 1) * NB, j * NB:(j + 1) * NB] = block
 
 
-def first_half_kernel(where_ref, *refs):
-    pieces, mine, other = refs[:4], refs[4:4 + CHUNKS], refs[4 + CHUNKS:4 + 2 * CHUNKS]
-    top_ref, inverse_ref, flat, gram, field, total, low0, low1, done0, done1, sems = refs[4 + 2 * CHUNKS:]
-    place, near, far = where_ref[0], where_ref[1], where_ref[2]
+def first_half_kernel(where_ref, gram_in, *refs):
+    mine, other = refs[:CHUNKS], refs[CHUNKS:2 * CHUNKS]
+    top_ref, inverse_ref, flat, gram, field, total, low0, low1, done0, done1, sems = refs[2 * CHUNKS:]
     size, columns = top_ref.shape
-    rows = pieces[0].shape[1]
+    place, far = where_ref[0], where_ref[1]
+    rows = gram_in.shape[2]
     pairs = [
-        (piece.at[j], rows_of(flat, ((near ^ i) * 4 + (far ^ j)) * rows, rows))
-        for i, piece in enumerate(pieces) for j in range(4)
+        (gram_in.at[i, j], rows_of(flat, (i * 4 + (far ^ j)) * rows, rows))
+        for i in range(4) for j in range(4)
     ]
 
     @pl.when(place == 0)
@@ -357,58 +358,57 @@
     lanes = lax.broadcasted_iota(jnp.int32, (size, size), 1)
     field[:, columns:] = jnp.where(rows == lanes, 1.0, 0.0)
     eliminate(gram, field, (low0, low1), (done0, done1), total, size // NB)
-    top_ref[...] = total[:, :columns]
-    inverse_ref[...] = total[:, columns:]
-
-
-def first_half(where, pieces, mine, other):
+    fetch([(total.at[:, :columns], top_ref), (total.at[:, columns:], inverse_ref)], sems)
+
+
+def first_half(where, gram, mine, other):
     size, columns = sum(part.shape[0] for part in mine), mine[0].shape[1]
     f32 = jnp.float32
-    flat_rows = 4 * pieces[0].shape[0] * pieces[0].shape[1]
-    operands = (*pieces, *mine, *other)
-    shapes = ((size, columns), (size, size))
     return pl.pallas_call(
         first_half_kernel,
-        out_shape=tuple(jax.ShapeDtypeStruct(shape, f32) for shape in shapes),
-        in_specs=[SCALARS] + [AFAR] * len(operands),
-        out_specs=(WHOLE, WHOLE),
+        out_shape=tuple(jax.ShapeDtypeStruct((size, n), f32) for n in (columns, size)),
+        in_specs=[SCALARS] + [AFAR] * (1 + 2 * CHUNKS),
+        out_specs=(AFAR, AFAR),
         scratch_shapes=[
-            pltpu.VMEM((flat_rows, NB), f32),
+            pltpu.VMEM((16 * gram.shape[2], NB), f32),
             pltpu.VMEM((size, size), f32),
             pltpu.VMEM((size, columns + size), f32),
             pltpu.VMEM((size, columns + size), f32),
         ] + elimination_scratch(size, columns + size) + [pltpu.SemaphoreType.DMA((16 + CHUNKS,))],
-        compiler_params=ROOMY,
+        compiler_params=ALONE,
         cost_estimate=pl.CostEstimate(flops=2 * 10 ** 10, bytes_accessed=10 ** 7, transcendentals=0),
         name="first_half",
-    )(where, *operands)
-
-
-def second_half_kernel(scale, where_ref, *refs):
-    rest, mine = refs[0], refs[1:1 + CHUNKS]
-    top_ref, inverse_ref, out_ref = refs[1 + CHUNKS:4 + CHUNKS]
-    flat, corner, gram, field, total, low0, low1, done0, done1, sems = refs[4 + CHUNKS:]
-    place = where_ref[0]
-    size, columns = top_ref.shape
+    )(where, gram, *mine, *other)
+
+
+def second_half_kernel(scale, where_ref, rest, *refs):
+    mine = refs[:CHUNKS]
+    top_in, inverse_in, out_ref = refs[CHUNKS:3 + CHUNKS]
+    flat, corner, gram, top, inverse, field, total, low0, low1, done0, done1, sems = refs[3 + CHUNKS:]
+    size, columns = top.shape
     blocks = size // NB
-    rows = rest.shape[2] - NB
-
-    @pl.when(place == 0)
+    rows = flat.shape[0] // 16
+
+    @pl.when(where_ref[0] == 0)
     def _():
-        out_ref[...] = top_ref[...] * scale
-
-    @pl.when(place != 0)
+        fetch([(top_in, top)], sems)
+        out_ref[...] = top[...] * scale
+
+    @pl.when(where_ref[0] != 0)
     def _():
-        pairs = stacked(mine, field, columns)
-        for i in range(4):
-            for j in range(4):
-                pairs.append((rest.at[i, j, :rows], rows_of(flat, (i * 4 + j) * rows, rows)))
-                pairs.append((rest.at[i, j, rows:], corner.at[i * NB:(i + 1) * NB, j * NB:(j + 1) * NB]))
+        pairs = stacked(mine, field, columns) + [(top_in, top), (inverse_in, inverse)]
+        far = where_ref[1]
+        for i in range(blocks):
+            for j in range(blocks):
+                here = far ^ j
+                pairs.append((rest.at[i, j, :rows], rows_of(flat, (i * blocks + here) * rows, rows)))
+                lanes = pl.ds(pl.multiple_of(here * NB, NB), NB)
+                pairs.append((rest.at[i, j, rows:], corner.at[i * NB:(i + 1) * NB, lanes]))
         fetch(pairs, sems)
         lower_blocks(flat, gram)
-        low = split(dot3(split(corner[...]), split(inverse_ref[...]), NT))
+        low = split(dot3(split(corner[...]), split(inverse[...]), NT))
         gram[...] = gram[...] - dot3(low, low, NT)
-        field[...] = field[...] - dot3(low, split(top_ref[...]), NN)
+        field[...] = field[...] - dot3(low, split(top[...]), NN)
         eliminate(gram, field, (low0, low1), (done0, done1), total, blocks)
         out_ref[...] = total[...] * scale
 
@@ -416,19 +416,16 @@
 def second_half(where, rest, mine, top, inverse, scale):
     size, columns = top.shape
     f32 = jnp.float32
+    square, wide = pltpu.VMEM((size, size), f32), pltpu.VMEM((size, columns), f32)
     return pl.pallas_call(
         functools.partial(second_half_kernel, scale),
         out_shape=jax.ShapeDtypeStruct((size, columns), f32),
-        in_specs=[SCALARS] + [AFAR] * (1 + CHUNKS) + [WHOLE] * 2,
+        in_specs=[SCALARS] + [AFAR] * (3 + CHUNKS),
         out_specs=WHOLE,
         scratch_shapes=[
-            pltpu.VMEM((16 * (rest.shape[2] - NB), NB), f32),
-            pltpu.VMEM((size, size), f32),
-            pltpu.VMEM((size, size), f32),
-            pltpu.VMEM((size, columns), f32),
-            pltpu.VMEM((size, columns), f32),
-        ] + elimination_scratch(size, columns) + [pltpu.SemaphoreType.DMA((32 + CHUNKS,))],
-        compiler_params=ROOMY,
+            pltpu.VMEM((16 * (rest.shape[2] - NB), NB), f32), square, square, wide, square, wide, wide,
+        ] + elimination_scratch(size, columns) + [pltpu.SemaphoreType.DMA((34 + CHUNKS,))],
+        compiler_params=ALONE,
         name="second_half",
     )(where, rest, *mine, top, inverse)
 
@@ -473,30 +470,28 @@
     rank = lax.axis_index("rows")
     place = lax.axis_index("vecs")
     near, far = rank % 4, rank // 4
-    where = jnp.stack([place, near, far]).astype(jnp.int32)
+    where = jnp.stack([place, far]).astype(jnp.int32)
     near_groups = [list(range(4 * g, 4 * g + 4)) for g in range(4)]
     far_groups = [list(range(g, 16, 4)) for g in range(4)]
     below = [send_up(part, 0) for part in current]
-    own, below[0] = together((current, below[0]))
-    half = swap_half(own_gram(own), near % 2, 1)
+    half = swap_half(own_gram(current), near % 2, 1)
+    half, below[0] = together((half, below[0]))
     fourth = swap_half(half, near // 2, 2)
     fourth, *below = together((fourth, *below))
-    corner = cross_gram(current, below)
-    corner = swap_half(corner, near % 2, 1, (1,))
+    fourth, corner = together((fourth, cross_gram(current, below)))
+    corner = lax.psum_scatter(corner, "rows", axis_index_groups=near_groups, tiled=True)
     mine = reduce_group(fourth, far, FAR)
-    mine, corner = together((mine, corner))
     first = jnp.where(place == 0, mine, send_up(mine, 0))
-    corner = swap_half(corner, near // 2, 2, (1,))
+    first = jnp.stack([first] + [send(first, i * FAR) for i in range(1, 4)])
     first, corner = together((first, corner))
-    first = jnp.stack([first] + [send(first, i * FAR) for i in range(1, 4)])
-    corner = reduce_group(corner, far, FAR, (1,))
-    first, corner = together((first, corner))
+    gram = lax.all_gather(first, "rows", axis_index_groups=near_groups)
+    corner = lax.all_to_all(corner.reshape(4, -1, NB), "rows", 0, 0, axis_index_groups=far_groups)
+    corner = jnp.sum(corner, axis=0)
     rest = jnp.concatenate([mine, corner], axis=0)
-    rest = lax.all_gather(rest, "rows", axis_index_groups=far_groups)
-    pieces = [first] + [send(first, i * NEAR) for i in range(1, 4)]
-    pieces, rest = together((pieces, rest))
+    rest = jnp.stack([rest] + [send(rest, i * FAR, (1,)) for i in range(1, 4)])
+    gram, rest = together((gram, rest))
     rest = lax.all_gather(rest, "rows", axis_index_groups=near_groups)
-    top, inverse = first_half(where, pieces, current, below)
+    top, inverse = first_half(where, gram, current, below)
     return second_half(where, rest, current, top, inverse, scale)
 
 

time: 231 us -> 233 us (level)
  blocking collectives: 13.4 us -> 22.2 us
  starting transfers between devices: 42.2 us -> 34.1 us
  local copies, waits for them, and re-layouts: 13.8 us -> 9.37 us
  waiting for transfers between devices: 86.7 us -> 90.8 us
  Pallas kernels: 58.2 us -> 60.6 us
    ppermute x3, waiting for transfers between devices: 7.59 us -> 20.4 us  [send_up(): return lax.ppermute(x, ('rows', 'vecs'), pairs)]
    all_to_all x0 -> x1, blocking collectives: none -> 11.2 us  [orthonormalize_planes(): lax.all_to_all(corner.reshape(4, -1, NB), 'rows', 0, 0, axis_index_groups...]
    ppermute x16, waiting for transfers between devices: 61.5 us -> 51.8 us  [exchange_edges(): return (lax.ppermute(last, 'rows', up), lax.ppermute(first, 'rows', down))]
    ppermute x16 -> x11, starting transfers between devices: 29.3 us -> 19.9 us  [send(): return lax.ppermute(x, ('rows', 'vecs'), pairs)]
    reduce_scatter x0 -> x1, waiting for transfers between devices: none -> 9.16 us  [orthonormalize_planes(): lax.psum_scatter(corner, 'rows', axis_index_groups=near_groups, tiled=True)]
    ppermute x16 -> x11, waiting for transfers between devices: 17.5 us -> 9.42 us  [send(): return lax.ppermute(x, ('rows', 'vecs'), pairs)]
    unnamed x30 -> x20, local copies, waits for them, and re-layouts: 8.98 us -> 5.43 us
    pallas_call x8, Pallas kernels: 7.73 us -> 10.9 us  [filter_step(): pl.pallas_call(functools.partial(step_kernel, previous is not None, has_e...]
  transfers between devices with their start and end apart: 36 -> 32, of which waited for: 22 -> 19; matrix products, arithmetic and copies ran while one was open for 1% -> 1% of each run, Pallas kernels for 13% -> 13%
where the time goes in v3:
time: 233 us; the launch traced here: 232 us
  waiting for transfers between devices  90.8 us (39%)
  Pallas kernels  60.6 us (26%)
  starting transfers between devices  34.1 us (15%)
  blocking collectives  22.2 us (10%)
  between operations  13.8 us (6%)
  local copies, waits for them, and re-layouts  9.37 us (4%)
    ppermute x16, waiting for transfers between devices, exchange_edges(): return (lax.ppermute(last, 'rows', up), lax.ppermute(first, 'rows', down))  51.8 us
    pallas_call x1, Pallas kernels, second_half(): pl.pallas_call(functools.partial(second_half_kernel, scale), out_shape=ja...  23.6 us
    pallas_call x1, Pallas kernels, first_half(): pl.pallas_call(first_half_kernel, out_shape=tuple((jax.ShapeDtypeStruct((...  20.6 us
    ppermute x3, waiting for transfers between devices, send_up(): return lax.ppermute(x, ('rows', 'vecs'), pairs)  20.4 us
    ppermute x11, starting transfers between devices, send(): return lax.ppermute(x, ('rows', 'vecs'), pairs)  19.9 us
    all_to_all x1, blocking collectives, orthonormalize_planes(): lax.all_to_all(corner.reshape(4, -1, NB), 'rows', 0, 0, axis_index_groups...  11.2 us
    all_gather x1, blocking collectives, orthonormalize_planes(): gram = lax.all_gather(first, 'rows', axis_index_groups=near_groups)  11 us
    pallas_call x8, Pallas kernels, filter_step(): pl.pallas_call(functools.partial(step_kernel, previous is not None, has_e...  10.9 us
  transfers between devices with their start and end apart: 32, of which 19 were waited for; matrix products, arithmetic and copies ran while one was open for 1% of the time, Pallas kernels for 13%

profile of v3, /device:TPU:5, one launch (start us, length us, event | category | flops | bytes accessed | tf_op | source)
XLA Modules:
  0.0 231.9 jit_solution(9340076710795544037)
XLA Ops:
  6.5 2.6 %fusion.5 = (f32[256,384]{1,0:T(8,128)}, f32[256,384]{1,0:T(8,128)}, f32[256,384]{1,0:T(8,128)}, f32[256,384]{1,0:T(8,128)}) fusion(f32[512,512]{1,0:T(8,128)} %param.5), kind=kLoop, calls=%fused_computation.22 | loop fusion | bytes 3145728 | tf_op jit(solution)/shard_map/slice | solution.py:119
  9.2 1.8 collective-permute-start.2
  10.9 1.7 collective-permute-start
  16.6 7.8 %collective-permute-done.2.refs_0_ = f32[256,384]{1,0:T(8,128)S(1)} collective-permute-done((f32[256,384]{1,0:T(8,128)}, f32[256,384]{1,0:T(8,128)S(1)}, u32[]{:S(2)}, u32[]{:S(2)}) %collective-permute-start.2) | collective-permute-done | bytes 393248 | tf_op jit(solution)/shard_map/ppermute | solution.py:111
  24.4 2.5 %collective-permute-done.3.refs_2_ = f32[256,384]{1,0:T(8,128)} collective-permute-done((f32[256,384]{1,0:T(8,128)}, f32[256,384]{1,0:T(8,128)}, u32[]{:S(2)}, u32[]{:S(2)}) %collective-permute-start.3) | collective-permute-done | bytes 393248 | tf_op jit(solution)/shard_map/ppermute | solution.py:111
  29.2 6.0 %collective-permute-done.1.refs_2_ = f32[256,384]{1,0:T(8,128)S(1)} collective-permute-done((f32[256,384]{1,0:T(8,128)}, f32[256,384]{1,0:T(8,128)S(1)}, u32[]{:S(2)}, u32[]{:S(2)}) %collective-permute-start.1) | collective-permute-done | bytes 393248 | tf_op jit(solution)/shard_map/ppermute | solution.py:111
  36.5 11.3 %collective-permute-done.7.refs_2_ = f32[256,384]{1,0:T(8,128)S(1)} collective-permute-done((f32[256,384]{1,0:T(8,128)S(1)}, f32[256,384]{1,0:T(8,128)S(1)}, u32[]{:S(2)}, u32[]{:S(2)}) %collective-permute-start.7) | collective-permute-done | bytes 393248 | tf_op jit(solution)/shard_map/ppermute | solution.py:111
  49.1 2.9 %collective-permute-done.5.refs_2_ = f32[256,384]{1,0:T(8,128)S(1)} collective-permute-done((f32[256,384]{1,0:T(8,128)S(1)}, f32[256,384]{1,0:T(8,128)S(1)}, u32[]{:S(2)}, u32[]{:S(2)}) %collective-permute-start.5) | collective-permute-done | bytes 393248 | tf_op jit(solution)/shard_map/ppermute | solution.py:111
  53.4 8.4 %collective-permute-done.10.refs_0_ = f32[256,384]{1,0:T(8,128)S(1)} collective-permute-done((f32[256,384]{1,0:T(8,128)S(1)}, f32[256,384]{1,0:T(8,128)S(1)}, u32[]{:S(2)}, u32[]{:S(2)}) %collective-permute-start.10) | collective-permute-done | bytes 393248 | tf_op jit(solution)/shard_map/ppermute | solution.py:111
  63.4 2.5 %collective-permute-start.14 = (f32[256,384]{1,0:T(8,128)}, f32[256,384]{1,0:T(8,128)}, u32[]{:S(2)}, u32[]{:S(2)}) collective-permute-start(f32[256,384]{1,0:T(8,128)} %get-tuple-element.92), channel_id=1, source_target_pairs={{0,2},{2,4},{4,6},{6,8},{8,10},{10,12},{12,14},{14,16},{16,18},{18... | collective-permute-start | bytes 1179656 | tf_op jit(solution)/shard_map/ppermute | solution.py:111
  66.0 2.9 %collective-permute-done.9.refs_2_ = f32[256,384]{1,0:T(8,128)S(1)} collective-permute-done((f32[256,384]{1,0:T(8,128)S(1)}, f32[256,384]{1,0:T(8,128)S(1)}, u32[]{:S(2)}, u32[]{:S(2)}) %collective-permute-start.9) | collective-permute-done | bytes 393248 | tf_op jit(solution)/shard_map/ppermute | solution.py:111
  71.8 7.5 %collective-permute-done.14.refs_0_ = f32[256,384]{1,0:T(8,128)} collective-permute-done((f32[256,384]{1,0:T(8,128)}, f32[256,384]{1,0:T(8,128)}, u32[]{:S(2)}, u32[]{:S(2)}) %collective-permute-start.14) | collective-permute-done | bytes 393248 | tf_op jit(solution)/shard_map/ppermute | solution.py:111
  79.4 1.9 filter_step.14.refs_0_
  81.3 2.3 collective-permute-done.12.refs_0_
  83.6 1.8 filter_step.15.refs_1_
  89.5 12.2 %collective-permute-done.17.refs_2_ = f32[256,512]{1,0:T(8,128)S(1)} collective-permute-done((f32[256,512]{1,0:T(8,128)S(1)}, f32[256,512]{1,0:T(8,128)S(1)}, u32[]{:S(2)}, u32[]{:S(2)}) %collective-permute-start.17) | collective-permute-done | bytes 524320 | tf_op jit(solution)/shard_map/ppermute | solution.py:448
  101.8 3.2 %collective-permute-start.18 = (f32[320,128]{1,0:T(8,128)S(1)}, f32[320,128]{1,0:T(8,128)S(1)}, u32[]{:S(2)}, u32[]{:S(2)}) collective-permute-start(f32[320,128]{1,0:T(8,128)S(1)} %dynamic-slice_bitcast_fusion.1), channel_id=1, source_target_pairs={{0,4},{1,5},{2,6},{3,7},{4,0},{5,1},{6,2},{7,3},{8,12},{9,13},{10,... | collective-permute-start | bytes 491528 | tf_op jit(solution)/shard_map/ppermute | solution.py:442
  104.9 3.3 %collective-permute-done.18 = f32[320,128]{1,0:T(8,128)S(1)} collective-permute-done((f32[320,128]{1,0:T(8,128)S(1)}, f32[320,128]{1,0:T(8,128)S(1)}, u32[]{:S(2)}, u32[]{:S(2)}) %collective-permute-start.18) | collective-permute-done | bytes 163872 | tf_op jit(solution)/shard_map/ppermute | solution.py:442
  108.3 4.7 %collective-permute-done.19.refs_3_ = f32[256,512]{1,0:T(8,128)S(1)} collective-permute-done((f32[256,512]{1,0:T(8,128)S(1)}, f32[256,512]{1,0:T(8,128)S(1)}, u32[]{:S(2)}, u32[]{:S(2)}) %collective-permute-start.19) | collective-permute-done | bytes 524320 | tf_op jit(solution)/shard_map/ppermute | solution.py:448
  113.0 3.1 %cross_gram.1 = f32[2048,128]{1,0:T(8,128)} custom-call(f32[256,512]{1,0:T(8,128)S(1)} %filter_step.14.refs_0_, f32[256,512]{1,0:T(8,128)S(1)} %filter_step.15.refs_1_, f32[256,512]{1,0:T(8,128)S(1)} %collective-permute-done.17.refs_2_, f32[256,512]{1,0:T(8,128)S(1)} %collective-permute-done.19.refs_3_), custom_call_target="tpu_custom_call" | custom-call | tf_op jit(solution)/shard_map/cross_gram/pallas_call | solution.py:301
  120.1 2.0 collective-permute-done.21
  122.1 2.2 collective-permute-done.22
  125.5 3.4 %collective-permute-done.23 = f32[80,128]{1,0:T(8,128)S(1)} collective-permute-done((f32[80,128]{1,0:T(8,128)S(1)}, f32[80,128]{1,0:T(8,128)S(1)}, u32[]{:S(2)}, u32[]{:S(2)}) %collective-permute-start.23) | collective-permute-done | bytes 40992 | tf_op jit(solution)/shard_map/ppermute | solution.py:448
  129.8 2.7 %collective-permute-start.26 = (f32[80,128]{1,0:T(8,128)S(1)}, f32[80,128]{1,0:T(8,128)S(1)}, u32[]{:S(2)}, u32[]{:S(2)}) collective-permute-start(f32[80,128]{1,0:T(8,128)S(1)} %broadcast_select_fusion), channel_id=1, source_target_pairs={{0,24},{1,25},{2,26},{3,27},{4,28},{5,29},{6,30},{7,31},{8,16},{9,... | collective-permute-start | bytes 122888 | tf_op jit(solution)/shard_map/ppermute | solution.py:442
  134.5 9.2 %reduce-scatter.2.cloned.1.call-done = f32[512,128]{1,0:T(8,128)} async-done(((f32[2048,128]{1,0:T(8,128)}), f32[512,128]{1,0:T(8,128)}) %reduce-scatter.2.cloned.1.call-update) | async-done | bytes 262160 | tf_op jit(solution)/shard_map/reduce_scatter | solution.py:482
  143.7 11.2 %all_to_all.5 = f32[4,128,128]{2,1,0:T(8,128)S(1)} all-to-all(f32[4,128,128]{2,1,0:T(8,128)} %bitcast.43), channel_id=1, replica_groups={{0,8,16,24},{2,10,18,26},{4,12,20,28},{6,14,22,30},{1,9,17,25},{3,11,19..., dimensions={0} | all-to-all | bytes 524288 | tf_op jit(solution)/shard_map/all_to_all | solution.py:488
  154.9 2.5 %collective-permute-start.27 = (f32[208,128]{1,0:T(8,128)S(1)}, f32[208,128]{1,0:T(8,128)S(1)}, u32[]{:S(2)}, u32[]{:S(2)}) collective-permute-start(f32[208,128]{1,0:T(8,128)S(1)} %get-tuple-element.125), channel_id=1, source_target_pairs={{1,9},{3,11},{5,13},{7,15},{9,1},{11,3},{13,5},{15,7},{17,25},{19,... | collective-permute-start | bytes 319496 | tf_op jit(solution)/shard_map/ppermute | solution.py:442
  157.4 4.6 %collective-permute-start.28 = (f32[208,128]{1,0:T(8,128)S(1)}, f32[208,128]{1,0:T(8,128)S(1)}, u32[]{:S(2)}, u32[]{:S(2)}) collective-permute-start(f32[208,128]{1,0:T(8,128)S(1)} %get-tuple-element.125), channel_id=1, source_target_pairs={{1,17},{3,19},{5,21},{7,23},{9,25},{11,27},{13,29},{15,31},{17,1},... | collective-permute-start | bytes 319496 | tf_op jit(solution)/shard_map/ppermute | solution.py:442
  162.0 2.2 collective-permute-start.29
  164.2 11.0 %all-gather = f32[16,80,128]{2,1,0:T(8,128)} all-gather(f32[4,80,128]{2,1,0:T(8,128)S(1)} %pad_maximum_fusion.1), channel_id=2, replica_groups={{0,2,4,6},{8,10,12,14},{16,18,20,22},{24,26,28,30},{1,3,5,7},{9,11,13,1..., dimensions={0}, use_global_device_ids=true | all-gather | bytes 819200 | tf_op jit(solution)/shard_map/all_gather | solution.py:487
  179.3 20.6 %first_half.1 = (f32[512,512]{1,0:T(8,128)S(1)}, f32[512,512]{1,0:T(8,128)S(1)}) custom-call(s32[2]{0:T(128)S(1)} %pad_add_fusion.where_ref, f32[4,4,80,128]{3,2,1,0:T(8,128)S(1)} %bitcast.38, f32[256,512]{1,0:T(8,128)S(1)} %filter_step.14.refs_0_, f32[256,512]{1,0:T(8,128)S(1)} %filter_step.15.refs_1_, f32[256,512]{1,0:T(8,128)S(1)} %copy-done.6, ...), custom_call_target="tpu_custom_call" | custom-call | flops 20000000000 | bytes 10000000 | tf_op jit(solution)/shard_map/first_half/pallas_call | solution.py:367
  201.4 23.6 %second_half.1 = f32[512,512]{1,0:T(8,128)} custom-call(s32[2]{0:T(128)S(1)} %pad_add_fusion.where_ref, f32[4,4,208,128]{3,2,1,0:T(8,128)S(1)} %bitcast.37, f32[256,512]{1,0:T(8,128)S(1)} %filter_step.14.refs_0_, f32[256,512]{1,0:T(8,128)S(1)} %filter_step.15.refs_1_, f32[512,512]{1,0:T(8,128)S(1)} %get-tuple-element.113.refs_2_, ...), custom_call_target="tpu_custom_call" | custom-call | tf_op jit(solution)/shard_map/second_half/pallas_call | solution.py:420
  (85 shorter events, 32.4 us)
Async XLA Ops:
  6.5 137.1 %reduce-scatter.2.cloned.1.call-start = ((), (), s32[]{:S(2)}) async-start(), calls=%async_computation.2 | async-start | bytes 1310720 | tf_op jit(solution)/shard_map/reduce_scatter | solution.py:482
  9.2 15.2 %collective-permute-start.2 = (f32[256,384]{1,0:T(8,128)}, f32[256,384]{1,0:T(8,128)S(1)}, u32[]{:S(2)}, u32[]{:S(2)}) collective-permute-start(f32[256,384]{1,0:T(8,128)} %get-tuple-element.118), channel_id=1, source_target_pairs={{0,2},{2,4},{4,6},{6,8},{8,10},{10,12},{12,14},{14,16},{16,18},{18... | collective-permute-start | bytes 1179656 | tf_op jit(solution)/shard_map/ppermute | solution.py:111
  10.9 15.9 %collective-permute-start.3 = (f32[256,384]{1,0:T(8,128)}, f32[256,384]{1,0:T(8,128)}, u32[]{:S(2)}, u32[]{:S(2)}) collective-permute-start(f32[256,384]{1,0:T(8,128)} %get-tuple-element.117), channel_id=1, source_target_pairs={{2,0},{4,2},{6,4},{8,6},{10,8},{12,10},{14,12},{16,14},{18,16},{20... | collective-permute-start | bytes 1179656 | tf_op jit(solution)/shard_map/ppermute | solution.py:111
  10.9 18.2 %collective-permute-start = (f32[256,384]{1,0:T(8,128)}, f32[256,384]{1,0:T(8,128)S(1)}, u32[]{:S(2)}, u32[]{:S(2)}) collective-permute-start(f32[256,384]{1,0:T(8,128)} %get-tuple-element.120), channel_id=1, source_target_pairs={{0,2},{2,4},{4,6},{6,8},{8,10},{10,12},{12,14},{14,16},{16,18},{18... | collective-permute-start | bytes 1179656 | tf_op jit(solution)/shard_map/ppermute | solution.py:111
  12.7 22.5 %collective-permute-start.1 = (f32[256,384]{1,0:T(8,128)}, f32[256,384]{1,0:T(8,128)S(1)}, u32[]{:S(2)}, u32[]{:S(2)}) collective-permute-start(f32[256,384]{1,0:T(8,128)} %get-tuple-element.119), channel_id=1, source_target_pairs={{2,0},{4,2},{6,4},{8,6},{10,8},{12,10},{14,12},{16,14},{18,16},{20... | collective-permute-start | bytes 1179656 | tf_op jit(solution)/shard_map/ppermute | solution.py:111
  28.6 7.9 %collective-permute-start.6 = (f32[256,384]{1,0:T(8,128)S(1)}, f32[256,384]{1,0:T(8,128)S(1)}, u32[]{:S(2)}, u32[]{:S(2)}) collective-permute-start(f32[256,384]{1,0:T(8,128)S(1)} %get-tuple-element.68), channel_id=1, source_target_pairs={{0,2},{2,4},{4,6},{6,8},{8,10},{10,12},{12,14},{14,16},{16,18},{18... | collective-permute-start | bytes 1179656 | tf_op jit(solution)/shard_map/ppermute | solution.py:111
  28.7 19.2 %collective-permute-start.7 = (f32[256,384]{1,0:T(8,128)S(1)}, f32[256,384]{1,0:T(8,128)S(1)}, u32[]{:S(2)}, u32[]{:S(2)}) collective-permute-start(f32[256,384]{1,0:T(8,128)S(1)} %get-tuple-element.69), channel_id=1, source_target_pairs={{2,0},{4,2},{6,4},{8,6},{10,8},{12,10},{14,12},{16,14},{18,16},{20... | collective-permute-start | bytes 1179656 | tf_op jit(solution)/shard_map/ppermute | solution.py:111
  35.9 13.2 %collective-permute-start.4 = (f32[256,384]{1,0:T(8,128)S(1)}, f32[256,384]{1,0:T(8,128)S(1)}, u32[]{:S(2)}, u32[]{:S(2)}) collective-permute-start(f32[256,384]{1,0:T(8,128)S(1)} %get-tuple-element.66), channel_id=1, source_target_pairs={{0,2},{2,4},{4,6},{6,8},{8,10},{10,12},{12,14},{14,16},{16,18},{18... | collective-permute-start | bytes 1179656 | tf_op jit(solution)/shard_map/ppermute | solution.py:111
  36.0 16.0 %collective-permute-start.5 = (f32[256,384]{1,0:T(8,128)S(1)}, f32[256,384]{1,0:T(8,128)S(1)}, u32[]{:S(2)}, u32[]{:S(2)}) collective-permute-start(f32[256,384]{1,0:T(8,128)S(1)} %get-tuple-element.67), channel_id=1, source_target_pairs={{2,0},{4,2},{6,4},{8,6},{10,8},{12,10},{14,12},{16,14},{18,16},{20... | collective-permute-start | bytes 1179656 | tf_op jit(solution)/shard_map/ppermute | solution.py:111
  48.6 13.2 %collective-permute-start.10 = (f32[256,384]{1,0:T(8,128)S(1)}, f32[256,384]{1,0:T(8,128)S(1)}, u32[]{:S(2)}, u32[]{:S(2)}) collective-permute-start(f32[256,384]{1,0:T(8,128)S(1)} %get-tuple-element.80), channel_id=1, source_target_pairs={{0,2},{2,4},{4,6},{6,8},{8,10},{10,12},{12,14},{14,16},{16,18},{18... | collective-permute-start | bytes 1179656 | tf_op jit(solution)/shard_map/ppermute | solution.py:111
  48.6 13.1 %collective-permute-start.11 = (f32[256,384]{1,0:T(8,128)S(1)}, f32[256,384]{1,0:T(8,128)S(1)}, u32[]{:S(2)}, u32[]{:S(2)}) collective-permute-start(f32[256,384]{1,0:T(8,128)S(1)} %get-tuple-element.81), channel_id=1, source_target_pairs={{2,0},{4,2},{6,4},{8,6},{10,8},{12,10},{14,12},{16,14},{18,16},{20... | collective-permute-start | bytes 1179656 | tf_op jit(solution)/shard_map/ppermute | solution.py:111
  52.8 13.2 %collective-permute-start.8 = (f32[256,384]{1,0:T(8,128)S(1)}, f32[256,384]{1,0:T(8,128)S(1)}, u32[]{:S(2)}, u32[]{:S(2)}) collective-permute-start(f32[256,384]{1,0:T(8,128)S(1)} %get-tuple-element.78), channel_id=1, source_target_pairs={{0,2},{2,4},{4,6},{6,8},{8,10},{10,12},{12,14},{14,16},{16,18},{18... | collective-permute-start | bytes 1179656 | tf_op jit(solution)/shard_map/ppermute | solution.py:111
  52.9 16.0 %collective-permute-start.9 = (f32[256,384]{1,0:T(8,128)S(1)}, f32[256,384]{1,0:T(8,128)S(1)}, u32[]{:S(2)}, u32[]{:S(2)}) collective-permute-start(f32[256,384]{1,0:T(8,128)S(1)} %get-tuple-element.79), channel_id=1, source_target_pairs={{2,0},{4,2},{6,4},{8,6},{10,8},{12,10},{14,12},{16,14},{18,16},{20... | collective-permute-start | bytes 1179656 | tf_op jit(solution)/shard_map/ppermute | solution.py:111
  63.4 15.9 %collective-permute-start.14 = (f32[256,384]{1,0:T(8,128)}, f32[256,384]{1,0:T(8,128)}, u32[]{:S(2)}, u32[]{:S(2)}) collective-permute-start(f32[256,384]{1,0:T(8,128)} %get-tuple-element.92), channel_id=1, source_target_pairs={{0,2},{2,4},{4,6},{6,8},{8,10},{10,12},{12,14},{14,16},{16,18},{18... | collective-permute-start | bytes 1179656 | tf_op jit(solution)/shard_map/ppermute | solution.py:111
  65.9 13.5 %collective-permute-start.15 = (f32[256,384]{1,0:T(8,128)}, f32[256,384]{1,0:T(8,128)}, u32[]{:S(2)}, u32[]{:S(2)}) collective-permute-start(f32[256,384]{1,0:T(8,128)} %get-tuple-element.93), channel_id=1, source_target_pairs={{2,0},{4,2},{6,4},{8,6},{10,8},{12,10},{14,12},{16,14},{18,16},{20... | collective-permute-start | bytes 1179656 | tf_op jit(solution)/shard_map/ppermute | solution.py:111
  71.3 12.3 %collective-permute-start.12 = (f32[256,384]{1,0:T(8,128)}, f32[256,384]{1,0:T(8,128)}, u32[]{:S(2)}, u32[]{:S(2)}) collective-permute-start(f32[256,384]{1,0:T(8,128)} %get-tuple-element.90), channel_id=1, source_target_pairs={{0,2},{2,4},{4,6},{6,8},{8,10},{10,12},{12,14},{14,16},{16,18},{18... | collective-permute-start | bytes 1179656 | tf_op jit(solution)/shard_map/ppermute | solution.py:111
  71.3 12.3 %collective-permute-start.13 = (f32[256,384]{1,0:T(8,128)}, f32[256,384]{1,0:T(8,128)}, u32[]{:S(2)}, u32[]{:S(2)}) collective-permute-start(f32[256,384]{1,0:T(8,128)} %get-tuple-element.91), channel_id=1, source_target_pairs={{2,0},{4,2},{6,4},{8,6},{10,8},{12,10},{14,12},{16,14},{18,16},{20... | collective-permute-start | bytes 1179656 | tf_op jit(solution)/shard_map/ppermute | solution.py:111
  86.8 2.7 %collective-permute-start.16 = (f32[640,128]{1,0:T(8,128)S(1)}, f32[640,128]{1,0:T(8,128)S(1)}, u32[]{:S(2)}, u32[]{:S(2)}) collective-permute-start(f32[640,128]{1,0:T(8,128)S(1)} %dynamic-slice_bitcast_fusion), channel_id=1, source_target_pairs={{0,2},{1,3},{2,0},{3,1},{4,6},{5,7},{6,4},{7,5},{8,10},{9,11},{10,... | collective-permute-start | bytes 983048 | tf_op jit(solution)/shard_map/ppermute | solution.py:442
  86.8 14.9 %collective-permute-start.17 = (f32[256,512]{1,0:T(8,128)S(1)}, f32[256,512]{1,0:T(8,128)S(1)}, u32[]{:S(2)}, u32[]{:S(2)}) collective-permute-start(f32[256,512]{1,0:T(8,128)S(1)} %filter_step.14.refs_0_), channel_id=1, source_target_pairs={{0,1},{2,3},{4,5},{6,7},{8,9},{10,11},{12,13},{14,15},{16,17},{18,... | collective-permute-start | bytes 1572872 | tf_op jit(solution)/shard_map/ppermute | solution.py:448
  88.2 24.8 %collective-permute-start.19 = (f32[256,512]{1,0:T(8,128)S(1)}, f32[256,512]{1,0:T(8,128)S(1)}, u32[]{:S(2)}, u32[]{:S(2)}) collective-permute-start(f32[256,512]{1,0:T(8,128)S(1)} %filter_step.15.refs_1_), channel_id=1, source_target_pairs={{0,1},{2,3},{4,5},{6,7},{8,9},{10,11},{12,13},{14,15},{16,17},{18,... | collective-permute-start | bytes 1572872 | tf_op jit(solution)/shard_map/ppermute | solution.py:448
  101.8 6.5 %collective-permute-start.18 = (f32[320,128]{1,0:T(8,128)S(1)}, f32[320,128]{1,0:T(8,128)S(1)}, u32[]{:S(2)}, u32[]{:S(2)}) collective-permute-start(f32[320,128]{1,0:T(8,128)S(1)} %dynamic-slice_bitcast_fusion.1), channel_id=1, source_target_pairs={{0,4},{1,5},{2,6},{3,7},{4,0},{5,1},{6,2},{7,3},{8,12},{9,13},{10,... | collective-permute-start | bytes 491528 | tf_op jit(solution)/shard_map/ppermute | solution.py:442
  116.1 83.8 %all-gather.4.cloned.1.call-start = ((), (), s32[]{:S(2)}) async-start(), calls=%async_computation.3 | async-start | bytes 2129920 | tf_op jit(solution)/shard_map/all_gather | solution.py:493
  116.2 3.8 %collective-permute-start.20 = (f32[80,128]{1,0:T(8,128)S(1)}, f32[80,128]{1,0:T(8,128)S(1)}, u32[]{:S(2)}, u32[]{:S(2)}) collective-permute-start(f32[80,128]{1,0:T(8,128)S(1)} %get-tuple-element.123), channel_id=1, source_target_pairs={{0,8},{1,9},{2,10},{3,11},{4,12},{5,13},{6,14},{7,15},{8,0},{9,1},... | collective-permute-start | bytes 122888 | tf_op jit(solution)/shard_map/ppermute | solution.py:442
  117.9 4.2 %collective-permute-start.21 = (f32[80,128]{1,0:T(8,128)S(1)}, f32[80,128]{1,0:T(8,128)S(1)}, u32[]{:S(2)}, u32[]{:S(2)}) collective-permute-start(f32[80,128]{1,0:T(8,128)S(1)} %get-tuple-element.122), channel_id=1, source_target_pairs={{0,16},{1,17},{2,18},{3,19},{4,20},{5,21},{6,22},{7,23},{8,24},{9,... | collective-permute-start | bytes 122888 | tf_op jit(solution)/shard_map/ppermute | solution.py:442
  119.2 5.1 %collective-permute-start.22 = (f32[80,128]{1,0:T(8,128)S(1)}, f32[80,128]{1,0:T(8,128)S(1)}, u32[]{:S(2)}, u32[]{:S(2)}) collective-permute-start(f32[80,128]{1,0:T(8,128)S(1)} %get-tuple-element.121), channel_id=1, source_target_pairs={{0,24},{1,25},{2,26},{3,27},{4,28},{5,29},{6,30},{7,31},{8,16},{9,... | collective-permute-start | bytes 122888 | tf_op jit(solution)/shard_map/ppermute | solution.py:442
  124.2 4.7 %collective-permute-start.23 = (f32[80,128]{1,0:T(8,128)S(1)}, f32[80,128]{1,0:T(8,128)S(1)}, u32[]{:S(2)}, u32[]{:S(2)}) collective-permute-start(f32[80,128]{1,0:T(8,128)S(1)} %fusion), channel_id=1, source_target_pairs={{0,1},{2,3},{4,5},{6,7},{8,9},{10,11},{12,13},{14,15},{16,17},{18,... | collective-permute-start | bytes 122888 | tf_op jit(solution)/shard_map/ppermute | solution.py:448
  129.0 3.6 %collective-permute-start.24 = (f32[80,128]{1,0:T(8,128)S(1)}, f32[80,128]{1,0:T(8,128)S(1)}, u32[]{:S(2)}, u32[]{:S(2)}) collective-permute-start(f32[80,128]{1,0:T(8,128)S(1)} %broadcast_select_fusion), channel_id=1, source_target_pairs={{0,8},{1,9},{2,10},{3,11},{4,12},{5,13},{6,14},{7,15},{8,0},{9,1},... | collective-permute-start | bytes 122888 | tf_op jit(solution)/shard_map/ppermute | solution.py:442
  129.0 3.8 %collective-permute-start.25 = (f32[80,128]{1,0:T(8,128)S(1)}, f32[80,128]{1,0:T(8,128)S(1)}, u32[]{:S(2)}, u32[]{:S(2)}) collective-permute-start(f32[80,128]{1,0:T(8,128)S(1)} %broadcast_select_fusion), channel_id=1, source_target_pairs={{0,16},{1,17},{2,18},{3,19},{4,20},{5,21},{6,22},{7,23},{8,24},{9,... | collective-permute-start | bytes 122888 | tf_op jit(solution)/shard_map/ppermute | solution.py:442
  129.8 4.7 %collective-permute-start.26 = (f32[80,128]{1,0:T(8,128)S(1)}, f32[80,128]{1,0:T(8,128)S(1)}, u32[]{:S(2)}, u32[]{:S(2)}) collective-permute-start(f32[80,128]{1,0:T(8,128)S(1)} %broadcast_select_fusion), channel_id=1, source_target_pairs={{0,24},{1,25},{2,26},{3,27},{4,28},{5,29},{6,30},{7,31},{8,16},{9,... | collective-permute-start | bytes 122888 | tf_op jit(solution)/shard_map/ppermute | solution.py:442
  154.9 20.3 %collective-permute-start.27 = (f32[208,128]{1,0:T(8,128)S(1)}, f32[208,128]{1,0:T(8,128)S(1)}, u32[]{:S(2)}, u32[]{:S(2)}) collective-permute-start(f32[208,128]{1,0:T(8,128)S(1)} %get-tuple-element.125), channel_id=1, source_target_pairs={{1,9},{3,11},{5,13},{7,15},{9,1},{11,3},{13,5},{15,7},{17,25},{19,... | collective-permute-start | bytes 319496 | tf_op jit(solution)/shard_map/ppermute | solution.py:442
  157.4 17.8 %collective-permute-start.28 = (f32[208,128]{1,0:T(8,128)S(1)}, f32[208,128]{1,0:T(8,128)S(1)}, u32[]{:S(2)}, u32[]{:S(2)}) collective-permute-start(f32[208,128]{1,0:T(8,128)S(1)} %get-tuple-element.125), channel_id=1, source_target_pairs={{1,17},{3,19},{5,21},{7,23},{9,25},{11,27},{13,29},{15,31},{17,1},... | collective-permute-start | bytes 319496 | tf_op jit(solution)/shard_map/ppermute | solution.py:442
  162.0 13.2 %collective-permute-start.29 = (f32[208,128]{1,0:T(8,128)S(1)}, f32[208,128]{1,0:T(8,128)S(1)}, u32[]{:S(2)}, u32[]{:S(2)}) collective-permute-start(f32[208,128]{1,0:T(8,128)S(1)} %get-tuple-element.125), channel_id=1, source_target_pairs={{1,25},{3,27},{5,29},{7,31},{9,17},{11,19},{13,21},{15,23},{17,9},... | collective-permute-start | bytes 319496 | tf_op jit(solution)/shard_map/ppermute | solution.py:442
  (10 other events, 42.7 us)
Sparse Core Ops, SparseCore 0:
  116.2 27.3 reduce-scatter.1
  176.2 19.3 all-gather.3

commit v4 on v2

--- a/solution.py
+++ b/solution.py
@@ -171,16 +171,16 @@
     for s in range(strips):
         inverse = small_factor(columns)
         factors = {}
-        for t in range(s + 1, strips):
+        if s + 1 < strips:
+            t = s + 1
             old = [lane(left[t], SUB * s + j) for j in range(SUB)]
             factors[t] = [
                 total_of([old[m] * inverse[j, m] for m in range(j + 1)]) for j in range(SUB)
             ]
-            if t == s + 1:
-                ahead = [lane(left[t], SUB * t + j) for j in range(SUB)]
-                columns = [
-                    ahead[j] - total_of([x * row(x, j) for x in factors[t]]) for j in range(SUB)
-                ]
+            ahead = [lane(left[t], SUB * t + j) for j in range(SUB)]
+            columns = [
+                ahead[j] - total_of([x * row(x, j) for x in factors[t]]) for j in range(SUB)
+            ]
         upper_rows = [row(left[s], j) for j in range(SUB)]
         solved_rows = [row(right[s], j) for j in range(SUB)]
         spread = []
@@ -194,6 +194,13 @@
         done.append(solved)
         upper_rows = [row(upper, j) for j in range(SUB)]
         solved_rows = [row(solved, j) for j in range(SUB)]
+        if s + 2 < strips:
+            turned = upper.T
+            for t in range(s + 2, strips):
+                strip = turned[SUB * t:SUB * (t + 1), :]
+                factors[t] = [
+                    jnp.broadcast_to(strip[:, j:j + 1], (SUB, NB)) for j in range(SUB)
+                ]
         for t in range(s + 1, strips):
             left[t] = left[t] - total_of([x * y for x, y in zip(factors[t], upper_rows)])
             right[t] = right[t] - total_of([x * y for x, y in zip(factors[t], solved_rows)])

time: 227 us -> 230 us (1.013)
  Pallas kernels: 60.4 us -> 63.2 us
  transfers between devices with their start and end apart: 41 -> 41, of which waited for: 20 -> 20; matrix products, arithmetic and copies ran while one was open for 1% -> 1% of each run, Pallas kernels for 14% -> 15%
where the time goes in v4:
time: 230 us; the launch traced here: 229 us
  waiting for transfers between devices  85.4 us (37%)
  Pallas kernels  63.2 us (27%)
  starting transfers between devices  63 us (27%)
  local copies, waits for them, and re-layouts  8.34 us (4%)
  blocking collectives  8.01 us (3%)
    ppermute x16, waiting for transfers between devices, exchange_edges(): return (lax.ppermute(last, 'rows', up), lax.ppermute(first, 'rows', down))  54.7 us
    ppermute x22, starting transfers between devices, send(): return lax.ppermute(x, ('rows', 'vecs'), pairs)  48.8 us
    pallas_call x2, Pallas kernels, quarter(): pl.pallas_call(kernel, out_shape=tuple((jax.ShapeDtypeStruct((results, n)...  25.5 us
    pallas_call x1, Pallas kernels, second_half(): pl.pallas_call(functools.partial(second_half_kernel, scale), out_shape=ja...  25.4 us
    ppermute x22, waiting for transfers between devices, send(): return lax.ppermute(x, ('rows', 'vecs'), pairs)  19.1 us
    ppermute x3, waiting for transfers between devices, send_up(): return lax.ppermute(x, ('rows', 'vecs'), pairs)  11.6 us
    ppermute x16, starting transfers between devices, exchange_edges(): return (lax.ppermute(last, 'rows', up), lax.ppermute(first, 'rows', down))  10.4 us
    all_gather x1, blocking collectives, orthonormalize_planes(): second = lax.all_gather(second, 'rows', axis_index_groups=near_groups)  8.01 us
  transfers between devices with their start and end apart: 41, of which 20 were waited for; matrix products, arithmetic and copies ran while one was open for 1% of the time, Pallas kernels for 15%

profile of v4, /device:TPU:5, one launch (start us, length us, event | category | flops | bytes accessed | tf_op | source)
XLA Modules:
  0.0 229.1 jit_solution(2472539942937777078)
XLA Ops:
  0.0 2.6 %fusion.5 = (f32[256,384]{1,0:T(8,128)}, f32[256,384]{1,0:T(8,128)}, f32[256,384]{1,0:T(8,128)}, f32[256,384]{1,0:T(8,128)}) fusion(f32[512,512]{1,0:T(8,128)} %param.5), kind=kLoop, calls=%fused_computation.31 | loop fusion | bytes 3145728 | tf_op jit(solution)/shard_map/slice | solution.py:119
  10.0 7.8 %collective-permute-done.2.refs_0_ = f32[256,384]{1,0:T(8,128)S(1)} collective-permute-done((f32[256,384]{1,0:T(8,128)}, f32[256,384]{1,0:T(8,128)S(1)}, u32[]{:S(2)}, u32[]{:S(2)}) %collective-permute-start.2) | collective-permute-done | bytes 393248 | tf_op jit(solution)/shard_map/ppermute | solution.py:111
  17.8 2.5 %collective-permute-done.3.refs_2_ = f32[256,384]{1,0:T(8,128)} collective-permute-done((f32[256,384]{1,0:T(8,128)}, f32[256,384]{1,0:T(8,128)}, u32[]{:S(2)}, u32[]{:S(2)}) %collective-permute-start.3) | collective-permute-done | bytes 393248 | tf_op jit(solution)/shard_map/ppermute | solution.py:111
  22.6 6.0 %collective-permute-done.1.refs_2_ = f32[256,384]{1,0:T(8,128)S(1)} collective-permute-done((f32[256,384]{1,0:T(8,128)}, f32[256,384]{1,0:T(8,128)S(1)}, u32[]{:S(2)}, u32[]{:S(2)}) %collective-permute-start.1) | collective-permute-done | bytes 393248 | tf_op jit(solution)/shard_map/ppermute | solution.py:111
  30.0 11.3 %collective-permute-done.7.refs_2_ = f32[256,384]{1,0:T(8,128)S(1)} collective-permute-done((f32[256,384]{1,0:T(8,128)S(1)}, f32[256,384]{1,0:T(8,128)S(1)}, u32[]{:S(2)}, u32[]{:S(2)}) %collective-permute-start.7) | collective-permute-done | bytes 393248 | tf_op jit(solution)/shard_map/ppermute | solution.py:111
  42.6 2.9 %collective-permute-done.5.refs_2_ = f32[256,384]{1,0:T(8,128)S(1)} collective-permute-done((f32[256,384]{1,0:T(8,128)S(1)}, f32[256,384]{1,0:T(8,128)S(1)}, u32[]{:S(2)}, u32[]{:S(2)}) %collective-permute-start.5) | collective-permute-done | bytes 393248 | tf_op jit(solution)/shard_map/ppermute | solution.py:111
  46.8 8.4 %collective-permute-done.10.refs_0_ = f32[256,384]{1,0:T(8,128)S(1)} collective-permute-done((f32[256,384]{1,0:T(8,128)S(1)}, f32[256,384]{1,0:T(8,128)S(1)}, u32[]{:S(2)}, u32[]{:S(2)}) %collective-permute-start.10) | collective-permute-done | bytes 393248 | tf_op jit(solution)/shard_map/ppermute | solution.py:111
  56.0 2.5 %collective-permute-start.14 = (f32[256,384]{1,0:T(8,128)S(1)}, f32[256,384]{1,0:T(8,128)S(1)}, u32[]{:S(2)}, u32[]{:S(2)}) collective-permute-start(f32[256,384]{1,0:T(8,128)S(1)} %get-tuple-element.101), channel_id=1, source_target_pairs={{0,2},{2,4},{4,6},{6,8},{8,10},{10,12},{12,14},{14,16},{16,18},{18... | collective-permute-start | bytes 1179656 | tf_op jit(solution)/shard_map/ppermute | solution.py:111
  59.5 2.9 %collective-permute-done.9.refs_2_ = f32[256,384]{1,0:T(8,128)S(1)} collective-permute-done((f32[256,384]{1,0:T(8,128)S(1)}, f32[256,384]{1,0:T(8,128)S(1)}, u32[]{:S(2)}, u32[]{:S(2)}) %collective-permute-start.9) | collective-permute-done | bytes 393248 | tf_op jit(solution)/shard_map/ppermute | solution.py:111
  63.7 8.4 %collective-permute-done.14.refs_0_ = f32[256,384]{1,0:T(8,128)S(1)} collective-permute-done((f32[256,384]{1,0:T(8,128)S(1)}, f32[256,384]{1,0:T(8,128)S(1)}, u32[]{:S(2)}, u32[]{:S(2)}) %collective-permute-start.14) | collective-permute-done | bytes 393248 | tf_op jit(solution)/shard_map/ppermute | solution.py:111
  72.8 3.5 %collective-permute-done.12.refs_0_ = f32[256,384]{1,0:T(8,128)S(1)} collective-permute-done((f32[256,384]{1,0:T(8,128)S(1)}, f32[256,384]{1,0:T(8,128)S(1)}, u32[]{:S(2)}, u32[]{:S(2)}) %collective-permute-start.12) | collective-permute-done | bytes 393248 | tf_op jit(solution)/shard_map/ppermute | solution.py:111
  81.9 6.0 %collective-permute-done.16.refs_2_.refs_5_ = f32[256,512]{1,0:T(8,128)} collective-permute-done((f32[256,512]{1,0:T(8,128)S(1)}, f32[256,512]{1,0:T(8,128)}, u32[]{:S(2)}, u32[]{:S(2)}) %collective-permute-start.16) | collective-permute-done | bytes 524320 | tf_op jit(solution)/shard_map/ppermute | solution.py:508
  90.9 3.4 %collective-permute-start.18 = (f32[320,128]{1,0:T(8,128)S(1)}, f32[320,128]{1,0:T(8,128)S(1)}, u32[]{:S(2)}, u32[]{:S(2)}) collective-permute-start(f32[320,128]{1,0:T(8,128)S(1)} %dynamic-slice_bitcast_fusion.3), channel_id=1, source_target_pairs={{0,4},{1,5},{2,6},{3,7},{4,0},{5,1},{6,2},{7,3},{8,12},{9,13},{10,... | collective-permute-start | bytes 491528 | tf_op jit(solution)/shard_map/ppermute | solution.py:502
  95.7 3.0 %collective-permute-done.18 = f32[320,128]{1,0:T(8,128)S(1)} collective-permute-done((f32[320,128]{1,0:T(8,128)S(1)}, f32[320,128]{1,0:T(8,128)S(1)}, u32[]{:S(2)}, u32[]{:S(2)}) %collective-permute-start.18) | collective-permute-done | bytes 163872 | tf_op jit(solution)/shard_map/ppermute | solution.py:502
  109.1 3.2 %cross_gram.1 = f32[2048,128]{1,0:T(8,128)S(1)} custom-call(f32[256,512]{1,0:T(8,128)S(1)} %filter_step.14.refs_0_.refs_4_.refs_5_, f32[256,512]{1,0:T(8,128)S(1)} %filter_step.15.refs_1_.refs_4_.refs_6_, f32[256,512]{1,0:T(8,128)} %collective-permute-done.16.refs_2_.refs_5_, f32[256,512]{1,0:T(8,128)S(1)} %collective-permute-done.22.refs_3_.refs_5_), custom_call_target="tpu_custom_call" | custom-call | tf_op jit(solution)/shard_map/cross_gram/pallas_call | solution.py:309
  113.1 3.4 %collective-permute-start.24 = (f32[1024,128]{1,0:T(8,128)}, f32[1024,128]{1,0:T(8,128)S(1)}, u32[]{:S(2)}, u32[]{:S(2)}) collective-permute-start(f32[1024,128]{1,0:T(8,128)} %dynamic-slice_bitcast_fusion), channel_id=1, source_target_pairs={{1,3},{3,1},{5,7},{7,5},{9,11},{11,9},{13,15},{15,13},{17,19},{19,... | collective-permute-start | bytes 1572872 | tf_op jit(solution)/shard_map/ppermute | solution.py:502
  117.8 3.4 %collective-permute-done.23 = f32[80,128]{1,0:T(8,128)S(1)} collective-permute-done((f32[80,128]{1,0:T(8,128)S(1)}, f32[80,128]{1,0:T(8,128)S(1)}, u32[]{:S(2)}, u32[]{:S(2)}) %collective-permute-start.23) | collective-permute-done | bytes 40992 | tf_op jit(solution)/shard_map/ppermute | solution.py:508
  127.4 2.6 %collective-permute-done.26 = f32[160,128]{1,0:T(8,128)S(1)} collective-permute-done((f32[160,128]{1,0:T(8,128)S(1)}, f32[160,128]{1,0:T(8,128)S(1)}, u32[]{:S(2)}, u32[]{:S(2)}) %collective-permute-start.26) | collective-permute-done | bytes 81952 | tf_op jit(solution)/shard_map/ppermute | solution.py:502
  130.0 2.7 %collective-permute-done.27 = f32[160,128]{1,0:T(8,128)S(1)} collective-permute-done((f32[160,128]{1,0:T(8,128)S(1)}, f32[160,128]{1,0:T(8,128)S(1)}, u32[]{:S(2)}, u32[]{:S(2)}) %collective-permute-start.27) | collective-permute-done | bytes 81952 | tf_op jit(solution)/shard_map/ppermute | solution.py:502
  132.9 2.6 %collective-permute-start.29 = (f32[4,80,128]{2,1,0:T(8,128)S(1)}, f32[4,80,128]{2,1,0:T(8,128)S(1)}, u32[]{:S(2)}, u32[]{:S(2)}) collective-permute-start(f32[4,80,128]{2,1,0:T(8,128)S(1)} %get-tuple-element.121.refs_0_), channel_id=1, source_target_pairs={{0,2},{1,3},{2,0},{3,1},{4,6},{5,7},{6,4},{7,5},{8,10},{9,11},{10,... | collective-permute-start | bytes 491528 | tf_op jit(solution)/shard_map/ppermute | solution.py:502
  136.9 2.9 %collective-permute-start.32 = (f32[128,128]{1,0:T(8,128)S(1)}, f32[128,128]{1,0:T(8,128)S(1)}, u32[]{:S(2)}, u32[]{:S(2)}) collective-permute-start(f32[128,128]{1,0:T(8,128)S(1)} %get-tuple-element.143), channel_id=1, source_target_pairs={{1,9},{3,11},{5,13},{7,15},{9,1},{11,3},{13,5},{15,7},{17,25},{19,... | collective-permute-start | bytes 196616 | tf_op jit(solution)/shard_map/ppermute | solution.py:502
  139.8 3.2 %collective-permute-start.33 = (f32[128,128]{1,0:T(8,128)S(1)}, f32[128,128]{1,0:T(8,128)S(1)}, u32[]{:S(2)}, u32[]{:S(2)}) collective-permute-start(f32[128,128]{1,0:T(8,128)S(1)} %get-tuple-element.142), channel_id=1, source_target_pairs={{1,17},{3,19},{5,21},{7,23},{9,25},{11,27},{13,29},{15,31},{17,1},... | collective-permute-start | bytes 196616 | tf_op jit(solution)/shard_map/ppermute | solution.py:502
  143.1 3.1 %collective-permute-start.34 = (f32[128,128]{1,0:T(8,128)S(1)}, f32[128,128]{1,0:T(8,128)S(1)}, u32[]{:S(2)}, u32[]{:S(2)}) collective-permute-start(f32[128,128]{1,0:T(8,128)S(1)} %get-tuple-element.141), channel_id=1, source_target_pairs={{1,25},{3,27},{5,29},{7,31},{9,17},{11,19},{13,21},{15,23},{17,9},... | collective-permute-start | bytes 196616 | tf_op jit(solution)/shard_map/ppermute | solution.py:502
  146.2 8.0 %all-gather = f32[16,80,128]{2,1,0:T(8,128)S(1)} all-gather(f32[4,80,128]{2,1,0:T(8,128)S(1)} %get-tuple-element.140), channel_id=2, replica_groups={{0,2,4,6},{8,10,12,14},{16,18,20,22},{24,26,28,30},{1,3,5,7},{9,11,13,1..., dimensions={0}, use_global_device_ids=true | all-gather | bytes 819200 | tf_op jit(solution)/shard_map/all_gather | solution.py:550
  155.5 4.7 %collective-permute-done.31.refs_3_ = f32[4,80,128]{2,1,0:T(8,128)S(1)} collective-permute-done((f32[4,80,128]{2,1,0:T(8,128)S(1)}, f32[4,80,128]{2,1,0:T(8,128)S(1)}, u32[]{:S(2)}, u32[]{:S(2)}) %collective-permute-start.31) | collective-permute-done | bytes 163872 | tf_op jit(solution)/shard_map/ppermute | solution.py:502
  162.2 4.1 %collective-permute-start.36 = (f32[128,128]{1,0:T(8,128)S(1)}, f32[128,128]{1,0:T(8,128)S(1)}, u32[]{:S(2)}, u32[]{:S(2)}) collective-permute-start(f32[128,128]{1,0:T(8,128)S(1)} %fusion), channel_id=1, source_target_pairs={{1,17},{3,19},{5,21},{7,23},{9,25},{11,27},{13,29},{15,31},{17,1},... | collective-permute-start | bytes 196616 | tf_op jit(solution)/shard_map/ppermute | solution.py:502
  166.3 3.1 %collective-permute-start.37 = (f32[128,128]{1,0:T(8,128)S(1)}, f32[128,128]{1,0:T(8,128)S(1)}, u32[]{:S(2)}, u32[]{:S(2)}) collective-permute-start(f32[128,128]{1,0:T(8,128)S(1)} %fusion), channel_id=1, source_target_pairs={{1,25},{3,27},{5,29},{7,31},{9,17},{11,19},{13,21},{15,23},{17,9},... | collective-permute-start | bytes 196616 | tf_op jit(solution)/shard_map/ppermute | solution.py:502
  169.5 12.4 %first_quarter.1 = (f32[256,512]{1,0:T(8,128)S(1)}, f32[256,256]{1,0:T(8,128)S(1)}) custom-call(s32[3]{0:T(128)S(1)} %pad_add_fusion.where_ref, f32[4,80,128]{2,1,0:T(8,128)S(1)} %get-tuple-element.121.refs_0_, f32[4,80,128]{2,1,0:T(8,128)S(1)} %collective-permute-done.29.refs_1_, f32[4,80,128]{2,1,0:T(8,128)S(1)} %collective-permute-done.30.refs_2_, ...), custom_call_target="tpu_custom_call" | custom-call | flops 10000000000 | bytes 10000000 | tf_op jit(solution)/shard_map/first_quarter/pallas_call | solution.py:431
  181.9 3.0 %collective-permute-start.38 = (f32[4,128,128]{2,1,0:T(8,128)S(1)}, f32[4,128,128]{2,1,0:T(8,128)S(1)}, u32[]{:S(2)}, u32[]{:S(2)}) collective-permute-start(f32[4,128,128]{2,1,0:T(8,128)S(1)} %pad_maximum_fusion.1.refs_1_), channel_id=1, source_target_pairs={{1,3},{3,1},{5,7},{7,5},{9,11},{11,9},{13,15},{15,13},{17,19},{19,... | collective-permute-start | bytes 786440 | tf_op jit(solution)/shard_map/ppermute | solution.py:502
  184.9 3.1 %collective-permute-start.39 = (f32[4,128,128]{2,1,0:T(8,128)S(1)}, f32[4,128,128]{2,1,0:T(8,128)S(1)}, u32[]{:S(2)}, u32[]{:S(2)}) collective-permute-start(f32[4,128,128]{2,1,0:T(8,128)S(1)} %pad_maximum_fusion.1.refs_1_), channel_id=1, source_target_pairs={{1,5},{3,7},{5,1},{7,3},{9,13},{11,15},{13,9},{15,11},{17,21},{19,... | collective-permute-start | bytes 786440 | tf_op jit(solution)/shard_map/ppermute | solution.py:502
  190.4 13.1 %second_quarter.1 = (f32[512,512]{1,0:T(8,128)S(1)}, f32[512,512]{1,0:T(8,128)S(1)}) custom-call(s32[3]{0:T(128)S(1)} %pad_add_fusion.where_ref, f32[4,80,128]{2,1,0:T(8,128)S(1)} %get-tuple-element.121.refs_0_, f32[4,80,128]{2,1,0:T(8,128)S(1)} %collective-permute-done.29.refs_1_, f32[4,80,128]{2,1,0:T(8,128)S(1)} %collective-permute-done.30.refs_2_, ...), custom_call_target="tpu_custom_call" | custom-call | flops 10000000000 | bytes 10000000 | tf_op jit(solution)/shard_map/second_quarter/pallas_call | solution.py:431
  203.5 25.4 %second_half.1 = f32[512,512]{1,0:T(8,128)} custom-call(s32[3]{0:T(128)S(1)} %pad_add_fusion.where_ref, f32[4,4,80,128]{3,2,1,0:T(8,128)S(1)} %bitcast.56, f32[4,128,128]{2,1,0:T(8,128)S(1)} %pad_maximum_fusion.1.refs_1_, f32[4,128,128]{2,1,0:T(8,128)S(1)} %collective-permute-done.38.refs_2_, f32[4,128,128]{2,1,0:T(8,128)S(1)} %collective-permute-done.39.refs_3_, ...), custom_call_target="tpu_custom_call" | custom-call | tf_op jit(solution)/shard_map/second_half/pallas_call | solution.py:480
  (100 shorter events, 52.9 us)
Async XLA Ops:
  2.6 15.2 %collective-permute-start.2 = (f32[256,384]{1,0:T(8,128)}, f32[256,384]{1,0:T(8,128)S(1)}, u32[]{:S(2)}, u32[]{:S(2)}) collective-permute-start(f32[256,384]{1,0:T(8,128)} %get-tuple-element.136), channel_id=1, source_target_pairs={{0,2},{2,4},{4,6},{6,8},{8,10},{10,12},{12,14},{14,16},{16,18},{18... | collective-permute-start | bytes 1179656 | tf_op jit(solution)/shard_map/ppermute | solution.py:111
  4.4 15.9 %collective-permute-start.3 = (f32[256,384]{1,0:T(8,128)}, f32[256,384]{1,0:T(8,128)}, u32[]{:S(2)}, u32[]{:S(2)}) collective-permute-start(f32[256,384]{1,0:T(8,128)} %get-tuple-element.135), channel_id=1, source_target_pairs={{2,0},{4,2},{6,4},{8,6},{10,8},{12,10},{14,12},{16,14},{18,16},{20... | collective-permute-start | bytes 1179656 | tf_op jit(solution)/shard_map/ppermute | solution.py:111
  4.4 18.2 %collective-permute-start = (f32[256,384]{1,0:T(8,128)}, f32[256,384]{1,0:T(8,128)S(1)}, u32[]{:S(2)}, u32[]{:S(2)}) collective-permute-start(f32[256,384]{1,0:T(8,128)} %get-tuple-element.138), channel_id=1, source_target_pairs={{0,2},{2,4},{4,6},{6,8},{8,10},{10,12},{12,14},{14,16},{16,18},{18... | collective-permute-start | bytes 1179656 | tf_op jit(solution)/shard_map/ppermute | solution.py:111
  6.1 22.5 %collective-permute-start.1 = (f32[256,384]{1,0:T(8,128)}, f32[256,384]{1,0:T(8,128)S(1)}, u32[]{:S(2)}, u32[]{:S(2)}) collective-permute-start(f32[256,384]{1,0:T(8,128)} %get-tuple-element.137), channel_id=1, source_target_pairs={{2,0},{4,2},{6,4},{8,6},{10,8},{12,10},{14,12},{16,14},{18,16},{20... | collective-permute-start | bytes 1179656 | tf_op jit(solution)/shard_map/ppermute | solution.py:111
  22.1 7.9 %collective-permute-start.6 = (f32[256,384]{1,0:T(8,128)S(1)}, f32[256,384]{1,0:T(8,128)S(1)}, u32[]{:S(2)}, u32[]{:S(2)}) collective-permute-start(f32[256,384]{1,0:T(8,128)S(1)} %get-tuple-element.77), channel_id=1, source_target_pairs={{0,2},{2,4},{4,6},{6,8},{8,10},{10,12},{12,14},{14,16},{16,18},{18... | collective-permute-start | bytes 1179656 | tf_op jit(solution)/shard_map/ppermute | solution.py:111
  22.1 19.2 %collective-permute-start.7 = (f32[256,384]{1,0:T(8,128)S(1)}, f32[256,384]{1,0:T(8,128)S(1)}, u32[]{:S(2)}, u32[]{:S(2)}) collective-permute-start(f32[256,384]{1,0:T(8,128)S(1)} %get-tuple-element.78), channel_id=1, source_target_pairs={{2,0},{4,2},{6,4},{8,6},{10,8},{12,10},{14,12},{16,14},{18,16},{20... | collective-permute-start | bytes 1179656 | tf_op jit(solution)/shard_map/ppermute | solution.py:111
  29.4 13.2 %collective-permute-start.4 = (f32[256,384]{1,0:T(8,128)S(1)}, f32[256,384]{1,0:T(8,128)S(1)}, u32[]{:S(2)}, u32[]{:S(2)}) collective-permute-start(f32[256,384]{1,0:T(8,128)S(1)} %get-tuple-element.75), channel_id=1, source_target_pairs={{0,2},{2,4},{4,6},{6,8},{8,10},{10,12},{12,14},{14,16},{16,18},{18... | collective-permute-start | bytes 1179656 | tf_op jit(solution)/shard_map/ppermute | solution.py:111
  29.5 16.0 %collective-permute-start.5 = (f32[256,384]{1,0:T(8,128)S(1)}, f32[256,384]{1,0:T(8,128)S(1)}, u32[]{:S(2)}, u32[]{:S(2)}) collective-permute-start(f32[256,384]{1,0:T(8,128)S(1)} %get-tuple-element.76), channel_id=1, source_target_pairs={{2,0},{4,2},{6,4},{8,6},{10,8},{12,10},{14,12},{16,14},{18,16},{20... | collective-permute-start | bytes 1179656 | tf_op jit(solution)/shard_map/ppermute | solution.py:111
  42.0 13.2 %collective-permute-start.10 = (f32[256,384]{1,0:T(8,128)S(1)}, f32[256,384]{1,0:T(8,128)S(1)}, u32[]{:S(2)}, u32[]{:S(2)}) collective-permute-start(f32[256,384]{1,0:T(8,128)S(1)} %get-tuple-element.89), channel_id=1, source_target_pairs={{0,2},{2,4},{4,6},{6,8},{8,10},{10,12},{12,14},{14,16},{16,18},{18... | collective-permute-start | bytes 1179656 | tf_op jit(solution)/shard_map/ppermute | solution.py:111
  42.1 13.1 %collective-permute-start.11 = (f32[256,384]{1,0:T(8,128)S(1)}, f32[256,384]{1,0:T(8,128)S(1)}, u32[]{:S(2)}, u32[]{:S(2)}) collective-permute-start(f32[256,384]{1,0:T(8,128)S(1)} %get-tuple-element.90), channel_id=1, source_target_pairs={{2,0},{4,2},{6,4},{8,6},{10,8},{12,10},{14,12},{16,14},{18,16},{20... | collective-permute-start | bytes 1179656 | tf_op jit(solution)/shard_map/ppermute | solution.py:111
  46.2 13.2 %collective-permute-start.8 = (f32[256,384]{1,0:T(8,128)S(1)}, f32[256,384]{1,0:T(8,128)S(1)}, u32[]{:S(2)}, u32[]{:S(2)}) collective-permute-start(f32[256,384]{1,0:T(8,128)S(1)} %get-tuple-element.87), channel_id=1, source_target_pairs={{0,2},{2,4},{4,6},{6,8},{8,10},{10,12},{12,14},{14,16},{16,18},{18... | collective-permute-start | bytes 1179656 | tf_op jit(solution)/shard_map/ppermute | solution.py:111
  46.3 16.0 %collective-permute-start.9 = (f32[256,384]{1,0:T(8,128)S(1)}, f32[256,384]{1,0:T(8,128)S(1)}, u32[]{:S(2)}, u32[]{:S(2)}) collective-permute-start(f32[256,384]{1,0:T(8,128)S(1)} %get-tuple-element.88), channel_id=1, source_target_pairs={{2,0},{4,2},{6,4},{8,6},{10,8},{12,10},{14,12},{16,14},{18,16},{20... | collective-permute-start | bytes 1179656 | tf_op jit(solution)/shard_map/ppermute | solution.py:111
  56.0 16.1 %collective-permute-start.14 = (f32[256,384]{1,0:T(8,128)S(1)}, f32[256,384]{1,0:T(8,128)S(1)}, u32[]{:S(2)}, u32[]{:S(2)}) collective-permute-start(f32[256,384]{1,0:T(8,128)S(1)} %get-tuple-element.101), channel_id=1, source_target_pairs={{0,2},{2,4},{4,6},{6,8},{8,10},{10,12},{12,14},{14,16},{16,18},{18... | collective-permute-start | bytes 1179656 | tf_op jit(solution)/shard_map/ppermute | solution.py:111
  58.5 13.6 %collective-permute-start.15 = (f32[256,384]{1,0:T(8,128)S(1)}, f32[256,384]{1,0:T(8,128)S(1)}, u32[]{:S(2)}, u32[]{:S(2)}) collective-permute-start(f32[256,384]{1,0:T(8,128)S(1)} %get-tuple-element.102), channel_id=1, source_target_pairs={{2,0},{4,2},{6,4},{8,6},{10,8},{12,10},{14,12},{16,14},{18,16},{20... | collective-permute-start | bytes 1179656 | tf_op jit(solution)/shard_map/ppermute | solution.py:111
  63.1 13.2 %collective-permute-start.12 = (f32[256,384]{1,0:T(8,128)S(1)}, f32[256,384]{1,0:T(8,128)S(1)}, u32[]{:S(2)}, u32[]{:S(2)}) collective-permute-start(f32[256,384]{1,0:T(8,128)S(1)} %get-tuple-element.99), channel_id=1, source_target_pairs={{0,2},{2,4},{4,6},{6,8},{8,10},{10,12},{12,14},{14,16},{16,18},{18... | collective-permute-start | bytes 1179656 | tf_op jit(solution)/shard_map/ppermute | solution.py:111
  63.2 13.9 %collective-permute-start.13 = (f32[256,384]{1,0:T(8,128)S(1)}, f32[256,384]{1,0:T(8,128)S(1)}, u32[]{:S(2)}, u32[]{:S(2)}) collective-permute-start(f32[256,384]{1,0:T(8,128)S(1)} %get-tuple-element.100), channel_id=1, source_target_pairs={{2,0},{4,2},{6,4},{8,6},{10,8},{12,10},{14,12},{16,14},{18,16},{20... | collective-permute-start | bytes 1179656 | tf_op jit(solution)/shard_map/ppermute | solution.py:111
  77.8 10.0 %collective-permute-start.16 = (f32[256,512]{1,0:T(8,128)S(1)}, f32[256,512]{1,0:T(8,128)}, u32[]{:S(2)}, u32[]{:S(2)}) collective-permute-start(f32[256,512]{1,0:T(8,128)S(1)} %filter_step.14.refs_0_.refs_4_.refs_5_), channel_id=1, source_target_pairs={{0,1},{2,3},{4,5},{6,7},{8,9},{10,11},{12,13},{14,15},{16,17},{18,... | collective-permute-start | bytes 1572872 | tf_op jit(solution)/shard_map/ppermute | solution.py:508
  90.9 7.7 %collective-permute-start.18 = (f32[320,128]{1,0:T(8,128)S(1)}, f32[320,128]{1,0:T(8,128)S(1)}, u32[]{:S(2)}, u32[]{:S(2)}) collective-permute-start(f32[320,128]{1,0:T(8,128)S(1)} %dynamic-slice_bitcast_fusion.3), channel_id=1, source_target_pairs={{0,4},{1,5},{2,6},{3,7},{4,0},{5,1},{6,2},{7,3},{8,12},{9,13},{10,... | collective-permute-start | bytes 491528 | tf_op jit(solution)/shard_map/ppermute | solution.py:502
  94.4 14.7 %collective-permute-start.22 = (f32[256,512]{1,0:T(8,128)S(1)}, f32[256,512]{1,0:T(8,128)S(1)}, u32[]{:S(2)}, u32[]{:S(2)}) collective-permute-start(f32[256,512]{1,0:T(8,128)S(1)} %filter_step.15.refs_1_.refs_4_.refs_6_), channel_id=1, source_target_pairs={{0,1},{2,3},{4,5},{6,7},{8,9},{10,11},{12,13},{14,15},{16,17},{18,... | collective-permute-start | bytes 1572872 | tf_op jit(solution)/shard_map/ppermute | solution.py:508
  113.1 8.2 %collective-permute-start.24 = (f32[1024,128]{1,0:T(8,128)}, f32[1024,128]{1,0:T(8,128)S(1)}, u32[]{:S(2)}, u32[]{:S(2)}) collective-permute-start(f32[1024,128]{1,0:T(8,128)} %dynamic-slice_bitcast_fusion), channel_id=1, source_target_pairs={{1,3},{3,1},{5,7},{7,5},{9,11},{11,9},{13,15},{15,13},{17,19},{19,... | collective-permute-start | bytes 1572872 | tf_op jit(solution)/shard_map/ppermute | solution.py:502
  121.4 11.4 %collective-permute-start.28 = (f32[512,128]{1,0:T(8,128)S(1)}, f32[512,128]{1,0:T(8,128)S(1)}, u32[]{:S(2)}, u32[]{:S(2)}) collective-permute-start(f32[512,128]{1,0:T(8,128)S(1)} %dynamic-slice_bitcast_fusion.2), channel_id=1, source_target_pairs={{1,5},{3,7},{5,1},{7,3},{9,13},{11,15},{13,9},{15,11},{17,21},{19,... | collective-permute-start | bytes 786440 | tf_op jit(solution)/shard_map/ppermute | solution.py:502
  132.9 22.6 %collective-permute-start.29 = (f32[4,80,128]{2,1,0:T(8,128)S(1)}, f32[4,80,128]{2,1,0:T(8,128)S(1)}, u32[]{:S(2)}, u32[]{:S(2)}) collective-permute-start(f32[4,80,128]{2,1,0:T(8,128)S(1)} %get-tuple-element.121.refs_0_), channel_id=1, source_target_pairs={{0,2},{1,3},{2,0},{3,1},{4,6},{5,7},{6,4},{7,5},{8,10},{9,11},{10,... | collective-permute-start | bytes 491528 | tf_op jit(solution)/shard_map/ppermute | solution.py:502
  135.4 20.0 %collective-permute-start.30 = (f32[4,80,128]{2,1,0:T(8,128)S(1)}, f32[4,80,128]{2,1,0:T(8,128)S(1)}, u32[]{:S(2)}, u32[]{:S(2)}) collective-permute-start(f32[4,80,128]{2,1,0:T(8,128)S(1)} %get-tuple-element.121.refs_0_), channel_id=1, source_target_pairs={{0,4},{1,5},{2,6},{3,7},{4,0},{5,1},{6,2},{7,3},{8,12},{9,13},{10,... | collective-permute-start | bytes 491528 | tf_op jit(solution)/shard_map/ppermute | solution.py:502
  136.9 17.3 %collective-permute-start.32 = (f32[128,128]{1,0:T(8,128)S(1)}, f32[128,128]{1,0:T(8,128)S(1)}, u32[]{:S(2)}, u32[]{:S(2)}) collective-permute-start(f32[128,128]{1,0:T(8,128)S(1)} %get-tuple-element.143), channel_id=1, source_target_pairs={{1,9},{3,11},{5,13},{7,15},{9,1},{11,3},{13,5},{15,7},{17,25},{19,... | collective-permute-start | bytes 196616 | tf_op jit(solution)/shard_map/ppermute | solution.py:502
  139.8 15.6 %collective-permute-start.33 = (f32[128,128]{1,0:T(8,128)S(1)}, f32[128,128]{1,0:T(8,128)S(1)}, u32[]{:S(2)}, u32[]{:S(2)}) collective-permute-start(f32[128,128]{1,0:T(8,128)S(1)} %get-tuple-element.142), channel_id=1, source_target_pairs={{1,17},{3,19},{5,21},{7,23},{9,25},{11,27},{13,29},{15,31},{17,1},... | collective-permute-start | bytes 196616 | tf_op jit(solution)/shard_map/ppermute | solution.py:502
  143.1 12.4 %collective-permute-start.34 = (f32[128,128]{1,0:T(8,128)S(1)}, f32[128,128]{1,0:T(8,128)S(1)}, u32[]{:S(2)}, u32[]{:S(2)}) collective-permute-start(f32[128,128]{1,0:T(8,128)S(1)} %get-tuple-element.141), channel_id=1, source_target_pairs={{1,25},{3,27},{5,29},{7,31},{9,17},{11,19},{13,21},{15,23},{17,9},... | collective-permute-start | bytes 196616 | tf_op jit(solution)/shard_map/ppermute | solution.py:502
  160.2 21.7 %collective-permute-start.35 = (f32[128,128]{1,0:T(8,128)S(1)}, f32[128,128]{1,0:T(8,128)S(1)}, u32[]{:S(2)}, u32[]{:S(2)}) collective-permute-start(f32[128,128]{1,0:T(8,128)S(1)} %fusion), channel_id=1, source_target_pairs={{1,9},{3,11},{5,13},{7,15},{9,1},{11,3},{13,5},{15,7},{17,25},{19,... | collective-permute-start | bytes 196616 | tf_op jit(solution)/shard_map/ppermute | solution.py:502
  162.2 19.7 %collective-permute-start.36 = (f32[128,128]{1,0:T(8,128)S(1)}, f32[128,128]{1,0:T(8,128)S(1)}, u32[]{:S(2)}, u32[]{:S(2)}) collective-permute-start(f32[128,128]{1,0:T(8,128)S(1)} %fusion), channel_id=1, source_target_pairs={{1,17},{3,19},{5,21},{7,23},{9,25},{11,27},{13,29},{15,31},{17,1},... | collective-permute-start | bytes 196616 | tf_op jit(solution)/shard_map/ppermute | solution.py:502
  166.3 15.6 %collective-permute-start.37 = (f32[128,128]{1,0:T(8,128)S(1)}, f32[128,128]{1,0:T(8,128)S(1)}, u32[]{:S(2)}, u32[]{:S(2)}) collective-permute-start(f32[128,128]{1,0:T(8,128)S(1)} %fusion), channel_id=1, source_target_pairs={{1,25},{3,27},{5,29},{7,31},{9,17},{11,19},{13,21},{15,23},{17,9},... | collective-permute-start | bytes 196616 | tf_op jit(solution)/shard_map/ppermute | solution.py:502
  181.9 21.6 %collective-permute-start.38 = (f32[4,128,128]{2,1,0:T(8,128)S(1)}, f32[4,128,128]{2,1,0:T(8,128)S(1)}, u32[]{:S(2)}, u32[]{:S(2)}) collective-permute-start(f32[4,128,128]{2,1,0:T(8,128)S(1)} %pad_maximum_fusion.1.refs_1_), channel_id=1, source_target_pairs={{1,3},{3,1},{5,7},{7,5},{9,11},{11,9},{13,15},{15,13},{17,19},{19,... | collective-permute-start | bytes 786440 | tf_op jit(solution)/shard_map/ppermute | solution.py:502
  184.9 18.6 %collective-permute-start.39 = (f32[4,128,128]{2,1,0:T(8,128)S(1)}, f32[4,128,128]{2,1,0:T(8,128)S(1)}, u32[]{:S(2)}, u32[]{:S(2)}) collective-permute-start(f32[4,128,128]{2,1,0:T(8,128)S(1)} %pad_maximum_fusion.1.refs_1_), channel_id=1, source_target_pairs={{1,5},{3,7},{5,1},{7,3},{9,13},{11,15},{13,9},{15,11},{17,21},{19,... | collective-permute-start | bytes 786440 | tf_op jit(solution)/shard_map/ppermute | solution.py:502
  188.0 15.5 %collective-permute-start.40 = (f32[4,128,128]{2,1,0:T(8,128)S(1)}, f32[4,128,128]{2,1,0:T(8,128)S(1)}, u32[]{:S(2)}, u32[]{:S(2)}) collective-permute-start(f32[4,128,128]{2,1,0:T(8,128)S(1)} %pad_maximum_fusion.1.refs_1_), channel_id=1, source_target_pairs={{1,7},{3,5},{5,3},{7,1},{9,15},{11,13},{13,11},{15,9},{17,23},{19,... | collective-permute-start | bytes 786440 | tf_op jit(solution)/shard_map/ppermute | solution.py:502
  (15 other events, 58.7 us)
